TPU v7x, 128 devices: a whole 4x4x4 slice. The times are simulated.
128 devices in a mesh: ph: 16 (over y, x_lo, core), el: 8 (over x_hi, z).
Axes of the slice: x: 4 (x_hi: 2, x_lo: 2; x = x_hi * 2 + x_lo), y: 4, z: 4, core: 2. Of those that a mesh axis runs over, the one named last changes fastest.
Arguments:
- wannier_g: bfloat16 [128, 1024, 4, 2, 1024], P('el', 'ph'), may hold values from -0.078125 to 0.078125
- el_vectors: int32 [3, 128], P(None, 'el'), may hold values from -6 to 6
- ph_vectors: int32 [3, 1024], P(None, 'ph'), may hold values from -6 to 6
- el_degen: int32 [128], P('el'), may hold values from 1 to 8
- ph_degen: int32 [1024], P('ph'), may hold values from 1 to 8
- k_points: float32 [3, 16], replicated, may hold values from 0 to 1
- q_points: float32 [3, 128], replicated, may hold values from 0 to 1
- rot_right: float32 [16, 2, 32, 32], P('el'), may hold values from -0.75 to 0.75
- rot_left: float32 [16, 128, 2, 32, 32], P('el', 'ph'), may hold values from -0.75 to 0.75
Outputs:
- bloch_g: float32 [16, 128, 4, 2, 1024], P('el', 'ph')
All inputs are finite; a program needn't handle non-finite values.
Results may differ from a plain program's by a relative error of at most 0.0034.
Values sent between devices are 32-bit elements; how exact they have to be, the bound alone decides.
No kernel may reach another device: no remote copies, remote signals or barrier semaphores. Data moves between devices by JAX's collectives and lax.ppermute only.
A program may use at most 448 MiB of HBM per device.

v0:
```python
import jax
import jax.numpy as jnp
from jax import lax
from jax.sharding import PartitionSpec as P


def phase_table(points, vectors, degen):
    coords = vectors.astype(jnp.float32)
    angle = points[0][:, None] * coords[0][None, :] + points[1][:, None] * coords[1][None, :]
    angle = angle + points[2][:, None] * coords[2][None, :]
    angle = 2.0 * jnp.pi * angle
    scale = 1.0 / degen.astype(jnp.float32)
    return (
        (jnp.cos(angle) * scale[None, :]).astype(jnp.bfloat16),
        (jnp.sin(angle) * scale[None, :]).astype(jnp.bfloat16),
    )


def combine(cos_part, sin_part):
    real_part = cos_part[..., 0, :] - sin_part[..., 1, :]
    imag_part = cos_part[..., 1, :] + sin_part[..., 0, :]
    return jnp.stack([real_part, imag_part], axis=-2)


def apply_phase(form, cos_table, sin_table, data, exact):
    if exact:
        cos_part = jnp.einsum(form, cos_table, data, precision=lax.Precision.HIGHEST)
        sin_part = jnp.einsum(form, sin_table, data, precision=lax.Precision.HIGHEST)
    else:
        cos_part = jnp.einsum(form, cos_table, data, preferred_element_type=jnp.float32)
        sin_part = jnp.einsum(form, sin_table, data, preferred_element_type=jnp.float32)
    return combine(cos_part, sin_part)


def rotate(summed, rot_right, rot_left):
    nk, nq, modes = (summed.shape[0], summed.shape[1], summed.shape[2])
    nw = rot_right.shape[-1]
    matrix = summed.reshape(nk, nq, modes, 2, nw, nw)
    g_real, g_imag = (matrix[:, :, :, 0], matrix[:, :, :, 1])
    r_real, r_imag = (rot_right[:, 0], rot_right[:, 1])
    l_real, l_imag = (rot_left[:, :, 0], rot_left[:, :, 1])
    hp = lax.Precision.HIGHEST
    a_real = jnp.einsum("kqmab,kbc->kqmac", g_real, r_real, precision=hp) - jnp.einsum(
        "kqmab,kbc->kqmac", g_imag, r_imag, precision=hp
    )
    a_imag = jnp.einsum("kqmab,kbc->kqmac", g_real, r_imag, precision=hp) + jnp.einsum(
        "kqmab,kbc->kqmac", g_imag, r_real, precision=hp
    )
    o_real = jnp.einsum("kqai,kqmac->kqmic", l_real, a_real, precision=hp) + jnp.einsum(
        "kqai,kqmac->kqmic", l_imag, a_imag, precision=hp
    )
    o_imag = jnp.einsum("kqai,kqmac->kqmic", l_real, a_imag, precision=hp) - jnp.einsum(
        "kqai,kqmac->kqmic", l_imag, a_real, precision=hp
    )
    return jnp.stack([o_real, o_imag], axis=3).reshape(nk, nq, modes, 2, nw * nw)


def body(
    wannier_g, el_vectors, ph_vectors, el_degen, ph_degen, k_points, q_points, rot_right, rot_left
):
    q_cos, q_sin = phase_table(q_points, ph_vectors, ph_degen)
    k_cos, k_sin = phase_table(k_points, el_vectors, el_degen)
    k_cos_wide, k_sin_wide = (k_cos.astype(jnp.float32), k_sin.astype(jnp.float32))
    mixed = lax.psum_scatter(
        apply_phase("qp,rpmcx->qrmcx", q_cos, q_sin, wannier_g, False),
        "ph",
        scatter_dimension=0,
        tiled=True,
    )
    summed = lax.psum_scatter(
        apply_phase("kr,qrmcx->kqmcx", k_cos_wide, k_sin_wide, mixed, True),
        "el",
        scatter_dimension=0,
        tiled=True,
    )
    return rotate(summed, rot_right, rot_left)


def solution(mesh):
    in_specs = (
        P("el", "ph", None, None, None),
        P(None, "el"),
        P(None, "ph"),
        P("el"),
        P("ph"),
        P(),
        P(),
        P("el", None, None, None),
        P("el", "ph", None, None, None),
    )
    out_specs = P("el", "ph", None, None, None)
    return jax.shard_map(body, mesh=mesh, in_specs=in_specs, out_specs=out_specs, check_vma=False)
```

profile of v0, /device:TPU:1, one launch (start us, length us, event | category | flops | bytes accessed | tf_op | source)
XLA Modules:
  0.0 993.2 jit_solution(14689675995407943827)
XLA Ops:
  6.5 0.0 reduce-scatter.3.cloned.1.call-start
  6.5 0.7 convert_element_type.29
  7.2 0.8 slice_bitcast_fusion.11
  8.0 0.7 convert_divide_fusion
  8.7 29.0 %fusion.2 = f32[128,16,4,2,1024]{4,0,3,2,1:T(8,128)} fusion(bf16[16,64,4,2,1024]{4,3,2,1,0:T(2,128)(2,1)} %param.9, f32[64]{0:T(128)S(1)} %convert_divide_fusion, f32[64]{0:T(128)S(1)} %get-tuple-element.19, f32[128]{0:T(128)S(1)} %get-tuple-element.16, f32[64]{0:T(128)S(1)} %get-tuple-element.20, f32[128]{0:T(128)S(1)} %get-tuple-element.17, ...), kind=kOutput, calls=%fused_computation.5 | convolution fusion | flops 2147549184 | bytes 83888640 | tf_op jit(solution)/shard_map/qp,rpmcx->qrmcx/dot_general | solution.py:30
  37.7 29.0 %fusion = f32[128,16,4,2,1024]{4,0,3,2,1:T(8,128)} fusion(bf16[16,64,4,2,1024]{4,3,2,1,0:T(2,128)(2,1)} %param.9, f32[64]{0:T(128)S(1)} %convert_divide_fusion, f32[64]{0:T(128)S(1)} %get-tuple-element.19, f32[128]{0:T(128)S(1)} %get-tuple-element.16, f32[64]{0:T(128)S(1)} %get-tuple-element.20, f32[128]{0:T(128)S(1)} %get-tuple-element.17, ...), kind=kOutput, calls=%fused_computation.3 | convolution fusion | flops 2147549184 | bytes 83888640 | tf_op jit(solution)/shard_map/qp,rpmcx->qrmcx/dot_general | solution.py:31
  66.7 64.6 %slice_subtract_fusion = (f32[128,16,4,1,1024]{4,0,3,2,1:T(8,128)}, f32[128,16,4,1,1024]{4,0,3,2,1:T(8,128)}) fusion(f32[128,16,4,2,1024]{4,0,3,2,1:T(8,128)} %fusion, f32[128,16,4,2,1024]{4,0,3,2,1:T(8,128)} %fusion.2), kind=kLoop, calls=%fused_computation.2 | loop fusion | flops 16777216 | bytes 201326592 | tf_op jit(solution)/shard_map/sub | solution.py:20
  131.3 43.5 %pad_maximum_fusion = f32[128,16,4,2,1024]{4,0,3,2,1:T(8,128)} fusion(f32[128,16,4,1,1024]{4,0,3,2,1:T(8,128)} %get-tuple-element.6, f32[128,16,4,1,1024]{4,0,3,2,1:T(8,128)} %get-tuple-element.5), kind=kLoop, calls=%fused_computation | loop fusion | flops 16777216 | bytes 134217728 | tf_op jit(solution)/shard_map/stack | solution.py:22
  174.8 0.0 copy-start.3
  174.8 0.0 copy-start.5
  174.8 0.0 copy-start.4
  174.9 0.0 reduce-scatter.3.cloned.1.call-update
  174.9 0.2 reduce-scatter.5.cloned.1.call-start
  175.1 0.4 copy-done.3
  175.5 0.0 copy-done.5
  175.5 0.0 copy-done.4
  175.5 688.9 %reduce-scatter.3.cloned.1.call-done = f32[8,16,4,2,1024]{4,0,3,2,1:T(8,128)} async-done(((f32[128,16,4,2,1024]{4,0,3,2,1:T(8,128)}), f32[8,16,4,2,1024]{4,0,3,2,1:T(8,128)}) %reduce-scatter.3.cloned.1.call-update) | async-done | bytes 4194320 | tf_op jit(solution)/shard_map/reduce_scatter | solution.py:64
  864.5 0.0 copy-start
  864.5 6.9 fusion.6
  871.3 0.0 copy-done
  871.3 4.6 fusion.4
  876.0 1.4 slice_subtract_fusion.1
  877.4 0.3 pad_maximum_fusion.1
  877.7 4.6 copy.45
  882.3 0.0 copy-start.2
  882.3 0.0 reduce-scatter.5.cloned.1.call-update
  882.3 84.3 %reduce-scatter.5.cloned.1.call-done = f32[2,8,4,2,1024]{4,1,3,2,0:T(8,128)} async-done(((f32[16,8,4,2,1024]{4,1,3,2,0:T(8,128)}), f32[2,8,4,2,1024]{4,1,3,2,0:T(8,128)}) %reduce-scatter.5.cloned.1.call-update) | async-done | bytes 524304 | tf_op jit(solution)/shard_map/reduce_scatter | solution.py:70
  966.6 1.4 copy.46
  968.0 0.7 reshape.16
  968.7 0.0 copy-done.2
  968.8 1.0 fusion.11
  969.8 0.0 copy-start.1
  969.8 1.0 fusion.10
  970.8 1.0 convolution_subtract_fusion
  971.8 1.0 convolution_add_fusion
  972.8 0.0 copy-done.1
  972.8 1.8 fusion.16
  974.7 1.8 fusion.14
  976.5 2.8 fusion.9
  979.2 1.8 copy.53
  981.1 0.5 stack.21
  981.5 2.8 fusion.8
  984.3 0.3 copy.56
  984.6 0.5 stack.22
  985.2 1.2 copy.57
  (5 shorter events, 0.1 us)
Async XLA Ops:
  6.5 857.9 %reduce-scatter.3.cloned.1.call-start = ((), (), s32[]{:S(2)}) async-start(), calls=%async_computation.2 | async-start | bytes 71303168 | tf_op jit(solution)/shard_map/reduce_scatter | solution.py:64
  174.8 0.7 copy-start.3
  174.8 0.7 copy-start.5
  174.8 0.7 copy-start.4
  174.9 791.8 %reduce-scatter.5.cloned.1.call-start = ((), (), s32[]{:S(2)}) async-start(), calls=%async_computation.3 | async-start | bytes 4718592 | tf_op jit(solution)/shard_map/reduce_scatter | solution.py:70
  864.5 6.9 copy-start
  882.3 86.5 %copy-start.2 = (f32[2,2,32,32]{3,2,1,0:T(8,128)S(1)}, f32[2,2,32,32]{3,2,1,0:T(8,128)}, u32[]{:S(2)}) copy-start(f32[2,2,32,32]{3,2,1,0:T(8,128)} %param.16) | copy-start | bytes 49156
  969.8 3.1 copy-start.1
Sparse Core Ops, SparseCore 0:
  175.0 689.4 reduce-scatter.2
  882.4 84.1 reduce-scatter.4
where the time goes:
time: 994 us; the launch traced here: 993 us
  waiting for transfers between devices  773 us (78%)
  other arithmetic  111 us (11%)
  matrix products  82.6 us (8%)
  between operations  13.6 us (1%)
  local copies, waits for them, and re-layouts  12.3 us (1%)
    reduce_scatter x1, waiting for transfers between devices, body(): lax.psum_scatter(apply_phase('qp,rpmcx->qrmcx', q_cos, q_sin, wannier_g,...  689 us
    reduce_scatter x1, waiting for transfers between devices, body(): lax.psum_scatter(apply_phase('kr,qrmcx->kqmcx', k_cos_wide, k_sin_wide, m...  84.3 us
    sub x2, other arithmetic, combine(): real_part = cos_part[..., 0, :] - sin_part[..., 1, :]  66 us
    another operation x2, other arithmetic, combine(): return jnp.stack([real_part, imag_part], axis=-2)  43.8 us
    dot_general x1, matrix products, apply_phase(): jnp.einsum(form, cos_table, data, preferred_element_type=jnp.float32)  29 us
    dot_general x1, matrix products, apply_phase(): jnp.einsum(form, sin_table, data, preferred_element_type=jnp.float32)  29 us
  transfers between devices with their start and end apart: 2, of which 2 were waited for; matrix products, arithmetic and copies ran while one was open for 0% of the time, Pallas kernels for 0%

commit v1 on v0

v1 whole, which is shorter than its diff:
```python
import jax
import jax.numpy as jnp
from jax import lax
from jax.experimental import pallas as pl
from jax.experimental.pallas import tpu as pltpu
from jax.sharding import Mesh, PartitionSpec as P

LANES = 256
PARTS = {"z": (0, 1, 2), "x": (3, 4, 5), "y": (6, 7)}
ORDER = {"z": ("z", "x", "y"), "x": ("x", "y", "z"), "y": ("y", "z", "x")}
DIMS = ("xh", "z", "i", "y", "xl", "c", "u", "m", "j", "w")
SIZES = {"xh": 2, "z": 4, "i": 2, "y": 4, "xl": 2, "c": 2}


def phase_table(points, coords, degen):
    angle = points[0][:, None] * coords[0][None, :] + points[1][:, None] * coords[1][None, :]
    angle = angle + points[2][:, None] * coords[2][None, :]
    angle = 2.0 * jnp.pi * angle
    scale = 1.0 / degen
    return (
        (jnp.cos(angle) * scale[None, :]).astype(jnp.bfloat16),
        (jnp.sin(angle) * scale[None, :]).astype(jnp.bfloat16),
    )


def partial_kernel(wq_ref, wk_ref, own_ref, got_ref, out_ref, mixed_ref):
    for r in range(16):
        own = own_ref[r, 0]
        got = got_ref[r, 0].astype(jnp.bfloat16)
        rows = jnp.concatenate([own[0], got[0], own[1], got[1]], axis=0)
        mixed = jnp.dot(wq_ref[...], rows, preferred_element_type=jnp.float32)
        mixed_ref[:, r] = mixed.reshape(2, 16, 8, LANES)
    for g in range(16):
        rows = mixed_ref[:, :, g].reshape(256, LANES).astype(jnp.bfloat16)
        summed = jnp.dot(wk_ref[...], rows, preferred_element_type=jnp.float32)
        out_ref[:, g, 0] = summed.reshape(16, 2, 8, LANES)


def partial_sums(wq, wk, own, got, first, count):
    return pl.pallas_call(
        partial_kernel,
        grid=(count,),
        in_specs=[
            pl.BlockSpec((256, 256), lambda u: (0, 0)),
            pl.BlockSpec((256, 256), lambda u: (0, 0)),
            pl.BlockSpec((16, 1, 2, 64, LANES), lambda u: (0, (u + first) // 4, 0, 0, (u + first) % 4)),
            pl.BlockSpec((16, 1, 2, 64, LANES), lambda u: (0, (u + first) // 4, 0, 0, (u + first) % 4)),
        ],
        out_specs=pl.BlockSpec((16, 16, 1, 2, 8, LANES), lambda u: (0, 0, u, 0, 0, 0)),
        out_shape=jax.ShapeDtypeStruct((16, 16, count, 2, 8, LANES), jnp.float32),
        scratch_shapes=[pltpu.VMEM((2, 16, 16, 8, LANES), jnp.float32)],
        compiler_params=pltpu.CompilerParams(vmem_limit_bytes=48 * 1024 * 1024),
        cost_estimate=pl.CostEstimate(
            flops=2 * 2 * 16 * 256 * 256 * LANES * count,
            bytes_accessed=count * LANES * (16 * 128 * 6 + 256 * 16 * 4),
            transcendentals=0,
        ),
    )(wq, wk, own, got)


def chunk(array, dims, axis, place):
    cuts = {"x": (("xh", place // 2), ("xl", place % 2))}.get(axis, ((axis, place),))
    starts = [0] * len(dims)
    sizes = list(array.shape)
    left = list(dims)
    for name, at in cuts:
        spot = dims.index(name)
        starts[spot], sizes[spot] = at, 1
        left.remove(name)
    piece = lax.dynamic_slice(array, starts, sizes)
    return piece.reshape([n for n, d in zip(sizes, dims) if d in left]), tuple(left)


def ring_pairs(axis):
    pairs = []
    for core in range(2):
        for at in range(4):
            to = (at + 1 - 2 * core) % 4
            if axis == "z":
                pairs.append((core * 4 + at, core * 4 + to))
            elif axis == "y":
                pairs.append((at * 2 + core, to * 2 + core))
            else:
                pairs.append(((at % 2) * 4 + core * 2 + at // 2, (to % 2) * 4 + core * 2 + to // 2))
    return pairs


RING_AXES = {"z": ("c", "z"), "y": ("y", "c"), "x": ("xl", "c", "xh")}


def rotate(summed, rot_right, rot_left):
    nk, nq, modes = (summed.shape[0], summed.shape[1], summed.shape[2])
    nw = rot_right.shape[-1]
    matrix = summed.reshape(nk, nq, modes, 2, nw, nw)
    g_real, g_imag = (matrix[:, :, :, 0], matrix[:, :, :, 1])
    r_real, r_imag = (rot_right[:, 0], rot_right[:, 1])
    l_real, l_imag = (rot_left[:, :, 0], rot_left[:, :, 1])
    hp = lax.Precision.HIGHEST
    a_real = jnp.einsum("kqmab,kbc->kqmac", g_real, r_real, precision=hp) - jnp.einsum(
        "kqmab,kbc->kqmac", g_imag, r_imag, precision=hp
    )
    a_imag = jnp.einsum("kqmab,kbc->kqmac", g_real, r_imag, precision=hp) + jnp.einsum(
        "kqmab,kbc->kqmac", g_imag, r_real, precision=hp
    )
    o_real = jnp.einsum("kqai,kqmac->kqmic", l_real, a_real, precision=hp) + jnp.einsum(
        "kqai,kqmac->kqmic", l_imag, a_imag, precision=hp
    )
    o_imag = jnp.einsum("kqai,kqmac->kqmic", l_real, a_imag, precision=hp) - jnp.einsum(
        "kqai,kqmac->kqmic", l_imag, a_real, precision=hp
    )
    return jnp.stack([o_real, o_imag], axis=3).reshape(nk, nq, modes, 2, nw * nw)


def complex_table(cos_part, sin_part):
    top = jnp.concatenate([cos_part, -sin_part], axis=1)
    bottom = jnp.concatenate([sin_part, cos_part], axis=1)
    return jnp.concatenate([top, bottom], axis=0)


def body(
    wannier_g, el_vectors, ph_vectors, el_degen, ph_degen, k_points, q_points, rot_right, rot_left
):
    core = lax.axis_index("c")
    place = {
        "z": lax.axis_index("z"),
        "y": lax.axis_index("y"),
        "x": lax.axis_index("xh") * 2 + lax.axis_index("xl"),
    }
    step = 1 - 2 * core
    swap = lambda v: lax.ppermute(v, "c", [(0, 1), (1, 0)])

    sent = lax.dynamic_slice_in_dim(wannier_g, 2 - 2 * core, 2, axis=2)
    got = swap(sent.transpose(0, 2, 3, 1, 4).astype(jnp.float32))
    own = lax.dynamic_slice_in_dim(wannier_g, 2 * core, 2, axis=2).transpose(0, 2, 3, 1, 4)

    vectors = jnp.concatenate([ph_vectors, ph_degen[None]], axis=0).astype(jnp.float32)
    vectors = jnp.concatenate([vectors, swap(vectors)], axis=1)
    wq = complex_table(*phase_table(q_points, vectors[:3], vectors[3]))
    k_cos, k_sin = phase_table(k_points, el_vectors.astype(jnp.float32), el_degen.astype(jnp.float32))
    wide = jnp.stack([jnp.stack([k_cos, -k_sin], 1), jnp.stack([k_sin, k_cos], 1)], 1)
    wk = wide.reshape(32, 1, 32, 1) * jnp.eye(8, dtype=jnp.bfloat16)[None, :, None, :]
    wk = wk.reshape(256, 256)

    held = {}
    for part, units in PARTS.items():
        sums = partial_sums(wq, wk, own, got, units[0], len(units))
        held[part] = (sums.reshape(2, 4, 2, 4, 2, 2, len(units), 2, 8, LANES), DIMS)
    for phase in range(3):
        running = {}
        for part in PARTS:
            axis = ORDER[part][phase]
            running[part] = chunk(*held[part], axis, (place[axis] - step) % 4)
        for hop in range(3):
            for part in PARTS:
                axis = ORDER[part][phase]
                arrived = lax.ppermute(running[part][0], RING_AXES[axis], ring_pairs(axis))
                mine, dims = chunk(*held[part], axis, (place[axis] - step * (hop + 2)) % 4)
                running[part] = (arrived + mine, dims)
        held = running

    done = jnp.concatenate([held[part][0] for part in PARTS], axis=2)
    mine = lax.dynamic_index_in_dim(done, core, axis=1, keepdims=False)
    other = swap(lax.dynamic_index_in_dim(done, 1 - core, axis=1, keepdims=False))
    modes = jnp.stack([jnp.where(core == 0, mine, other), jnp.where(core == 0, other, mine)], axis=1)
    modes = modes.reshape(2, 4, 4, 2, 8, LANES)
    summed = modes.transpose(0, 4, 1, 3, 2, 5).reshape(2, 8, 4, 2, 4 * LANES)
    return rotate(summed, rot_right, rot_left)


def solution(mesh):
    fine = Mesh(mesh.devices.reshape(4, 2, 2, 2, 4), ("y", "xl", "c", "xh", "z"))
    ph, el = ("y", "xl", "c"), ("xh", "z")
    in_specs = (
        P(el, ph, None, None, None),
        P(None, el),
        P(None, ph),
        P(el),
        P(ph),
        P(),
        P(),
        P(el, None, None, None),
        P(el, ph, None, None, None),
    )
    out_specs = P(el, ph, None, None, None)
    return jax.shard_map(body, mesh=fine, in_specs=in_specs, out_specs=out_specs, check_vma=False)
```

time: 994 us -> 333 us (0.34)
  waiting for transfers between devices: 773 us -> 124 us
  matrix products: 82.6 us -> 14.2 us
  starting transfers between devices: 0.22 us -> 56.4 us
  other arithmetic: 111 us -> 59.9 us
  local copies, waits for them, and re-layouts: 12.3 us -> 43.7 us
  Pallas kernels: 0 us -> 29.2 us
  between operations: 13.6 us -> 0.97 us
    reduce_scatter x2 -> x0, waiting for transfers between devices: 773 us -> none  [the longest x1 689 us: body(): lax.psum_scatter(apply_phase('qp,rpmcx->qrmcx', q_cos, q_sin, wannier_g,...]
    ppermute x0 -> x30, waiting for transfers between devices: none -> 124 us  [the longest x27 112 us: body(): arrived = lax.ppermute(running[part][0], RING_AXES[axis], ring_pairs(axis))]
    dot_general x4 -> x0, matrix products: 69.5 us -> none  [the longest x1 29 us: apply_phase(): jnp.einsum(form, cos_table, data, preferred_element_type=jnp.float32)]
    sub x2 -> x0, other arithmetic: 66 us -> none  [combine(): real_part = cos_part[..., 0, :] - sin_part[..., 1, :]]
    ppermute x0 -> x30, starting transfers between devices: none -> 56.4 us  [the longest x27 41.9 us: body(): arrived = lax.ppermute(running[part][0], RING_AXES[axis], ring_pairs(axis))]
    add x0 -> x27, other arithmetic: none -> 45.8 us  [body(): running[part] = (arrived + mine, dims)]
    another operation x2 -> x4, other arithmetic: 43.8 us -> 0.1 us  [the longest x2 0.08 us: body(): jnp.stack([jnp.where(core == 0, mine, other), jnp.where(core == 0, other,...]
    pallas_call x0 -> x3, Pallas kernels: none -> 29.2 us  [partial_sums(): pl.pallas_call(partial_kernel, grid=(count,), in_specs=[pl.BlockSpec((256...]
  transfers between devices with their start and end apart: 2 -> 30, of which waited for: 2 -> 16; matrix products, arithmetic and copies ran while one was open for 0% -> 21% of each run, Pallas kernels for 0% -> 6%
where the time goes in v1:
time: 333 us; the launch traced here: 328 us
  waiting for transfers between devices  124 us (37%)
  other arithmetic  59.9 us (18%)
  starting transfers between devices  56.4 us (17%)
  local copies, waits for them, and re-layouts  43.7 us (13%)
  Pallas kernels  29.2 us (9%)
  matrix products  14.2 us (4%)
    ppermute x27, waiting for transfers between devices, body(): arrived = lax.ppermute(running[part][0], RING_AXES[axis], ring_pairs(axis))  112 us
    add x27, other arithmetic, body(): running[part] = (arrived + mine, dims)  45.8 us
    ppermute x27, starting transfers between devices, body(): arrived = lax.ppermute(running[part][0], RING_AXES[axis], ring_pairs(axis))  41.9 us
    pallas_call x3, Pallas kernels, partial_sums(): pl.pallas_call(partial_kernel, grid=(count,), in_specs=[pl.BlockSpec((256...  29.2 us
    ppermute x3, starting transfers between devices, body(): swap = lambda v: lax.ppermute(v, 'c', [(0, 1), (1, 0)])  14.5 us
    dynamic_slice x1, local copies, waits for them, and re-layouts, body(): sent = lax.dynamic_slice_in_dim(wannier_g, 2 - 2 * core, 2, axis=2)  14.4 us
    convert_element_type x1, other arithmetic, body(): got = swap(sent.transpose(0, 2, 3, 1, 4).astype(jnp.float32))  12.6 us
    ppermute x3, waiting for transfers between devices, body(): swap = lambda v: lax.ppermute(v, 'c', [(0, 1), (1, 0)])  11.5 us
  transfers between devices with their start and end apart: 30, of which 16 were waited for; matrix products, arithmetic and copies ran while one was open for 21% of the time, Pallas kernels for 6%

profile of v1, /device:TPU:1, one launch (start us, length us, event | category | flops | bytes accessed | tf_op | source)
XLA Modules:
  0.0 328.2 jit_solution(10352810631786929469)
XLA Ops:
  0.0 14.4 %constant_dynamic-slice_fusion = (bf16[16,64,2,2,1024]{4,3,2,1,0:T(2,128)(2,1)}, bf16[16,64,2,2,1024]{4,3,2,1,0:T(2,128)(2,1)}) fusion(bf16[16,64,4,2,1024]{4,3,2,1,0:T(2,128)(2,1)} %param.9, s32[]{:T(128)S(6)} %select_n.259, s32[]{:T(128)S(6)} %select_n.258), kind=kLoop, calls=%fused_computation.80 | loop fusion | bytes 33554440 | tf_op jit(solution)/shard_map/dynamic_slice | solution.py:132
  14.4 12.6 %convert_bitcast_fusion = f32[16,2,2,64,1024]{4,3,2,1,0:T(8,128)} fusion(bf16[16,64,2,2,1024]{4,3,2,1,0:T(2,128)(2,1)} %get-tuple-element.5), kind=kLoop, calls=%fused_computation | loop fusion | flops 4194304 | bytes 25165824 | tf_op jit(solution)/shard_map/convert_element_type | solution.py:133
  27.1 1.4 collective-permute-start.1
  29.6 2.9 mul.318.wk_ref
  32.4 10.1 %copy.174 = bf16[16,64,2,2,1024]{4,1,3,2,0:T(8,128)(2,1)} copy(bf16[16,64,2,2,1024]{4,3,2,1,0:T(2,128)(2,1)} %get-tuple-element.6) | data formatting | bytes 16777216
  43.3 10.3 %collective-permute-done.1.got_ref = f32[16,2,2,64,1024]{4,3,2,1,0:T(8,128)} collective-permute-done((f32[16,2,2,64,1024]{4,3,2,1,0:T(8,128)}, f32[16,2,2,64,1024]{4,3,2,1,0:T(8,128)}, u32[]{:S(2)}, u32[]{:S(2)}) %collective-permute-start.1) | collective-permute-done | bytes 16777248 | tf_op jit(solution)/shard_map/ppermute | solution.py:130
  53.6 11.1 %shard_map.92 = f32[16,16,3,2,8,256]{5,4,3,2,1,0:T(8,128)} custom-call(bf16[256,256]{1,0:T(8,128)(2,1)S(1)} %maximum_maximum_fusion.wq_ref, bf16[256,256]{1,0:T(8,128)(2,1)S(1)} %mul.318.wk_ref, bf16[16,2,2,64,1024]{4,3,2,1,0:T(8,128)(2,1)} %bitcast.221, f32[16,2,2,64,1024]{4,3,2,1,0:T(8,128)} %collective-permute-done.1.got_ref), custom_call_target="tpu_custom_call" | custom-call | flops 3221225472 | bytes 22020096 | tf_op jit(solution)/shard_map/pallas_call | solution.py:40
  64.7 2.2 dynamic-slice_bitcast_fusion
  67.0 2.6 collective-permute-start.11
  69.6 11.3 %shard_map.91 = f32[16,16,3,2,8,256]{5,4,3,2,1,0:T(8,128)} custom-call(bf16[256,256]{1,0:T(8,128)(2,1)S(1)} %maximum_maximum_fusion.wq_ref, bf16[256,256]{1,0:T(8,128)(2,1)S(1)} %mul.318.wk_ref, bf16[16,2,2,64,1024]{4,3,2,1,0:T(8,128)(2,1)} %bitcast.222, f32[16,2,2,64,1024]{4,3,2,1,0:T(8,128)} %collective-permute-done.1.got_ref), custom_call_target="tpu_custom_call" | custom-call | flops 3221225472 | bytes 22020096 | tf_op jit(solution)/shard_map/pallas_call | solution.py:40
  80.9 4.1 %dynamic-slice_bitcast_fusion.1 = f32[2,2,4,2,2,3,2,8,256]{8,7,6,5,4,3,2,1,0:T(8,128)} fusion(f32[2,4,2,4,2,2,3,2,8,256]{9,8,7,6,5,4,3,2,1,0:T(8,128)} %bitcast.228, s32[]{:T(128)S(6)} %select_n.261), kind=kLoop, calls=%fused_computation.9 | loop fusion | bytes 6291460 | tf_op jit(solution)/shard_map/reshape | solution.py:71
  85.0 3.8 %collective-permute-start.2 = (f32[2,2,4,2,2,3,2,8,256]{8,7,6,5,4,3,2,1,0:T(8,128)}, f32[2,2,4,2,2,3,2,8,256]{8,7,6,5,4,3,2,1,0:T(8,128)}, u32[]{:S(2)}, u32[]{:S(2)}) collective-permute-start(f32[2,2,4,2,2,3,2,8,256]{8,7,6,5,4,3,2,1,0:T(8,128)} %dynamic-slice_bitcast_fusion.1), channel_id=1, source_target_pairs={{0,1},{1,2},{2,3},{3,0},{8,11},{9,8},{10,9},{11,10},{4,5},{5,6},{6... | collective-permute-start | bytes 9437192 | tf_op jit(solution)/shard_map/ppermute | solution.py:156
  88.8 6.8 %shard_map.93 = f32[16,16,2,2,8,256]{5,4,3,2,1,0:T(8,128)} custom-call(bf16[256,256]{1,0:T(8,128)(2,1)S(1)} %maximum_maximum_fusion.wq_ref, bf16[256,256]{1,0:T(8,128)(2,1)S(1)} %mul.318.wk_ref, bf16[16,2,2,64,1024]{4,3,2,1,0:T(8,128)(2,1)} %bitcast.223, f32[16,2,2,64,1024]{4,3,2,1,0:T(8,128)} %collective-permute-done.1.got_ref), custom_call_target="tpu_custom_call" | custom-call | flops 2147483648 | bytes 14680064 | tf_op jit(solution)/shard_map/pallas_call | solution.py:40
  95.6 3.3 dynamic-slice_bitcast_fusion.2
  98.9 3.1 collective-permute-start.20
  102.0 1.8 collective-permute-done.11
  103.8 3.6 %bitcast_add_fusion.2 = f32[4,2,4,2,3,2,8,256]{7,6,5,4,3,2,1,0:T(8,128)S(1)} fusion(f32[4,2,4,2,3,2,8,256]{7,6,5,4,3,2,1,0:T(8,128)} %collective-permute-done.11, f32[2,4,2,4,2,2,3,2,8,256]{9,8,7,6,5,4,3,2,1,0:T(8,128)} %bitcast.225, s32[]{:T(128)S(6)} %select_n.275, s32[]{:T(128)S(6)} %select_n.277), kind=kLoop, calls=%fused_computation.4 | loop fusion | flops 786432 | bytes 9437192 | tf_op jit(solution)/shard_map/add | solution.py:158
  107.4 3.6 %collective-permute-start.12 = (f32[4,2,4,2,3,2,8,256]{7,6,5,4,3,2,1,0:T(8,128)S(1)}, f32[4,2,4,2,3,2,8,256]{7,6,5,4,3,2,1,0:T(8,128)}, u32[]{:S(2)}, u32[]{:S(2)}) collective-permute-start(f32[4,2,4,2,3,2,8,256]{7,6,5,4,3,2,1,0:T(8,128)S(1)} %bitcast_add_fusion.2), channel_id=1, source_target_pairs={{0,16},{16,4},{4,20},{20,0},{8,28},{24,8},{12,24},{28,12},{1,17},{... | collective-permute-start | bytes 9437192 | tf_op jit(solution)/shard_map/ppermute | solution.py:156
  111.0 12.3 %collective-permute-done.2 = f32[2,2,4,2,2,3,2,8,256]{8,7,6,5,4,3,2,1,0:T(8,128)} collective-permute-done((f32[2,2,4,2,2,3,2,8,256]{8,7,6,5,4,3,2,1,0:T(8,128)}, f32[2,2,4,2,2,3,2,8,256]{8,7,6,5,4,3,2,1,0:T(8,128)}, u32[]{:S(2)}, u32[]{:S(2)}) %collective-permute-start.2) | collective-permute-done | bytes 3145760 | tf_op jit(solution)/shard_map/ppermute | solution.py:156
  123.3 5.6 %bitcast_add_fusion.5 = f32[2,2,4,2,2,3,2,8,256]{8,7,6,5,4,3,2,1,0:T(8,128)} fusion(f32[2,2,4,2,2,3,2,8,256]{8,7,6,5,4,3,2,1,0:T(8,128)} %collective-permute-done.2, f32[2,4,2,4,2,2,3,2,8,256]{9,8,7,6,5,4,3,2,1,0:T(8,128)} %bitcast.229, s32[]{:T(128)S(6)} %select_n.263), kind=kLoop, calls=%fused_computation.7 | loop fusion | flops 786432 | bytes 9437188 | tf_op jit(solution)/shard_map/add | solution.py:158
  128.9 3.4 %collective-permute-start.3 = (f32[2,2,4,2,2,3,2,8,256]{8,7,6,5,4,3,2,1,0:T(8,128)}, f32[2,2,4,2,2,3,2,8,256]{8,7,6,5,4,3,2,1,0:T(8,128)}, u32[]{:S(2)}, u32[]{:S(2)}) collective-permute-start(f32[2,2,4,2,2,3,2,8,256]{8,7,6,5,4,3,2,1,0:T(8,128)} %bitcast_add_fusion.5), channel_id=1, source_target_pairs={{0,1},{1,2},{2,3},{3,0},{8,11},{9,8},{10,9},{11,10},{4,5},{5,6},{6... | collective-permute-start | bytes 9437192 | tf_op jit(solution)/shard_map/ppermute | solution.py:156
  132.3 4.3 %bitcast_add_fusion.8 = f32[2,4,2,2,2,2,2,8,256]{8,7,6,5,4,3,2,1,0:T(8,128)} fusion(f32[2,4,2,2,2,2,2,8,256]{8,7,6,5,4,3,2,1,0:T(8,128)} %collective-permute-done.20, f32[2,4,2,4,2,2,2,2,8,256]{9,8,7,6,5,4,3,2,1,0:T(8,128)} %bitcast.233, s32[]{:T(128)S(6)} %select_n.291), kind=kLoop, calls=%fused_computation.12 | loop fusion | flops 524288 | bytes 6291460 | tf_op jit(solution)/shard_map/add | solution.py:158
  136.6 2.7 collective-permute-start.21
  139.3 23.3 %collective-permute-done.21 = f32[2,4,2,2,2,2,2,8,256]{8,7,6,5,4,3,2,1,0:T(8,128)} collective-permute-done((f32[2,4,2,2,2,2,2,8,256]{8,7,6,5,4,3,2,1,0:T(8,128)}, f32[2,4,2,2,2,2,2,8,256]{8,7,6,5,4,3,2,1,0:T(8,128)}, u32[]{:S(2)}, u32[]{:S(2)}) %collective-permute-start.21) | collective-permute-done | bytes 2097184 | tf_op jit(solution)/shard_map/ppermute | solution.py:156
  162.6 4.2 %bitcast_add_fusion.7 = f32[2,4,2,2,2,2,2,8,256]{8,7,6,5,4,3,2,1,0:T(8,128)} fusion(f32[2,4,2,2,2,2,2,8,256]{8,7,6,5,4,3,2,1,0:T(8,128)} %collective-permute-done.21, f32[2,4,2,4,2,2,2,2,8,256]{9,8,7,6,5,4,3,2,1,0:T(8,128)} %bitcast.234, s32[]{:T(128)S(6)} %select_n.293), kind=kLoop, calls=%fused_computation.11 | loop fusion | flops 524288 | bytes 6291460 | tf_op jit(solution)/shard_map/add | solution.py:158
  166.8 3.4 %collective-permute-start.22 = (f32[2,4,2,2,2,2,2,8,256]{8,7,6,5,4,3,2,1,0:T(8,128)}, f32[2,4,2,2,2,2,2,8,256]{8,7,6,5,4,3,2,1,0:T(8,128)}, u32[]{:S(2)}, u32[]{:S(2)}) collective-permute-start(f32[2,4,2,2,2,2,2,8,256]{8,7,6,5,4,3,2,1,0:T(8,128)} %bitcast_add_fusion.7), channel_id=1, source_target_pairs={{0,32},{32,64},{64,96},{96,0},{8,104},{40,8},{72,40},{104,72},{1,3... | collective-permute-start | bytes 6291464 | tf_op jit(solution)/shard_map/ppermute | solution.py:156
  170.2 5.6 %bitcast_add_fusion.1 = f32[4,2,4,2,3,2,8,256]{7,6,5,4,3,2,1,0:T(8,128)} fusion(f32[4,2,4,2,3,2,8,256]{7,6,5,4,3,2,1,0:T(8,128)} %collective-permute-done.12, f32[2,4,2,4,2,2,3,2,8,256]{9,8,7,6,5,4,3,2,1,0:T(8,128)} %bitcast.226, s32[]{:T(128)S(6)} %select_n.280, s32[]{:T(128)S(6)} %select_n.282), kind=kLoop, calls=%fused_computation.3 | loop fusion | flops 786432 | bytes 9437192 | tf_op jit(solution)/shard_map/add | solution.py:158
  176.1 5.6 %bitcast_add_fusion.4 = f32[2,2,4,2,2,3,2,8,256]{8,7,6,5,4,3,2,1,0:T(8,128)} fusion(f32[2,2,4,2,2,3,2,8,256]{8,7,6,5,4,3,2,1,0:T(8,128)} %collective-permute-done.3, f32[2,4,2,4,2,2,3,2,8,256]{9,8,7,6,5,4,3,2,1,0:T(8,128)} %bitcast.230, s32[]{:T(128)S(6)} %select_n.265), kind=kLoop, calls=%fused_computation.6 | loop fusion | flops 786432 | bytes 9437188 | tf_op jit(solution)/shard_map/add | solution.py:158
  181.7 11.9 %collective-permute-done.22 = f32[2,4,2,2,2,2,2,8,256]{8,7,6,5,4,3,2,1,0:T(8,128)} collective-permute-done((f32[2,4,2,2,2,2,2,8,256]{8,7,6,5,4,3,2,1,0:T(8,128)}, f32[2,4,2,2,2,2,2,8,256]{8,7,6,5,4,3,2,1,0:T(8,128)}, u32[]{:S(2)}, u32[]{:S(2)}) %collective-permute-start.22) | collective-permute-done | bytes 2097184 | tf_op jit(solution)/shard_map/ppermute | solution.py:156
  193.5 2.7 bitcast_add_fusion.6
  196.5 27.1 %collective-permute-done.23 = f32[2,2,2,2,2,2,8,256]{7,6,5,4,3,2,1,0:T(8,128)S(1)} collective-permute-done((f32[2,2,2,2,2,2,8,256]{7,6,5,4,3,2,1,0:T(8,128)S(1)}, f32[2,2,2,2,2,2,8,256]{7,6,5,4,3,2,1,0:T(8,128)S(1)}, u32[]{:S(2)}, u32[]{:S(2)}) %collective-permute-start.23) | collective-permute-done | bytes 524320 | tf_op jit(solution)/shard_map/ppermute | solution.py:156
  223.7 1.3 collective-permute-start.24
  225.0 3.6 %bitcast_add_fusion = f32[4,2,4,2,3,2,8,256]{7,6,5,4,3,2,1,0:T(8,128)S(1)} fusion(f32[4,2,4,2,3,2,8,256]{7,6,5,4,3,2,1,0:T(8,128)} %collective-permute-done.13, f32[2,4,2,4,2,2,3,2,8,256]{9,8,7,6,5,4,3,2,1,0:T(8,128)} %bitcast.227, s32[]{:T(128)S(6)} %select_n.285, s32[]{:T(128)S(6)} %select_n.287), kind=kLoop, calls=%fused_computation.2 | loop fusion | flops 786432 | bytes 9437192 | tf_op jit(solution)/shard_map/add | solution.py:158
  228.8 4.0 %bitcast_add_fusion.3 = f32[2,2,4,2,2,3,2,8,256]{8,7,6,5,4,3,2,1,0:T(8,128)S(1)} fusion(f32[2,2,4,2,2,3,2,8,256]{8,7,6,5,4,3,2,1,0:T(8,128)} %collective-permute-done.4, f32[2,4,2,4,2,2,3,2,8,256]{9,8,7,6,5,4,3,2,1,0:T(8,128)} %bitcast.231, s32[]{:T(128)S(6)} %select_n.267), kind=kLoop, calls=%fused_computation.5 | loop fusion | flops 786432 | bytes 9437188 | tf_op jit(solution)/shard_map/add | solution.py:158
  233.3 1.3 collective-permute-start.25
  234.7 5.2 %collective-permute-done.14 = f32[4,2,2,3,2,8,256]{6,5,4,3,2,1,0:T(8,128)S(1)} collective-permute-done((f32[4,2,2,3,2,8,256]{6,5,4,3,2,1,0:T(8,128)S(1)}, f32[4,2,2,3,2,8,256]{6,5,4,3,2,1,0:T(8,128)S(1)}, u32[]{:S(2)}, u32[]{:S(2)}) %collective-permute-start.14) | collective-permute-done | bytes 786464 | tf_op jit(solution)/shard_map/ppermute | solution.py:156
  240.1 1.5 collective-permute-start.15
  241.5 2.6 collective-permute-done.5
  244.3 1.5 collective-permute-start.6
  246.1 10.8 %collective-permute-done.26 = f32[2,2,2,2,8,256]{5,4,3,2,1,0:T(8,128)S(1)} collective-permute-done((f32[2,2,2,2,8,256]{5,4,3,2,1,0:T(8,128)S(1)}, f32[2,2,2,2,8,256]{5,4,3,2,1,0:T(8,128)S(1)}, u32[]{:S(2)}, u32[]{:S(2)}) %collective-permute-start.26) | collective-permute-done | bytes 131104 | tf_op jit(solution)/shard_map/ppermute | solution.py:156
  256.9 2.5 collective-permute-start.27
  259.4 1.0 bitcast_add_fusion.10
  260.4 1.0 bitcast_add_fusion.13
  261.5 3.0 collective-permute-start.28
  264.5 9.8 %collective-permute-done.28 = f32[2,2,2,2,8,256]{5,4,3,2,1,0:T(8,128)S(1)} collective-permute-done((f32[2,2,2,2,8,256]{5,4,3,2,1,0:T(8,128)S(1)}, f32[2,2,2,2,8,256]{5,4,3,2,1,0:T(8,128)S(1)}, u32[]{:S(2)}, u32[]{:S(2)}) %collective-permute-start.28) | collective-permute-done | bytes 131104 | tf_op jit(solution)/shard_map/ppermute | solution.py:156
  275.3 1.3 bitcast_add_fusion.9
  276.7 1.5 bitcast_add_fusion.12
  278.3 2.8 collective-permute-done.17
  281.2 1.3 collective-permute-start.18
  282.9 1.5 collective-permute-start.9
  284.4 1.4 collective-permute-done.18
  285.8 2.5 collective-permute-start.19
  288.3 1.9 collective-permute-start.10
  291.0 2.3 collective-permute-done.10
  293.3 12.8 %collective-permute-start.29 = (f32[2,8,2,8,256]{4,3,2,1,0:T(8,128)S(1)}, f32[2,8,2,8,256]{4,3,2,1,0:T(8,128)S(1)}, u32[]{:S(2)}, u32[]{:S(2)}) collective-permute-start(f32[2,8,2,8,256]{4,3,2,1,0:T(8,128)S(1)} %dynamic-slice_bitcast_fusion.6), channel_id=1, source_target_pairs={{0,8},{8,0},{1,9},{9,1},{2,10},{10,2},{3,11},{11,3},{4,12},{12,4},... | collective-permute-start | bytes 786440 | tf_op jit(solution)/shard_map/ppermute | solution.py:130
  306.1 1.2 collective-permute-done.29
  310.5 1.0 convolution_add_fusion
  312.5 1.8 fusion.6
  314.3 1.8 fusion.8
  316.1 2.8 fusion
  318.9 1.6 copy.144
  321.0 3.8 %fusion.1 = f32[2,8,4,32,32]{3,4,2,1,0:T(8,128)} fusion(f32[2,8,4,32,32]{4,3,2,1,0:T(8,128)S(1)} %fusion.8, f32[2,8,4,32,32]{4,3,2,1,0:T(8,128)S(1)} %convolution_add_fusion, f32[2,8,2,32,32]{4,3,2,1,0:T(8,128)} %param.17), kind=kOutput, calls=%fused_computation.19 | convolution fusion | flops 25231360 | bytes 1048576 | tf_op jit(solution)/shard_map/kqai,kqmac->kqmic/dot_general | solution.py:105
  324.7 1.6 copy.141
  326.8 1.2 copy.145
  (102 shorter events, 11.0 us)
Async XLA Ops:
  14.4 14.1 %copy-start.6 = (s32[3,64]{1,0:T(4,128)S(1)}, s32[3,64]{1,0:T(4,128)}, u32[]{:S(2)}) copy-start(s32[3,64]{1,0:T(4,128)} %param.11) | copy-start | bytes 2308
  14.4 14.1 %copy-start.10 = (s32[64]{0:T(128)S(1)}, s32[64]{0:T(128)}, u32[]{:S(2)}) copy-start(s32[64]{0:T(128)} %param.13) | copy-start | bytes 772
  14.4 14.4 %copy-start.7 = (s32[3,16]{1,0:T(4,128)S(1)}, s32[3,16]{1,0:T(4,128)}, u32[]{:S(2)}) copy-start(s32[3,16]{1,0:T(4,128)} %param.10) | copy-start | bytes 580
  14.4 14.4 %copy-start.11 = (s32[16]{0:T(128)S(1)}, s32[16]{0:T(128)}, u32[]{:S(2)}) copy-start(s32[16]{0:T(128)} %param.12) | copy-start | bytes 196
  14.4 14.5 %copy-start.9 = (f32[3,16]{1,0:T(4,128)S(1)}, f32[3,16]{1,0:T(4,128)}, u32[]{:S(2)}) copy-start(f32[3,16]{1,0:T(4,128)} %param.14) | copy-start | bytes 580
  14.4 14.9 %copy-start.8 = (f32[3,128]{1,0:T(4,128)S(1)}, f32[3,128]{1,0:T(4,128)}, u32[]{:S(2)}) copy-start(f32[3,128]{1,0:T(4,128)} %param.15) | copy-start | bytes 4612
  27.1 26.5 %collective-permute-start.1 = (f32[16,2,2,64,1024]{4,3,2,1,0:T(8,128)}, f32[16,2,2,64,1024]{4,3,2,1,0:T(8,128)}, u32[]{:S(2)}, u32[]{:S(2)}) collective-permute-start(f32[16,2,2,64,1024]{4,3,2,1,0:T(8,128)} %convert_bitcast_fusion), channel_id=1, source_target_pairs={{0,8},{8,0},{1,9},{9,1},{2,10},{10,2},{3,11},{11,3},{4,12},{12,4},... | collective-permute-start | bytes 50331656 | tf_op jit(solution)/shard_map/ppermute | solution.py:130
  28.5 14.0 %collective-permute-start = (f32[4,64]{1,0:T(4,128)S(1)}, f32[4,64]{1,0:T(4,128)S(1)}, u32[]{:S(2)}, u32[]{:S(2)}) collective-permute-start(f32[4,64]{1,0:T(4,128)S(1)} %add_convert_fusion), channel_id=1, source_target_pairs={{0,8},{8,0},{1,9},{9,1},{2,10},{10,2},{3,11},{11,3},{4,12},{12,4},... | collective-permute-start | bytes 3080 | tf_op jit(solution)/shard_map/ppermute | solution.py:130
  67.0 36.8 %collective-permute-start.11 = (f32[4,2,4,2,3,2,8,256]{7,6,5,4,3,2,1,0:T(8,128)S(1)}, f32[4,2,4,2,3,2,8,256]{7,6,5,4,3,2,1,0:T(8,128)}, u32[]{:S(2)}, u32[]{:S(2)}) collective-permute-start(f32[4,2,4,2,3,2,8,256]{7,6,5,4,3,2,1,0:T(8,128)S(1)} %dynamic-slice_bitcast_fusion), channel_id=1, source_target_pairs={{0,16},{16,4},{4,20},{20,0},{8,28},{24,8},{12,24},{28,12},{1,17},{... | collective-permute-start | bytes 9437192 | tf_op jit(solution)/shard_map/ppermute | solution.py:156
  85.0 38.3 %collective-permute-start.2 = (f32[2,2,4,2,2,3,2,8,256]{8,7,6,5,4,3,2,1,0:T(8,128)}, f32[2,2,4,2,2,3,2,8,256]{8,7,6,5,4,3,2,1,0:T(8,128)}, u32[]{:S(2)}, u32[]{:S(2)}) collective-permute-start(f32[2,2,4,2,2,3,2,8,256]{8,7,6,5,4,3,2,1,0:T(8,128)} %dynamic-slice_bitcast_fusion.1), channel_id=1, source_target_pairs={{0,1},{1,2},{2,3},{3,0},{8,11},{9,8},{10,9},{11,10},{4,5},{5,6},{6... | collective-permute-start | bytes 9437192 | tf_op jit(solution)/shard_map/ppermute | solution.py:156
  98.9 33.4 %collective-permute-start.20 = (f32[2,4,2,2,2,2,2,8,256]{8,7,6,5,4,3,2,1,0:T(8,128)}, f32[2,4,2,2,2,2,2,8,256]{8,7,6,5,4,3,2,1,0:T(8,128)}, u32[]{:S(2)}, u32[]{:S(2)}) collective-permute-start(f32[2,4,2,2,2,2,2,8,256]{8,7,6,5,4,3,2,1,0:T(8,128)} %dynamic-slice_bitcast_fusion.2), channel_id=1, source_target_pairs={{0,32},{32,64},{64,96},{96,0},{8,104},{40,8},{72,40},{104,72},{1,3... | collective-permute-start | bytes 6291464 | tf_op jit(solution)/shard_map/ppermute | solution.py:156
  107.4 62.8 %collective-permute-start.12 = (f32[4,2,4,2,3,2,8,256]{7,6,5,4,3,2,1,0:T(8,128)S(1)}, f32[4,2,4,2,3,2,8,256]{7,6,5,4,3,2,1,0:T(8,128)}, u32[]{:S(2)}, u32[]{:S(2)}) collective-permute-start(f32[4,2,4,2,3,2,8,256]{7,6,5,4,3,2,1,0:T(8,128)S(1)} %bitcast_add_fusion.2), channel_id=1, source_target_pairs={{0,16},{16,4},{4,20},{20,0},{8,28},{24,8},{12,24},{28,12},{1,17},{... | collective-permute-start | bytes 9437192 | tf_op jit(solution)/shard_map/ppermute | solution.py:156
  128.9 47.2 %collective-permute-start.3 = (f32[2,2,4,2,2,3,2,8,256]{8,7,6,5,4,3,2,1,0:T(8,128)}, f32[2,2,4,2,2,3,2,8,256]{8,7,6,5,4,3,2,1,0:T(8,128)}, u32[]{:S(2)}, u32[]{:S(2)}) collective-permute-start(f32[2,2,4,2,2,3,2,8,256]{8,7,6,5,4,3,2,1,0:T(8,128)} %bitcast_add_fusion.5), channel_id=1, source_target_pairs={{0,1},{1,2},{2,3},{3,0},{8,11},{9,8},{10,9},{11,10},{4,5},{5,6},{6... | collective-permute-start | bytes 9437192 | tf_op jit(solution)/shard_map/ppermute | solution.py:156
  136.6 26.0 %collective-permute-start.21 = (f32[2,4,2,2,2,2,2,8,256]{8,7,6,5,4,3,2,1,0:T(8,128)}, f32[2,4,2,2,2,2,2,8,256]{8,7,6,5,4,3,2,1,0:T(8,128)}, u32[]{:S(2)}, u32[]{:S(2)}) collective-permute-start(f32[2,4,2,2,2,2,2,8,256]{8,7,6,5,4,3,2,1,0:T(8,128)} %bitcast_add_fusion.8), channel_id=1, source_target_pairs={{0,32},{32,64},{64,96},{96,0},{8,104},{40,8},{72,40},{104,72},{1,3... | collective-permute-start | bytes 6291464 | tf_op jit(solution)/shard_map/ppermute | solution.py:156
  166.8 26.7 %collective-permute-start.22 = (f32[2,4,2,2,2,2,2,8,256]{8,7,6,5,4,3,2,1,0:T(8,128)}, f32[2,4,2,2,2,2,2,8,256]{8,7,6,5,4,3,2,1,0:T(8,128)}, u32[]{:S(2)}, u32[]{:S(2)}) collective-permute-start(f32[2,4,2,2,2,2,2,8,256]{8,7,6,5,4,3,2,1,0:T(8,128)} %bitcast_add_fusion.7), channel_id=1, source_target_pairs={{0,32},{32,64},{64,96},{96,0},{8,104},{40,8},{72,40},{104,72},{1,3... | collective-permute-start | bytes 6291464 | tf_op jit(solution)/shard_map/ppermute | solution.py:156
  175.8 49.2 %collective-permute-start.13 = (f32[4,2,4,2,3,2,8,256]{7,6,5,4,3,2,1,0:T(8,128)}, f32[4,2,4,2,3,2,8,256]{7,6,5,4,3,2,1,0:T(8,128)}, u32[]{:S(2)}, u32[]{:S(2)}) collective-permute-start(f32[4,2,4,2,3,2,8,256]{7,6,5,4,3,2,1,0:T(8,128)} %bitcast_add_fusion.1), channel_id=1, source_target_pairs={{0,16},{16,4},{4,20},{20,0},{8,28},{24,8},{12,24},{28,12},{1,17},{... | collective-permute-start | bytes 9437192 | tf_op jit(solution)/shard_map/ppermute | solution.py:156
  181.7 47.2 %collective-permute-start.4 = (f32[2,2,4,2,2,3,2,8,256]{8,7,6,5,4,3,2,1,0:T(8,128)}, f32[2,2,4,2,2,3,2,8,256]{8,7,6,5,4,3,2,1,0:T(8,128)}, u32[]{:S(2)}, u32[]{:S(2)}) collective-permute-start(f32[2,2,4,2,2,3,2,8,256]{8,7,6,5,4,3,2,1,0:T(8,128)} %bitcast_add_fusion.4), channel_id=1, source_target_pairs={{0,1},{1,2},{2,3},{3,0},{8,11},{9,8},{10,9},{11,10},{4,5},{5,6},{6... | collective-permute-start | bytes 9437192 | tf_op jit(solution)/shard_map/ppermute | solution.py:156
  196.2 28.8 %copy-start.1 = (f32[2,4,2,2,2,2,2,8,256]{8,7,6,5,4,3,2,1,0:T(8,128)}, f32[2,4,2,2,2,2,2,8,256]{8,7,6,5,4,3,2,1,0:T(8,128)S(1)}, u32[]{:S(2)}) copy-start(f32[2,4,2,2,2,2,2,8,256]{8,7,6,5,4,3,2,1,0:T(8,128)S(1)} %bitcast_add_fusion.6) | copy-start | bytes 6291460
  196.3 27.3 %collective-permute-start.23 = (f32[2,2,2,2,2,2,8,256]{7,6,5,4,3,2,1,0:T(8,128)S(1)}, f32[2,2,2,2,2,2,8,256]{7,6,5,4,3,2,1,0:T(8,128)S(1)}, u32[]{:S(2)}, u32[]{:S(2)}) collective-permute-start(f32[2,2,2,2,2,2,8,256]{7,6,5,4,3,2,1,0:T(8,128)S(1)} %dynamic-slice_bitcast_fusion.5), channel_id=1, source_target_pairs={{0,1},{1,2},{2,3},{3,0},{8,11},{9,8},{10,9},{11,10},{4,5},{5,6},{6... | collective-permute-start | bytes 1572872 | tf_op jit(solution)/shard_map/ppermute | solution.py:156
  223.7 9.5 %collective-permute-start.24 = (f32[2,2,2,2,2,2,8,256]{7,6,5,4,3,2,1,0:T(8,128)S(1)}, f32[2,2,2,2,2,2,8,256]{7,6,5,4,3,2,1,0:T(8,128)S(1)}, u32[]{:S(2)}, u32[]{:S(2)}) collective-permute-start(f32[2,2,2,2,2,2,8,256]{7,6,5,4,3,2,1,0:T(8,128)S(1)} %bitcast_add_fusion.17), channel_id=1, source_target_pairs={{0,1},{1,2},{2,3},{3,0},{8,11},{9,8},{10,9},{11,10},{4,5},{5,6},{6... | collective-permute-start | bytes 1572872 | tf_op jit(solution)/shard_map/ppermute | solution.py:156
  228.7 4.5 %copy-start.2 = (f32[2,4,2,2,2,2,2,8,256]{8,7,6,5,4,3,2,1,0:T(8,128)S(1)}, f32[2,4,2,2,2,2,2,8,256]{8,7,6,5,4,3,2,1,0:T(8,128)}, u32[]{:S(2)}) copy-start(f32[2,4,2,2,2,2,2,8,256]{8,7,6,5,4,3,2,1,0:T(8,128)} %copy-done.1) | copy-start | bytes 6291460
  228.7 11.2 %collective-permute-start.14 = (f32[4,2,2,3,2,8,256]{6,5,4,3,2,1,0:T(8,128)S(1)}, f32[4,2,2,3,2,8,256]{6,5,4,3,2,1,0:T(8,128)S(1)}, u32[]{:S(2)}, u32[]{:S(2)}) collective-permute-start(f32[4,2,2,3,2,8,256]{6,5,4,3,2,1,0:T(8,128)S(1)} %dynamic-slice_bitcast_fusion.3), channel_id=1, source_target_pairs={{0,32},{32,64},{64,96},{96,0},{8,104},{40,8},{72,40},{104,72},{1,3... | collective-permute-start | bytes 2359304 | tf_op jit(solution)/shard_map/ppermute | solution.py:156
  232.8 27.6 %copy-start = (f32[2,2,4,2,2,3,2,8,256]{8,7,6,5,4,3,2,1,0:T(8,128)}, f32[2,2,4,2,2,3,2,8,256]{8,7,6,5,4,3,2,1,0:T(8,128)S(1)}, u32[]{:S(2)}) copy-start(f32[2,2,4,2,2,3,2,8,256]{8,7,6,5,4,3,2,1,0:T(8,128)S(1)} %bitcast_add_fusion.3) | copy-start | bytes 9437188
  232.9 11.2 %collective-permute-start.5 = (f32[2,4,2,3,2,8,256]{6,5,4,3,2,1,0:T(8,128)S(1)}, f32[2,4,2,3,2,8,256]{6,5,4,3,2,1,0:T(8,128)S(1)}, u32[]{:S(2)}, u32[]{:S(2)}) collective-permute-start(f32[2,4,2,3,2,8,256]{6,5,4,3,2,1,0:T(8,128)S(1)} %dynamic-slice_bitcast_fusion.4), channel_id=1, source_target_pairs={{0,16},{16,4},{4,20},{20,0},{8,28},{24,8},{12,24},{28,12},{1,17},{... | collective-permute-start | bytes 2359304 | tf_op jit(solution)/shard_map/ppermute | solution.py:156
  233.3 12.5 %collective-permute-start.25 = (f32[2,2,2,2,2,2,8,256]{7,6,5,4,3,2,1,0:T(8,128)S(1)}, f32[2,2,2,2,2,2,8,256]{7,6,5,4,3,2,1,0:T(8,128)S(1)}, u32[]{:S(2)}, u32[]{:S(2)}) collective-permute-start(f32[2,2,2,2,2,2,8,256]{7,6,5,4,3,2,1,0:T(8,128)S(1)} %bitcast_add_fusion.16), channel_id=1, source_target_pairs={{0,1},{1,2},{2,3},{3,0},{8,11},{9,8},{10,9},{11,10},{4,5},{5,6},{6... | collective-permute-start | bytes 1572872 | tf_op jit(solution)/shard_map/ppermute | solution.py:156
  240.1 19.3 %collective-permute-start.15 = (f32[4,2,2,3,2,8,256]{6,5,4,3,2,1,0:T(8,128)S(1)}, f32[4,2,2,3,2,8,256]{6,5,4,3,2,1,0:T(8,128)S(1)}, u32[]{:S(2)}, u32[]{:S(2)}) collective-permute-start(f32[4,2,2,3,2,8,256]{6,5,4,3,2,1,0:T(8,128)S(1)} %bitcast_add_fusion.11), channel_id=1, source_target_pairs={{0,32},{32,64},{64,96},{96,0},{8,104},{40,8},{72,40},{104,72},{1,3... | collective-permute-start | bytes 2359304 | tf_op jit(solution)/shard_map/ppermute | solution.py:156
  244.3 16.1 %collective-permute-start.6 = (f32[2,4,2,3,2,8,256]{6,5,4,3,2,1,0:T(8,128)S(1)}, f32[2,4,2,3,2,8,256]{6,5,4,3,2,1,0:T(8,128)S(1)}, u32[]{:S(2)}, u32[]{:S(2)}) collective-permute-start(f32[2,4,2,3,2,8,256]{6,5,4,3,2,1,0:T(8,128)S(1)} %bitcast_add_fusion.14), channel_id=1, source_target_pairs={{0,16},{16,4},{4,20},{20,0},{8,28},{24,8},{12,24},{28,12},{1,17},{... | collective-permute-start | bytes 2359304 | tf_op jit(solution)/shard_map/ppermute | solution.py:156
  245.9 15.6 %copy-start.3 = (f32[2,2,2,2,2,2,8,256]{7,6,5,4,3,2,1,0:T(8,128)}, f32[2,2,2,2,2,2,8,256]{7,6,5,4,3,2,1,0:T(8,128)S(1)}, u32[]{:S(2)}) copy-start(f32[2,2,2,2,2,2,8,256]{7,6,5,4,3,2,1,0:T(8,128)S(1)} %bitcast_add_fusion.15) | copy-start | bytes 1572868
  246.0 10.9 %collective-permute-start.26 = (f32[2,2,2,2,8,256]{5,4,3,2,1,0:T(8,128)S(1)}, f32[2,2,2,2,8,256]{5,4,3,2,1,0:T(8,128)S(1)}, u32[]{:S(2)}, u32[]{:S(2)}) collective-permute-start(f32[2,2,2,2,8,256]{5,4,3,2,1,0:T(8,128)S(1)} %dynamic-slice_bitcast_fusion.9), channel_id=1, source_target_pairs={{0,16},{16,4},{4,20},{20,0},{8,28},{24,8},{12,24},{28,12},{1,17},{... | collective-permute-start | bytes 393224 | tf_op jit(solution)/shard_map/ppermute | solution.py:156
  256.9 4.6 %collective-permute-start.27 = (f32[2,2,2,2,8,256]{5,4,3,2,1,0:T(8,128)S(1)}, f32[2,2,2,2,8,256]{5,4,3,2,1,0:T(8,128)S(1)}, u32[]{:S(2)}, u32[]{:S(2)}) collective-permute-start(f32[2,2,2,2,8,256]{5,4,3,2,1,0:T(8,128)S(1)} %bitcast_add_fusion.26), channel_id=1, source_target_pairs={{0,16},{16,4},{4,20},{20,0},{8,28},{24,8},{12,24},{28,12},{1,17},{... | collective-permute-start | bytes 393224 | tf_op jit(solution)/shard_map/ppermute | solution.py:156
  260.4 14.8 %collective-permute-start.16 = (f32[4,2,2,3,2,8,256]{6,5,4,3,2,1,0:T(8,128)}, f32[4,2,2,3,2,8,256]{6,5,4,3,2,1,0:T(8,128)}, u32[]{:S(2)}, u32[]{:S(2)}) collective-permute-start(f32[4,2,2,3,2,8,256]{6,5,4,3,2,1,0:T(8,128)} %bitcast_add_fusion.10), channel_id=1, source_target_pairs={{0,32},{32,64},{64,96},{96,0},{8,104},{40,8},{72,40},{104,72},{1,3... | collective-permute-start | bytes 2359304 | tf_op jit(solution)/shard_map/ppermute | solution.py:156
  261.5 15.2 %collective-permute-start.7 = (f32[2,4,2,3,2,8,256]{6,5,4,3,2,1,0:T(8,128)}, f32[2,4,2,3,2,8,256]{6,5,4,3,2,1,0:T(8,128)}, u32[]{:S(2)}, u32[]{:S(2)}) collective-permute-start(f32[2,4,2,3,2,8,256]{6,5,4,3,2,1,0:T(8,128)} %bitcast_add_fusion.13), channel_id=1, source_target_pairs={{0,16},{16,4},{4,20},{20,0},{8,28},{24,8},{12,24},{28,12},{1,17},{... | collective-permute-start | bytes 2359304 | tf_op jit(solution)/shard_map/ppermute | solution.py:156
  261.5 12.8 %collective-permute-start.28 = (f32[2,2,2,2,8,256]{5,4,3,2,1,0:T(8,128)S(1)}, f32[2,2,2,2,8,256]{5,4,3,2,1,0:T(8,128)S(1)}, u32[]{:S(2)}, u32[]{:S(2)}) collective-permute-start(f32[2,2,2,2,8,256]{5,4,3,2,1,0:T(8,128)S(1)} %bitcast_add_fusion.25), channel_id=1, source_target_pairs={{0,16},{16,4},{4,20},{20,0},{8,28},{24,8},{12,24},{28,12},{1,17},{... | collective-permute-start | bytes 393224 | tf_op jit(solution)/shard_map/ppermute | solution.py:156
  276.6 4.6 %collective-permute-start.17 = (f32[2,2,3,2,8,256]{5,4,3,2,1,0:T(8,128)S(1)}, f32[2,2,3,2,8,256]{5,4,3,2,1,0:T(8,128)S(1)}, u32[]{:S(2)}, u32[]{:S(2)}) collective-permute-start(f32[2,2,3,2,8,256]{5,4,3,2,1,0:T(8,128)S(1)} %dynamic-slice_bitcast_fusion.7), channel_id=1, source_target_pairs={{0,1},{1,2},{2,3},{3,0},{8,11},{9,8},{10,9},{11,10},{4,5},{5,6},{6... | collective-permute-start | bytes 589832 | tf_op jit(solution)/shard_map/ppermute | solution.py:156
  278.2 4.6 %collective-permute-start.8 = (f32[2,2,3,2,8,256]{5,4,3,2,1,0:T(8,128)S(1)}, f32[2,2,3,2,8,256]{5,4,3,2,1,0:T(8,128)S(1)}, u32[]{:S(2)}, u32[]{:S(2)}) collective-permute-start(f32[2,2,3,2,8,256]{5,4,3,2,1,0:T(8,128)S(1)} %dynamic-slice_bitcast_fusion.8), channel_id=1, source_target_pairs={{0,32},{32,64},{64,96},{96,0},{8,104},{40,8},{72,40},{104,72},{1,3... | collective-permute-start | bytes 589832 | tf_op jit(solution)/shard_map/ppermute | solution.py:156
  281.2 4.6 %collective-permute-start.18 = (f32[2,2,3,2,8,256]{5,4,3,2,1,0:T(8,128)S(1)}, f32[2,2,3,2,8,256]{5,4,3,2,1,0:T(8,128)S(1)}, u32[]{:S(2)}, u32[]{:S(2)}) collective-permute-start(f32[2,2,3,2,8,256]{5,4,3,2,1,0:T(8,128)S(1)} %bitcast_add_fusion.20), channel_id=1, source_target_pairs={{0,1},{1,2},{2,3},{3,0},{8,11},{9,8},{10,9},{11,10},{4,5},{5,6},{6... | collective-permute-start | bytes 589832 | tf_op jit(solution)/shard_map/ppermute | solution.py:156
  282.9 5.5 %collective-permute-start.9 = (f32[2,2,3,2,8,256]{5,4,3,2,1,0:T(8,128)S(1)}, f32[2,2,3,2,8,256]{5,4,3,2,1,0:T(8,128)S(1)}, u32[]{:S(2)}, u32[]{:S(2)}) collective-permute-start(f32[2,2,3,2,8,256]{5,4,3,2,1,0:T(8,128)S(1)} %bitcast_add_fusion.23), channel_id=1, source_target_pairs={{0,32},{32,64},{64,96},{96,0},{8,104},{40,8},{72,40},{104,72},{1,3... | collective-permute-start | bytes 589832 | tf_op jit(solution)/shard_map/ppermute | solution.py:156
  285.8 5.1 %collective-permute-start.19 = (f32[2,2,3,2,8,256]{5,4,3,2,1,0:T(8,128)S(1)}, f32[2,2,3,2,8,256]{5,4,3,2,1,0:T(8,128)S(1)}, u32[]{:S(2)}, u32[]{:S(2)}) collective-permute-start(f32[2,2,3,2,8,256]{5,4,3,2,1,0:T(8,128)S(1)} %bitcast_add_fusion.19), channel_id=1, source_target_pairs={{0,1},{1,2},{2,3},{3,0},{8,11},{9,8},{10,9},{11,10},{4,5},{5,6},{6... | collective-permute-start | bytes 589832 | tf_op jit(solution)/shard_map/ppermute | solution.py:156
  288.3 4.9 %collective-permute-start.10 = (f32[2,2,3,2,8,256]{5,4,3,2,1,0:T(8,128)S(1)}, f32[2,2,3,2,8,256]{5,4,3,2,1,0:T(8,128)S(1)}, u32[]{:S(2)}, u32[]{:S(2)}) collective-permute-start(f32[2,2,3,2,8,256]{5,4,3,2,1,0:T(8,128)S(1)} %bitcast_add_fusion.22), channel_id=1, source_target_pairs={{0,32},{32,64},{64,96},{96,0},{8,104},{40,8},{72,40},{104,72},{1,3... | collective-permute-start | bytes 589832 | tf_op jit(solution)/shard_map/ppermute | solution.py:156
  293.3 14.0 %collective-permute-start.29 = (f32[2,8,2,8,256]{4,3,2,1,0:T(8,128)S(1)}, f32[2,8,2,8,256]{4,3,2,1,0:T(8,128)S(1)}, u32[]{:S(2)}, u32[]{:S(2)}) collective-permute-start(f32[2,8,2,8,256]{4,3,2,1,0:T(8,128)S(1)} %dynamic-slice_bitcast_fusion.6), channel_id=1, source_target_pairs={{0,8},{8,0},{1,9},{9,1},{2,10},{10,2},{3,11},{11,3},{4,12},{12,4},... | collective-permute-start | bytes 786440 | tf_op jit(solution)/shard_map/ppermute | solution.py:130
  307.4 1.1 copy-start.5
  310.5 2.1 copy-start.4

commit v2 on v0

v2 whole, which is shorter than its diff:
```python
import itertools
import math

import jax
import jax.numpy as jnp
from jax import lax
from jax.experimental import pallas as pl
from jax.experimental.pallas import tpu as pltpu
from jax.sharding import Mesh, PartitionSpec as P

FIRST = 384
BLOCK = 128
BLOCKS = 5
PAIRS = 3
ORDER = {"z": "zxy", "x": "xyz", "y": "yzx"}
EVENTS = (
    *("z0", "x0", "y0", "z1", "x1", "zk"),
    *("y1", "x2", "z2", "y2", "x3", "z3"),
    *("y3", "z4", "x4", "y4", "z5", "x5", "y5"),
)


def block_place(part, t):
    if part == "x":
        return t // 3, t + 3
    return (t + 1) // 3, jnp.where(t < 2, t + 6, t + 1)


def phase_table(points, coords, degen):
    angle = points[0][:, None] * coords[0][None, :] + points[1][:, None] * coords[1][None, :]
    angle = angle + points[2][:, None] * coords[2][None, :]
    angle = 2.0 * jnp.pi * angle
    scale = 1.0 / degen
    return (
        (jnp.cos(angle) * scale[None, :]).astype(jnp.bfloat16),
        (jnp.sin(angle) * scale[None, :]).astype(jnp.bfloat16),
    )


def ring_place(place, core, first, second):
    high = place >> 1
    low = high ^ (place & 1)
    low = low ^ jnp.where(core == 0, first, second)
    high = high ^ jnp.where(core == 0, second, first)
    return 2 * high + (low ^ high)


def widen_kernel(where_ref, own_ref, out_ref):
    out_ref[...] = own_ref[:, 0].astype(jnp.float32)


def spread(table_ref, wide_ref):
    rows = lax.broadcasted_iota(jnp.int32, (256, 32), 0)
    entry = lax.broadcasted_iota(jnp.int32, (256, 32), 1)
    pick = (rows // 8 == entry).astype(jnp.float32).astype(jnp.bfloat16)
    table = jnp.dot(pick, table_ref[...], preferred_element_type=jnp.float32).astype(jnp.bfloat16)
    table = lax.dot_general(table, pick, (((1,), (1,)), ((), ())), preferred_element_type=jnp.float32)
    rows = lax.broadcasted_iota(jnp.int32, (256, 256), 0)
    entry = lax.broadcasted_iota(jnp.int32, (256, 256), 1)
    table = jnp.where(rows % 8 == entry % 8, table, 0.0).astype(jnp.bfloat16)
    wide_ref[...] = table.reshape(8, 32, 256)


def partial_kernel(order, where_ref, wq_ref, wk_ref, even_ref, odd_ref, got_ref, *refs):
    *out_refs, mixed_ref, rows_ref, wide_ref = refs
    core, y, z, xh, xl = (where_ref[n] for n in range(5))
    lanes = got_ref.shape[-1]

    @pl.when(pl.program_id(0) == 0)
    def _():
        spread(wk_ref, wide_ref)
        for h, zf, zs in itertools.product(range(2), repeat=3):
            zat = ring_place(z, core, zf, zs)
            spot = 32 * (4 * h + 2 * zf + zs)
            rows_ref[0, spot : spot + 32] = wide_ref[(xh ^ h) * 4 + zat]
            rows_ref[1, spot : spot + 32] = wide_ref[(xh ^ h ^ core) * 4 + zat]

    for r in range(16):
        even = even_ref[r, 0].reshape(128, BLOCK)
        odd = odd_ref[r, 0].reshape(128, BLOCK)
        own = jnp.concatenate([even, odd], axis=1)
        got = got_ref[r].reshape(128, lanes).astype(jnp.bfloat16)
        rows = jnp.concatenate([own, got], axis=0)
        mixed = jnp.dot(wq_ref[...], rows, preferred_element_type=jnp.float32)
        mixed_ref[r] = mixed.reshape(2, 16, 8, lanes)
    for yf, ys, cross, other in itertools.product(range(2), repeat=4):
        g = ring_place(y, core, yf, ys) * 4 + (xl ^ cross) * 2 + (core ^ other)
        rows = mixed_ref[:, :, g].reshape(256, lanes).astype(jnp.bfloat16)
        summed = jnp.dot(rows_ref[cross], rows, preferred_element_type=jnp.float32)
        summed = summed.reshape(2, 2, 2, 2, 2, 8, lanes)
        for h, zf, zs in itertools.product(range(2), repeat=3):
            bits = {"y": (yf, ys), "z": (zf, zs), "x": (h ^ cross, h)}
            spot = sum((bits[axis] for axis in order), ())
            out_refs[spot[0]][(*spot[1:], other)] = summed[h, zf, zs]


def electron_kernel(where_ref, wk_ref, own_ref, *refs):
    *out_refs, rows_ref, wide_ref = refs
    core, z, xh = (where_ref[n] for n in (0, 2, 3))
    lanes = own_ref.shape[-1]

    @pl.when(pl.program_id(0) == 0)
    def _():
        spread(wk_ref, wide_ref)
        for zf, zs, h in itertools.product(range(2), repeat=3):
            spot = 32 * (4 * zf + 2 * zs + h)
            rows_ref[spot : spot + 32] = wide_ref[(xh ^ h) * 4 + ring_place(z, core, zf, zs)]

    for pair in range(4):
        wide = own_ref[:, 0, :, 16 * pair : 16 * pair + 16].astype(jnp.float32)
        for half in range(2):
            rows = wide[:, :, 8 * half : 8 * half + 8].reshape(256, lanes).astype(jnp.bfloat16)
            summed = jnp.dot(rows_ref[...], rows, preferred_element_type=jnp.float32)
            summed = summed.reshape(2, 2, 2, 2, 2, 8, lanes)
            for n in range(2):
                out_refs[n][:, 0, :, :, 2 * pair + half, 0] = summed[n]


def phonon_kernel(where_ref, wq_ref, own_ref, got_ref, keep_ref, send_ref, summed_ref):
    core, y, xl = (where_ref[n] for n in (0, 1, 4))
    lanes = own_ref.shape[-1]
    for h, i in itertools.product(range(2), repeat=2):
        rows = [jnp.swapaxes(ref[h, i, :, 0], 0, 1).reshape(128, lanes) for ref in (own_ref, got_ref)]
        rows = jnp.concatenate(rows, axis=0).astype(jnp.bfloat16)
        summed = jnp.dot(wq_ref[...], rows, preferred_element_type=jnp.float32)
        summed_ref[h, i] = summed.reshape(2, 16, 8, lanes)
    for xf, xs in itertools.product(range(2), repeat=2):
        h = jnp.where(core == 0, xs, xf)
        for yf, ys, other in itertools.product(range(2), repeat=3):
            g = ring_place(y, core, yf, ys) * 4 + (xl ^ xf ^ xs) * 2 + (core ^ other)
            for i in range(2):
                (keep_ref, send_ref)[xf][xs, yf, ys, other, i, 0] = summed_ref[h, i, :, g]


def kernel_call(kernel, where, inputs, in_specs, count, out, block, place, grid, scratch):
    read = sum(v.size * v.dtype.itemsize for v in inputs)
    return pl.pallas_call(
        kernel,
        grid_spec=pltpu.PrefetchScalarGridSpec(
            num_scalar_prefetch=1,
            grid=(grid,),
            in_specs=in_specs,
            out_specs=[pl.BlockSpec(block, place)] * count,
            scratch_shapes=scratch,
        ),
        out_shape=[jax.ShapeDtypeStruct(out, jnp.float32)] * count,
        compiler_params=pltpu.CompilerParams(vmem_limit_bytes=48 * 1024 * 1024),
        cost_estimate=pl.CostEstimate(
            flops=2**31, bytes_accessed=read + 4 * count * math.prod(out), transcendentals=0
        ),
    )(where, *inputs)


def electron_sums(where, wk, own):
    return kernel_call(
        electron_kernel,
        where,
        (wk, own),
        [
            pl.BlockSpec((32, 32), lambda m, w: (0, 0)),
            pl.BlockSpec((16, 1, 2, 64, FIRST), lambda m, w: (0, (2 * w[0] + m) % 4, 0, 0, 0)),
        ],
        2,
        (2, 2, 2, 2, 8, 2, 2, 8, FIRST),
        (2, 1, 2, 2, 8, 1, 2, 8, FIRST),
        lambda m, w: (0, m // 2, 0, 0, 0, m % 2, 0, 0, 0),
        4,
        [pltpu.VMEM((256, 256), jnp.bfloat16), pltpu.VMEM((8, 32, 256), jnp.bfloat16)],
    )


def phonon_sums(where, wq, own, got):
    spec = pl.BlockSpec((2, 2, 8, 1, 2, 8, FIRST), lambda u, w: (0, 0, 0, u, 0, 0, 0))
    return kernel_call(
        phonon_kernel,
        where,
        (wq, own, got),
        [pl.BlockSpec((256, 256), lambda u, w: (0, 0)), spec, spec],
        2,
        (2, 2, 2, 2, 2, 2, 2, 8, FIRST),
        (2, 2, 2, 2, 2, 1, 2, 8, FIRST),
        lambda u, w: (0, 0, 0, 0, 0, u, 0, 0, 0),
        2,
        [pltpu.VMEM((2, 2, 2, 16, 8, FIRST), jnp.float32)],
    )


def own_spec(part, flip, block_of):
    def place(t, w):
        mode, block = block_place(part, block_of(t))
        return (0, 2 * (w[0] ^ flip) + mode, 0, 0, block)

    return pl.BlockSpec((16, 1, 2, 64, BLOCK), place)


def widened(part, where, own):
    return kernel_call(
        widen_kernel,
        where,
        (own,),
        [own_spec(part, 1, lambda t: t)],
        1,
        (16, 2, 64, BLOCKS * BLOCK),
        (16, 2, 64, BLOCK),
        lambda t, w: (0, 0, 0, t),
        BLOCKS,
        [],
    )[0]


def partial_sums(part, where, wq, wk, own, got):
    return kernel_call(
        lambda *refs: partial_kernel(ORDER[part], *refs),
        where,
        (wq, wk, own, own, got),
        [
            pl.BlockSpec((256, 256), lambda t, w: (0, 0)),
            pl.BlockSpec((32, 32), lambda t, w: (0, 0)),
            own_spec(part, 0, lambda t: 2 * t),
            own_spec(part, 0, lambda t: jnp.minimum(2 * t + 1, BLOCKS - 1)),
            pl.BlockSpec((16, 2, 64, 2 * BLOCK), lambda t, w: (0, 0, 0, t)),
        ],
        2,
        (2, 2, 2, 2, 2, 2, 2, 2, 8, BLOCKS * BLOCK),
        (2, 2, 2, 2, 2, 2, 2, 2, 8, 2 * BLOCK),
        lambda t, w: (0, 0, 0, 0, 0, 0, 0, 0, 0, t),
        PAIRS,
        [
            pltpu.VMEM((16, 2, 16, 8, 2 * BLOCK), jnp.float32),
            pltpu.VMEM((2, 256, 256), jnp.bfloat16),
            pltpu.VMEM((8, 32, 256), jnp.bfloat16),
        ],
    )


def exchange(value, axis, step):
    pairs = []
    for core in range(2):
        for at in range(4):
            to = at ^ 1 if core == step else 3 - at
            if axis == "z":
                pairs.append((core * 4 + at, core * 4 + to))
            elif axis == "y":
                pairs.append((at * 2 + core, to * 2 + core))
            else:
                pairs.append(((at % 2) * 4 + core * 2 + at // 2, (to % 2) * 4 + core * 2 + to // 2))
    names = {"z": ("c", "z"), "y": ("y", "c"), "x": ("xl", "c", "xh")}[axis]
    return lax.ppermute(value, names, pairs)


def swap(value):
    return lax.ppermute(value, "c", [(0, 1), (1, 0)])


def rotation_tables(rot_right, rot_left):
    r_real, r_imag = (rot_right[:, 0], rot_right[:, 1])
    l_real, l_imag = (rot_left[:, :, 0], rot_left[:, :, 1])
    right = jnp.stack([jnp.stack([r_real, r_imag], 2), jnp.stack([-r_imag, r_real], 2)], 1)
    left = jnp.stack([jnp.stack([l_real, -l_imag], 3), jnp.stack([l_imag, l_real], 3)], 2)
    right = right.transpose(0, 1, 3, 2, 4)[:, :, :, None, :, None, :]
    right = right * jnp.eye(8, dtype=jnp.float32)[:, None, :, None]
    left = left.transpose(0, 1, 4, 5, 2, 3)
    return right.reshape(2, 2, 2, 256, 256), left.reshape(2, 8, 64, 64)


def split(value):
    high = value.astype(jnp.bfloat16)
    return high, (value - high.astype(jnp.float32)).astype(jnp.bfloat16)


def dot(left, right):
    return jnp.dot(left, right, preferred_element_type=jnp.float32)


def regroup(parts):
    group = lax.broadcasted_iota(jnp.int32, (8, 128), 1) // 32
    out = []
    for n in range(4):
        total = parts[n]
        for m in range(4):
            if m != n:
                total = jnp.where(group == m, pltpu.roll(parts[m], 32 * (m - n) % 128, 1), total)
        out.append(total)
    return out


def rotation_kernel(sum_ref, right_ref, left_ref, out_ref, turned_ref, done_ref):
    turned = [0.0, 0.0]
    for p in range(2):
        rows = sum_ref[0, p].reshape(32, 1024)
        rows = jnp.concatenate([rows[:, 256 * t : 256 * t + 256] for t in range(4)], axis=0)
        high, low = split(rows)
        both = jnp.concatenate([high, low], axis=0)
        for s in range(2):
            right_high, right_low = split(right_ref[0, p, s])
            product = dot(both, right_high)
            turned[s] = turned[s] + product[:128] + product[128:] + dot(high, right_low)
    for s in range(2):
        blocks = turned[s].reshape(4, 4, 8, 256)
        for t in range(8):
            parts = [blocks[t // 2, m, :, 128 * (t % 2) : 128 * (t % 2) + 128] for m in range(4)]
            for n, part in enumerate(regroup(parts)):
                spot = 8 * (32 * s + 4 * t + n)
                turned_ref[spot : spot + 8] = part
    for j in range(8):
        high, low = split(turned_ref[pl.ds(j, 64, stride=8), :])
        left_high, left_low = split(left_ref[0, j])
        product = dot(jnp.concatenate([left_high, left_low], axis=0), high)
        done_ref[pl.ds(j, 64, stride=8), :] = product[:64] + product[64:] + dot(left_high, low)
    for s in range(2):
        for t in range(8):
            spot = 8 * (32 * s + 4 * t)
            parts = [done_ref[spot + 8 * n : spot + 8 * n + 8] for n in range(4)]
            for m, part in enumerate(regroup(parts)):
                out_ref[0, :, m, s, 128 * t : 128 * t + 128] = part


def rotate(summed, right, left):
    return pl.pallas_call(
        rotation_kernel,
        grid=(2,),
        in_specs=[
            pl.BlockSpec((1, 2, 4, 8, 1024), lambda k: (k, 0, 0, 0, 0)),
            pl.BlockSpec((1, 2, 2, 256, 256), lambda k: (k, 0, 0, 0, 0)),
            pl.BlockSpec((1, 8, 64, 64), lambda k: (k, 0, 0, 0)),
        ],
        out_specs=pl.BlockSpec((1, 8, 4, 2, 1024), lambda k: (k, 0, 0, 0, 0)),
        out_shape=jax.ShapeDtypeStruct((2, 8, 4, 2, 1024), jnp.float32),
        scratch_shapes=[pltpu.VMEM((512, 128), jnp.float32)] * 2,
        compiler_params=pltpu.CompilerParams(vmem_limit_bytes=48 * 1024 * 1024),
        cost_estimate=pl.CostEstimate(flops=2**28, bytes_accessed=2**22, transcendentals=0),
    )(summed, right, left)


def complex_table(cos_part, sin_part):
    top = jnp.concatenate([cos_part, -sin_part], axis=1)
    bottom = jnp.concatenate([sin_part, cos_part], axis=1)
    return jnp.concatenate([top, bottom], axis=0)


def body(
    wannier_g, el_vectors, ph_vectors, el_degen, ph_degen, k_points, q_points, rot_right, rot_left
):
    core = lax.axis_index("c")
    where = jnp.stack([core, *(lax.axis_index(a) for a in ("y", "z", "xh", "xl"))]).astype(jnp.int32)

    vectors = jnp.concatenate([ph_vectors, ph_degen[None]], axis=0).astype(jnp.float32)
    others = swap(vectors)
    k_cos, k_sin = phase_table(k_points, el_vectors.astype(jnp.float32), el_degen.astype(jnp.float32))
    wide = jnp.stack([jnp.stack([k_cos, -k_sin], 2), jnp.stack([k_sin, k_cos], 2)], 1)
    wk = wide.reshape(32, 32)
    tables = [complex_table(*phase_table(q_points, v[:3], v[3])) for v in (vectors, others)]
    wq = jnp.concatenate(tables, axis=1)

    own = lax.optimization_barrier(wannier_g.transpose(0, 2, 3, 1, 4))

    def after(earlier, *values):
        return lax.optimization_barrier((*values, earlier))[:-1]

    keep, send, arrived = {}, {}, {}

    def begin(part, sums):
        keep[part], send[part] = sums
        arrived[part] = exchange(send[part], part, 0)

    (own,) = after(others, own)
    got_x = widened("x", where, own)
    (wk,) = after(got_x, wk)
    got_x = swap(got_x)
    begin("z", electron_sums(where, wk, own))
    (later,) = after(keep["z"], own)
    got_y = widened("y", where, later)
    wq, got_x = after(got_y, wq, got_x)
    got_y = swap(got_y)
    begin("x", partial_sums("x", where, wq, wk, own, got_x))
    wq, got_y = after(keep["x"], wq, got_y)
    begin("y", partial_sums("y", where, wq, wk, own, got_y))
    rot_right, rot_left = after(keep["y"], rot_right, rot_left)
    right, left = rotation_tables(rot_right, rot_left)
    latest = (right, left, keep["y"])
    for event in EVENTS:
        part, step = event
        axes = ORDER[part]
        (arrived[part],) = after(latest, arrived[part])
        if step == "0":
            latest = send[part] = keep[part][1] + arrived[part][1]
            held, came = after(latest, keep[part], arrived[part])
            arrived[part] = exchange(send[part], axes[0], 1)
            keep[part] = held[0] + came[0]
        elif step == "k":
            keep[part], send[part] = phonon_sums(where, wq, keep[part], arrived[part])
            arrived[part] = exchange(send[part], axes[1], 0)
            latest = keep[part]
        elif step == "5":
            latest = keep[part] = keep[part] + arrived[part]
        else:
            latest = send[part] = keep[part][1] + arrived[part][1]
            keep[part] = keep[part][0] + arrived[part][0]
            if event == "z1":
                arrived[part] = swap(send[part])
            else:
                arrived[part] = exchange(send[part], axes[(int(step) + 1) // 2], (int(step) + 1) % 2)

    modes = []
    for ours in (True, False):
        z, x, y = (keep[part][0] if ours else swap(keep[part][1]) for part in "zxy")
        wide, narrow = 3 * BLOCK, 2 * BLOCK
        modes.append(jnp.concatenate([z[:, 0], x[..., :wide], y[..., :narrow]], axis=-1))
        modes.append(jnp.concatenate([z[:, 1], y[..., narrow:], x[..., wide:]], axis=-1))
    mine, theirs = jnp.stack(modes[:2], axis=2), jnp.stack(modes[2:], axis=2)
    modes = jnp.concatenate([jnp.where(core == 0, mine, theirs), jnp.where(core == 0, theirs, mine)], axis=2)
    return rotate(modes, right, left)


def solution(mesh):
    fine = Mesh(mesh.devices.reshape(4, 2, 2, 2, 4), ("y", "xl", "c", "xh", "z"))
    ph, el = ("y", "xl", "c"), ("xh", "z")
    in_specs = (
        P(el, ph, None, None, None),
        P(None, el),
        P(None, ph),
        P(el),
        P(ph),
        P(),
        P(),
        P(el, None, None, None),
        P(el, ph, None, None, None),
    )
    out_specs = P(el, ph, None, None, None)
    return jax.shard_map(body, mesh=fine, in_specs=in_specs, out_specs=out_specs, check_vma=False)
```

time: 994 us -> 233 us (0.23)
  waiting for transfers between devices: 773 us -> 76 us
  matrix products: 82.6 us -> 0 us
  other arithmetic: 111 us -> 34.8 us
  Pallas kernels: 0 us -> 46.8 us
  starting transfers between devices: 0.22 us -> 35.1 us
  local copies, waits for them, and re-layouts: 12.3 us -> 39.1 us
  between operations: 13.6 us -> 0.57 us
    reduce_scatter x2 -> x0, waiting for transfers between devices: 773 us -> none  [the longest x1 689 us: body(): lax.psum_scatter(apply_phase('qp,rpmcx->qrmcx', q_cos, q_sin, wannier_g,...]
    dot_general x12 -> x0, matrix products: 82.6 us -> none  [the longest x1 29 us: apply_phase(): jnp.einsum(form, cos_table, data, preferred_element_type=jnp.float32)]
    ppermute x0 -> x25, waiting for transfers between devices: none -> 76 us  [the longest x18 75.2 us: exchange(): return lax.ppermute(value, names, pairs)]
    sub x2 -> x0, other arithmetic: 66 us -> none  [combine(): real_part = cos_part[..., 0, :] - sin_part[..., 1, :]]
    pallas_call x0 -> x7, Pallas kernels: none -> 46.8 us  [the longest x6 43.7 us: kernel_call(): pl.pallas_call(kernel, grid_spec=pltpu.PrefetchScalarGridSpec(num_scalar_...]
    another operation x3 -> x8, other arithmetic: 43.9 us -> 0.21 us  [the longest x1 0.13 us: rotation_tables(): jnp.stack([jnp.stack([l_real, -l_imag], 3), jnp.stack([l_imag, l_real], 3...]
    ppermute x0 -> x25, starting transfers between devices: none -> 35.1 us  [the longest x18 25.1 us: exchange(): return lax.ppermute(value, names, pairs)]
    add x0 -> x21, other arithmetic: none -> 28.8 us  [the longest x10 15.8 us: body(): latest = send[part] = keep[part][1] + arrived[part][1]]
  transfers between devices with their start and end apart: 2 -> 25, of which waited for: 2 -> 14; matrix products, arithmetic and copies ran while one was open for 0% -> 29% of each run, Pallas kernels for 0% -> 16%
where the time goes in v2:
time: 233 us; the launch traced here: 232 us
  waiting for transfers between devices  76 us (33%)
  Pallas kernels  46.8 us (20%)
  local copies, waits for them, and re-layouts  39.1 us (17%)
  starting transfers between devices  35.1 us (15%)
  other arithmetic  34.8 us (15%)
    ppermute x18, waiting for transfers between devices, exchange(): return lax.ppermute(value, names, pairs)  75.2 us
    pallas_call x6, Pallas kernels, kernel_call(): pl.pallas_call(kernel, grid_spec=pltpu.PrefetchScalarGridSpec(num_scalar_...  43.7 us
    ppermute x18, starting transfers between devices, exchange(): return lax.ppermute(value, names, pairs)  25.1 us
    unnamed x31, local copies, waits for them, and re-layouts  24.4 us
    add x10, other arithmetic, body(): latest = send[part] = keep[part][1] + arrived[part][1]  15.8 us
    mul x4, local copies, waits for them, and re-layouts, rotation_tables(): right = right * jnp.eye(8, dtype=jnp.float32)[:, None, :, None]  11.9 us
    ppermute x7, starting transfers between devices, swap(): return lax.ppermute(value, 'c', [(0, 1), (1, 0)])  9.95 us
    add x3, other arithmetic, body(): keep[part] = held[0] + came[0]  6.75 us
  transfers between devices with their start and end apart: 25, of which 14 were waited for; matrix products, arithmetic and copies ran while one was open for 29% of the time, Pallas kernels for 16%

profile of v2, /device:TPU:1, one launch (start us, length us, event | category | flops | bytes accessed | tf_op | source)
XLA Modules:
  0.0 232.3 jit_solution(7611486936787816347)
XLA Ops:
  0.0 0.7 add_convert_fusion
  0.7 1.5 collective-permute-start
  2.2 0.7 convert_divide_fusion
  2.8 0.7 convert_element_type.57
  3.5 0.8 slice_bitcast_fusion.40
  4.5 18.6 %copy.67 = bf16[16,64,4,2,1024]{4,1,3,2,0:T(8,128)(2,1)} copy(bf16[16,64,4,2,1024]{4,3,2,1,0:T(2,128)(2,1)} %param.9) | data formatting | bytes 33554432 | tf_op args[0]
  23.2 6.0 %shard_map.91 = f32[16,2,64,640]{3,2,1,0:T(8,128)} custom-call(s32[5]{0:T(128)S(1)} %stack.92.where_ref.refs_0_, bf16[16,4,2,64,1024]{4,3,2,1,0:T(8,128)(2,1)} %bitcast.283), custom_call_target="tpu_custom_call" | custom-call | flops 2147483648 | bytes 22020096 | tf_op jit(solution)/shard_map/pallas_call | solution.py:137
  29.8 9.8 %shard_map.92 = (f32[2,2,2,2,8,2,2,8,384]{8,7,6,5,4,3,2,1,0:T(8,128)}, f32[2,2,2,2,8,2,2,8,384]{8,7,6,5,4,3,2,1,0:T(8,128)}) custom-call(s32[5]{0:T(128)S(1)} %stack.92.where_ref.refs_0_, bf16[32,32]{1,0:T(8,128)(2,1)S(1)} %reshape.653.wk_ref.refs_2_, bf16[16,4,2,64,1024]{4,3,2,1,0:T(8,128)(2,1)} %bitcast.284), custom_call_target="tpu_custom_call" | custom-call | flops 2147483648 | bytes 29362176 | tf_op jit(solution)/shard_map/pallas_call | solution.py:137
  39.6 6.0 %shard_map.93 = f32[16,2,64,640]{3,2,1,0:T(8,128)} custom-call(s32[5]{0:T(128)S(1)} %stack.92.where_ref.refs_0_, bf16[16,4,2,64,1024]{4,3,2,1,0:T(8,128)(2,1)} %bitcast.285), custom_call_target="tpu_custom_call" | custom-call | flops 2147483648 | bytes 22020096 | tf_op jit(solution)/shard_map/pallas_call | solution.py:137
  45.6 0.5 collective-permute-start.2
  46.1 3.8 %collective-permute-start.3 = (f32[2,2,2,2,8,2,2,8,384]{8,7,6,5,4,3,2,1,0:T(8,128)}, f32[2,2,2,2,8,2,2,8,384]{8,7,6,5,4,3,2,1,0:T(8,128)}, u32[]{:S(2)}, u32[]{:S(2)}) collective-permute-start(f32[2,2,2,2,8,2,2,8,384]{8,7,6,5,4,3,2,1,0:T(8,128)} %get-tuple-element.55), channel_id=1, source_target_pairs={{0,1},{1,0},{2,3},{3,2},{8,11},{9,10},{10,9},{11,8},{4,5},{5,4},{6... | collective-permute-start | bytes 18874376 | tf_op jit(solution)/shard_map/ppermute | solution.py:248
  50.0 0.6 fusion.47
  50.5 0.6 multiply_convert_fusion.2
  51.3 9.4 %shard_map.94 = (f32[2,2,2,2,2,2,2,2,8,640]{9,8,7,6,5,4,3,2,1,0:T(8,128)S(1)}, f32[2,2,2,2,2,2,2,2,8,640]{9,8,7,6,5,4,3,2,1,0:T(8,128)}) custom-call(s32[5]{0:T(128)S(1)} %stack.92.where_ref.refs_0_, bf16[256,256]{1,0:T(8,128)(2,1)S(1)} %maximum_maximum_fusion.refs_1_.wq_ref, bf16[32,32]{1,0:T(8,128)(2,1)S(1)} %reshape.653.wk_ref.refs_2_, ...), custom_call_target="tpu_custom_call" | custom-call | flops 2147483648 | bytes 49416192 | tf_op jit(solution)/shard_map/pallas_call | solution.py:137
  60.7 2.3 copy-done.1
  63.0 2.5 %collective-permute-start.6 = (f32[2,2,2,2,2,2,2,2,8,640]{9,8,7,6,5,4,3,2,1,0:T(8,128)}, f32[2,2,2,2,2,2,2,2,8,640]{9,8,7,6,5,4,3,2,1,0:T(8,128)}, u32[]{:S(2)}, u32[]{:S(2)}) collective-permute-start(f32[2,2,2,2,2,2,2,2,8,640]{9,8,7,6,5,4,3,2,1,0:T(8,128)} %get-tuple-element.64), channel_id=1, source_target_pairs={{0,16},{16,0},{4,20},{20,4},{8,28},{24,12},{12,24},{28,8},{1,17},{... | collective-permute-start | bytes 15728648 | tf_op jit(solution)/shard_map/ppermute | solution.py:248
  65.9 9.4 %shard_map.95 = (f32[2,2,2,2,2,2,2,2,8,640]{9,8,7,6,5,4,3,2,1,0:T(8,128)S(1)}, f32[2,2,2,2,2,2,2,2,8,640]{9,8,7,6,5,4,3,2,1,0:T(8,128)}) custom-call(s32[5]{0:T(128)S(1)} %stack.92.where_ref.refs_0_, bf16[256,256]{1,0:T(8,128)(2,1)S(1)} %maximum_maximum_fusion.refs_1_.wq_ref, bf16[32,32]{1,0:T(8,128)(2,1)S(1)} %reshape.653.wk_ref.refs_2_, ...), custom_call_target="tpu_custom_call" | custom-call | flops 2147483648 | bytes 49416192 | tf_op jit(solution)/shard_map/pallas_call | solution.py:137
  75.4 2.3 copy-done
  77.6 2.7 %collective-permute-start.5 = (f32[2,2,2,2,2,2,2,2,8,640]{9,8,7,6,5,4,3,2,1,0:T(8,128)}, f32[2,2,2,2,2,2,2,2,8,640]{9,8,7,6,5,4,3,2,1,0:T(8,128)}, u32[]{:S(2)}, u32[]{:S(2)}) collective-permute-start(f32[2,2,2,2,2,2,2,2,8,640]{9,8,7,6,5,4,3,2,1,0:T(8,128)} %get-tuple-element.63), channel_id=1, source_target_pairs={{0,32},{32,0},{64,96},{96,64},{8,104},{40,72},{72,40},{104,8},{1,3... | collective-permute-start | bytes 15728648 | tf_op jit(solution)/shard_map/ppermute | solution.py:248
  80.4 4.4 %mul.351 = f32[2,2,2,8,32,8,32]{6,5,4,3,2,1,0:T(8,128)} broadcast(f32[2,2,2,32,32]{4,3,2,1,0:T(8,128)S(1)} %copy.51), dimensions={0,1,2,4,6} | broadcast | bytes 2129920 | tf_op jit(solution)/shard_map/mul | solution.py:261
  84.8 7.1 %mul.352 = f32[2,2,2,256,256]{4,3,2,1,0:T(8,128)} reshape(f32[2,2,2,8,32,8,32]{6,5,4,3,2,1,0:T(8,128)} %mul.351) | data formatting | bytes 4194304 | tf_op jit(solution)/shard_map/mul | solution.py:261
  92.2 0.6 copy.53
  92.9 0.6 reshape.654.left_ref
  93.5 1.9 broadcast_multiply_fusion.right_ref
  95.4 23.2 %collective-permute-done.3 = f32[2,2,2,2,8,2,2,8,384]{8,7,6,5,4,3,2,1,0:T(8,128)} collective-permute-done((f32[2,2,2,2,8,2,2,8,384]{8,7,6,5,4,3,2,1,0:T(8,128)}, f32[2,2,2,2,8,2,2,8,384]{8,7,6,5,4,3,2,1,0:T(8,128)}, u32[]{:S(2)}, u32[]{:S(2)}) %collective-permute-start.3) | collective-permute-done | bytes 6291488 | tf_op jit(solution)/shard_map/ppermute | solution.py:248
  118.6 3.5 %add_bitcast_fusion = f32[2,2,2,8,2,2,8,384]{7,6,5,4,3,2,1,0:T(8,128)S(1)} fusion(f32[2,2,2,2,8,2,2,8,384]{8,7,6,5,4,3,2,1,0:T(8,128)} %collective-permute-done.3, f32[2,2,2,2,8,2,2,8,384]{8,7,6,5,4,3,2,1,0:T(8,128)} %get-tuple-element.61), kind=kLoop, calls=%fused_computation.2 | loop fusion | flops 786432 | bytes 9437184 | tf_op jit(solution)/shard_map/add | solution.py:386
  122.2 0.9 collective-permute-done.6
  123.1 2.3 add_bitcast_fusion.2
  125.8 2.5 %slice_add_fusion = f32[1,2,2,2,8,2,2,8,384]{8,7,6,5,4,3,2,1,0:T(8,128)S(1)} fusion(f32[2,2,2,2,8,2,2,8,384]{8,7,6,5,4,3,2,1,0:T(8,128)} %collective-permute-done.3, f32[2,2,2,2,8,2,2,8,384]{8,7,6,5,4,3,2,1,0:T(8,128)S(1)} %bitcast.291), kind=kLoop, calls=%fused_computation.1 | loop fusion | flops 786432 | bytes 9437184 | tf_op jit(solution)/shard_map/add | solution.py:389
  128.4 9.6 %collective-permute-done.5 = f32[2,2,2,2,2,2,2,2,8,640]{9,8,7,6,5,4,3,2,1,0:T(8,128)} collective-permute-done((f32[2,2,2,2,2,2,2,2,8,640]{9,8,7,6,5,4,3,2,1,0:T(8,128)}, f32[2,2,2,2,2,2,2,2,8,640]{9,8,7,6,5,4,3,2,1,0:T(8,128)}, u32[]{:S(2)}, u32[]{:S(2)}) %collective-permute-start.5) | collective-permute-done | bytes 5242912 | tf_op jit(solution)/shard_map/ppermute | solution.py:248
  138.0 3.6 %add_bitcast_fusion.1 = f32[2,2,2,2,2,2,2,8,640]{8,7,6,5,4,3,2,1,0:T(8,128)} fusion(f32[2,2,2,2,2,2,2,2,8,640]{9,8,7,6,5,4,3,2,1,0:T(8,128)} %collective-permute-done.5, f32[2,2,2,2,2,2,2,2,8,640]{9,8,7,6,5,4,3,2,1,0:T(8,128)S(1)} %bitcast.280), kind=kLoop, calls=%fused_computation.5 | loop fusion | flops 655360 | bytes 7864320 | tf_op jit(solution)/shard_map/add | solution.py:386
  141.7 17.0 %collective-permute-done.4 = f32[2,2,2,8,2,2,8,384]{7,6,5,4,3,2,1,0:T(8,128)S(1)} collective-permute-done((f32[2,2,2,8,2,2,8,384]{7,6,5,4,3,2,1,0:T(8,128)S(1)}, f32[2,2,2,8,2,2,8,384]{7,6,5,4,3,2,1,0:T(8,128)S(1)}, u32[]{:S(2)}, u32[]{:S(2)}) %collective-permute-start.4) | collective-permute-done | bytes 3145760 | tf_op jit(solution)/shard_map/ppermute | solution.py:248
  158.7 0.6 fusion.3
  159.3 1.7 collective-permute-start.7
  161.0 2.1 slice_add_fusion.2
  163.1 1.9 fusion.9
  165.0 2.7 %collective-permute-start.10 = (f32[2,2,2,2,2,2,8,640]{7,6,5,4,3,2,1,0:T(8,128)}, f32[2,2,2,2,2,2,8,640]{7,6,5,4,3,2,1,0:T(8,128)}, u32[]{:S(2)}, u32[]{:S(2)}) collective-permute-start(f32[2,2,2,2,2,2,8,640]{7,6,5,4,3,2,1,0:T(8,128)} %get-tuple-element.93), channel_id=1, source_target_pairs={{0,32},{32,0},{64,96},{96,64},{8,104},{40,72},{72,40},{104,8},{1,3... | collective-permute-start | bytes 3932168 | tf_op jit(solution)/shard_map/ppermute | solution.py:248
  167.8 1.2 copy-done.8
  168.9 3.1 %shard_map.96 = (f32[2,2,2,2,2,2,2,8,384]{8,7,6,5,4,3,2,1,0:T(8,128)S(1)}, f32[2,2,2,2,2,2,2,8,384]{8,7,6,5,4,3,2,1,0:T(8,128)S(1)}) custom-call(s32[5]{0:T(128)S(1)} %stack.92.where_ref.refs_0_, bf16[256,256]{1,0:T(8,128)(2,1)S(1)} %maximum_maximum_fusion.refs_1_.wq_ref, f32[2,2,8,2,2,8,384]{6,5,4,3,2,1,0:T(8,128)S(1)} %get-tuple-element.89.own_ref, ...), custom_call_target="tpu_custom_call" | custom-call | flops 2147483648 | bytes 6422528 | tf_op jit(solution)/shard_map/pallas_call | solution.py:137
  172.2 2.6 %collective-permute-start.9 = (f32[2,2,2,2,2,2,2,8,384]{8,7,6,4,5,3,2,1,0:T(8,128)S(1)}, f32[2,2,2,2,2,2,2,8,384]{8,7,6,4,5,3,2,1,0:T(8,128)S(1)}, u32[]{:S(2)}, u32[]{:S(2)}) collective-permute-start(f32[2,2,2,2,2,2,2,8,384]{8,7,6,4,5,3,2,1,0:T(8,128)S(1)} %copy.55), channel_id=1, source_target_pairs={{0,16},{16,0},{4,20},{20,4},{8,28},{24,12},{12,24},{28,8},{1,17},{... | collective-permute-start | bytes 4718600 | tf_op jit(solution)/shard_map/ppermute | solution.py:248
  174.7 2.1 slice_add_fusion.1
  176.9 2.2 fusion.4
  179.1 3.0 %collective-permute-start.14 = (f32[2,2,2,2,2,2,8,640]{7,6,5,4,3,2,1,0:T(8,128)S(1)}, f32[2,2,2,2,2,2,8,640]{7,6,5,4,3,2,1,0:T(8,128)S(1)}, u32[]{:S(2)}, u32[]{:S(2)}) collective-permute-start(f32[2,2,2,2,2,2,8,640]{7,6,5,4,3,2,1,0:T(8,128)S(1)} %get-tuple-element.92), channel_id=1, source_target_pairs={{0,1},{1,0},{2,3},{3,2},{8,11},{9,10},{10,9},{11,8},{4,5},{5,4},{6... | collective-permute-start | bytes 3932168 | tf_op jit(solution)/shard_map/ppermute | solution.py:248
  182.1 3.0 %collective-permute-done.10 = f32[2,2,2,2,2,2,8,640]{7,6,5,4,3,2,1,0:T(8,128)} collective-permute-done((f32[2,2,2,2,2,2,8,640]{7,6,5,4,3,2,1,0:T(8,128)}, f32[2,2,2,2,2,2,8,640]{7,6,5,4,3,2,1,0:T(8,128)}, u32[]{:S(2)}, u32[]{:S(2)}) %collective-permute-start.10) | collective-permute-done | bytes 1310752 | tf_op jit(solution)/shard_map/ppermute | solution.py:248
  185.1 1.4 fusion.16
  186.6 0.5 collective-permute-start.13
  187.0 5.7 %collective-permute-done.9 = f32[2,2,2,2,2,2,2,8,384]{8,7,6,4,5,3,2,1,0:T(8,128)S(1)} collective-permute-done((f32[2,2,2,2,2,2,2,8,384]{8,7,6,4,5,3,2,1,0:T(8,128)S(1)}, f32[2,2,2,2,2,2,2,8,384]{8,7,6,4,5,3,2,1,0:T(8,128)S(1)}, u32[]{:S(2)}, u32[]{:S(2)}) %collective-permute-start.9) | collective-permute-done | bytes 1572896 | tf_op jit(solution)/shard_map/ppermute | solution.py:248
  193.4 4.0 %collective-permute-done.14 = f32[2,2,2,2,2,2,8,640]{7,6,5,4,3,2,1,0:T(8,128)S(1)} collective-permute-done((f32[2,2,2,2,2,2,8,640]{7,6,5,4,3,2,1,0:T(8,128)S(1)}, f32[2,2,2,2,2,2,8,640]{7,6,5,4,3,2,1,0:T(8,128)S(1)}, u32[]{:S(2)}, u32[]{:S(2)}) %collective-permute-start.14) | collective-permute-done | bytes 1310752 | tf_op jit(solution)/shard_map/ppermute | solution.py:248
  197.4 1.0 fusion.11
  198.5 0.9 fusion.25
  199.4 4.9 %collective-permute-done.12 = f32[2,2,2,2,2,2,8,384]{7,6,5,3,4,2,1,0:T(8,128)S(1)} collective-permute-done((f32[2,2,2,2,2,2,8,384]{7,6,5,3,4,2,1,0:T(8,128)S(1)}, f32[2,2,2,2,2,2,8,384]{7,6,5,3,4,2,1,0:T(8,128)S(1)}, u32[]{:S(2)}, u32[]{:S(2)}) %collective-permute-start.12) | collective-permute-done | bytes 786464 | tf_op jit(solution)/shard_map/ppermute | solution.py:248
  204.3 1.0 fusion.18
  205.3 3.5 %collective-permute-start.19 = (f32[2,2,2,2,8,640]{5,4,3,2,1,0:T(8,128)}, f32[2,2,2,2,8,640]{5,4,3,2,1,0:T(8,128)S(1)}, u32[]{:S(2)}, u32[]{:S(2)}) collective-permute-start(f32[2,2,2,2,8,640]{5,4,3,2,1,0:T(8,128)} %get-tuple-element.105), channel_id=1, source_target_pairs={{0,1},{1,0},{2,3},{3,2},{8,11},{9,10},{10,9},{11,8},{4,5},{5,4},{6... | collective-permute-start | bytes 983048 | tf_op jit(solution)/shard_map/ppermute | solution.py:248
  208.9 1.1 fusion.21
  210.0 2.6 %collective-permute-start.18 = (f32[2,2,2,2,8,640]{5,4,3,2,1,0:T(8,128)S(1)}, f32[2,2,2,2,8,640]{5,4,3,2,1,0:T(8,128)S(1)}, u32[]{:S(2)}, u32[]{:S(2)}) collective-permute-start(f32[2,2,2,2,8,640]{5,4,3,2,1,0:T(8,128)S(1)} %get-tuple-element.104), channel_id=1, source_target_pairs={{0,16},{16,0},{4,20},{20,4},{8,28},{24,12},{12,24},{28,8},{1,17},{... | collective-permute-start | bytes 983048 | tf_op jit(solution)/shard_map/ppermute | solution.py:248
  212.6 0.9 collective-permute-done.15
  213.5 1.0 fusion.29
  214.7 2.5 %collective-permute-done.18 = f32[2,2,2,2,8,640]{5,4,3,2,1,0:T(8,128)S(1)} collective-permute-done((f32[2,2,2,2,8,640]{5,4,3,2,1,0:T(8,128)S(1)}, f32[2,2,2,2,8,640]{5,4,3,2,1,0:T(8,128)S(1)}, u32[]{:S(2)}, u32[]{:S(2)}) %collective-permute-start.18) | collective-permute-done | bytes 327712 | tf_op jit(solution)/shard_map/ppermute | solution.py:248
  217.3 1.8 collective-permute-done.17
  219.1 1.0 fusion.32
  220.2 1.6 collective-permute-done.21
  221.9 5.7 %collective-permute-start.23 = (f32[2,2,8,640]{3,2,1,0:T(8,128)S(1)}, f32[2,2,8,640]{3,2,1,0:T(8,128)S(1)}, u32[]{:S(2)}, u32[]{:S(2)}) collective-permute-start(f32[2,2,8,640]{3,2,1,0:T(8,128)S(1)} %get-tuple-element.116), channel_id=1, source_target_pairs={{0,8},{8,0},{1,9},{9,1},{2,10},{10,2},{3,11},{11,3},{4,12},{12,4},... | collective-permute-start | bytes 245768 | tf_op jit(solution)/shard_map/ppermute | solution.py:252
  228.2 0.7 collective-permute-done.24
  229.2 3.1 %shard_map.97 = f32[2,8,4,2,1024]{4,3,2,1,0:T(2,128)} custom-call(f32[2,2,4,8,1024]{4,3,2,1,0:T(8,128)S(1)} %pad_maximum_fusion.sum_ref, f32[2,2,2,256,256]{4,3,2,1,0:T(8,128)S(1)} %broadcast_multiply_fusion.right_ref, f32[2,8,64,64]{3,2,1,0:T(8,128)S(1)} %reshape.654.left_ref), custom_call_target="tpu_custom_call" | custom-call | flops 268435456 | bytes 4194304 | tf_op jit(solution)/shard_map/pallas_call | solution.py:319
  (104 shorter events, 4.4 us)
Async XLA Ops:
  0.7 22.5 %collective-permute-start = (f32[4,64]{1,0:T(4,128)S(1)}, f32[4,64]{1,0:T(4,128)S(1)}, u32[]{:S(2)}, u32[]{:S(2)}) collective-permute-start(f32[4,64]{1,0:T(4,128)S(1)} %add_convert_fusion), channel_id=1, source_target_pairs={{0,8},{8,0},{1,9},{9,1},{2,10},{10,2},{3,11},{11,3},{4,12},{12,4},... | collective-permute-start | bytes 3080 | tf_op jit(solution)/shard_map/ppermute | solution.py:252
  29.2 22.1 %collective-permute-start.1 = (f32[16,2,64,640]{3,2,1,0:T(8,128)}, f32[16,2,64,640]{3,2,1,0:T(8,128)}, u32[]{:S(2)}, u32[]{:S(2)}) collective-permute-start(f32[16,2,64,640]{3,2,1,0:T(8,128)} %shard_map.91), channel_id=1, source_target_pairs={{0,8},{8,0},{1,9},{9,1},{2,10},{10,2},{3,11},{11,3},{4,12},{12,4},... | collective-permute-start | bytes 15728648 | tf_op jit(solution)/shard_map/ppermute | solution.py:252
  39.6 10.3 %copy-start.7 = (f32[3,128]{1,0:T(4,128)S(1)}, f32[3,128]{1,0:T(4,128)}, u32[]{:S(2)}) copy-start(f32[3,128]{1,0:T(4,128)} %param.15) | copy-start | bytes 4612
  45.6 20.3 %collective-permute-start.2 = (f32[16,2,64,640]{3,2,1,0:T(8,128)}, f32[16,2,64,640]{3,2,1,0:T(8,128)}, u32[]{:S(2)}, u32[]{:S(2)}) collective-permute-start(f32[16,2,64,640]{3,2,1,0:T(8,128)} %shard_map.93), channel_id=1, source_target_pairs={{0,8},{8,0},{1,9},{9,1},{2,10},{10,2},{3,11},{11,3},{4,12},{12,4},... | collective-permute-start | bytes 15728648 | tf_op jit(solution)/shard_map/ppermute | solution.py:252
  46.1 72.5 %collective-permute-start.3 = (f32[2,2,2,2,8,2,2,8,384]{8,7,6,5,4,3,2,1,0:T(8,128)}, f32[2,2,2,2,8,2,2,8,384]{8,7,6,5,4,3,2,1,0:T(8,128)}, u32[]{:S(2)}, u32[]{:S(2)}) collective-permute-start(f32[2,2,2,2,8,2,2,8,384]{8,7,6,5,4,3,2,1,0:T(8,128)} %get-tuple-element.55), channel_id=1, source_target_pairs={{0,1},{1,0},{2,3},{3,2},{8,11},{9,10},{10,9},{11,8},{4,5},{5,4},{6... | collective-permute-start | bytes 18874376 | tf_op jit(solution)/shard_map/ppermute | solution.py:248
  60.7 2.3 copy-start.1
  63.0 60.1 %collective-permute-start.6 = (f32[2,2,2,2,2,2,2,2,8,640]{9,8,7,6,5,4,3,2,1,0:T(8,128)}, f32[2,2,2,2,2,2,2,2,8,640]{9,8,7,6,5,4,3,2,1,0:T(8,128)}, u32[]{:S(2)}, u32[]{:S(2)}) collective-permute-start(f32[2,2,2,2,2,2,2,2,8,640]{9,8,7,6,5,4,3,2,1,0:T(8,128)} %get-tuple-element.64), channel_id=1, source_target_pairs={{0,16},{16,0},{4,20},{20,4},{8,28},{24,12},{12,24},{28,8},{1,17},{... | collective-permute-start | bytes 15728648 | tf_op jit(solution)/shard_map/ppermute | solution.py:248
  65.9 14.5 %copy-start.6 = (f32[2,2,32,32]{3,2,1,0:T(8,128)S(1)}, f32[2,2,32,32]{3,2,1,0:T(8,128)}, u32[]{:S(2)}) copy-start(f32[2,2,32,32]{3,2,1,0:T(8,128)} %param.16) | copy-start | bytes 49156
  75.4 2.3 copy-start
  77.6 60.4 %collective-permute-start.5 = (f32[2,2,2,2,2,2,2,2,8,640]{9,8,7,6,5,4,3,2,1,0:T(8,128)}, f32[2,2,2,2,2,2,2,2,8,640]{9,8,7,6,5,4,3,2,1,0:T(8,128)}, u32[]{:S(2)}, u32[]{:S(2)}) collective-permute-start(f32[2,2,2,2,2,2,2,2,8,640]{9,8,7,6,5,4,3,2,1,0:T(8,128)} %get-tuple-element.63), channel_id=1, source_target_pairs={{0,32},{32,0},{64,96},{96,64},{8,104},{40,72},{72,40},{104,8},{1,3... | collective-permute-start | bytes 15728648 | tf_op jit(solution)/shard_map/ppermute | solution.py:248
  84.8 7.1 %copy-start.5 = (f32[2,8,2,32,32]{4,3,2,1,0:T(8,128)S(1)}, f32[2,8,2,32,32]{4,3,2,1,0:T(8,128)}, u32[]{:S(2)}) copy-start(f32[2,8,2,32,32]{4,3,2,1,0:T(8,128)} %param.17) | copy-start | bytes 393220
  93.5 29.6 %slice-start.2 = ((s8[5242880]{0:T(1024)(128)(4,1)}), s8[4194304]{0:T(1024)(128)(4,1)S(1)}, s32[]{:S(2)}) async-start(s8[5242880]{0:T(1024)(128)(4,1)} %bitcast.281), calls=%async_computation.2 | async-start | bytes 8388608
  93.5 32.4 %slice-start.4 = ((s8[6291456]{0:T(1024)(128)(4,1)}), s8[4194304]{0:T(1024)(128)(4,1)S(1)}, s32[]{:S(2)}) async-start(s8[6291456]{0:T(1024)(128)(4,1)} %bitcast.290), calls=%async_computation.4 | async-start | bytes 8388608
  95.4 27.7 %slice-start.3 = ((s8[5242880]{0:T(1024)(128)(4,1)}), s8[1048576]{0:T(1024)(128)(4,1)S(1)}, s32[]{:S(2)}) async-start(s8[5242880]{0:T(1024)(128)(4,1)} %bitcast.281), calls=%async_computation.3 | async-start | bytes 2097152
  95.4 30.4 %slice-start.5 = ((s8[6291456]{0:T(1024)(128)(4,1)}), s8[2097152]{0:T(1024)(128)(4,1)S(1)}, s32[]{:S(2)}) async-start(s8[6291456]{0:T(1024)(128)(4,1)} %bitcast.290), calls=%async_computation.5 | async-start | bytes 4194304
  122.1 36.6 %collective-permute-start.4 = (f32[2,2,2,8,2,2,8,384]{7,6,5,4,3,2,1,0:T(8,128)S(1)}, f32[2,2,2,8,2,2,8,384]{7,6,5,4,3,2,1,0:T(8,128)S(1)}, u32[]{:S(2)}, u32[]{:S(2)}) collective-permute-start(f32[2,2,2,8,2,2,8,384]{7,6,5,4,3,2,1,0:T(8,128)S(1)} %add_bitcast_fusion), channel_id=1, source_target_pairs={{0,3},{1,2},{2,1},{3,0},{8,9},{9,8},{10,11},{11,10},{4,7},{5,6},{6... | collective-permute-start | bytes 9437192 | tf_op jit(solution)/shard_map/ppermute | solution.py:248
  123.1 14.9 %slice-start = ((s8[5242880]{0:T(1024)(128)(4,1)}), s8[4194304]{0:T(1024)(128)(4,1)S(1)}, s32[]{:S(2)}) async-start(s8[5242880]{0:T(1024)(128)(4,1)} %bitcast.279), calls=%async_computation | async-start | bytes 8388608
  125.4 12.6 %slice-start.1 = ((s8[5242880]{0:T(1024)(128)(4,1)}), s8[1048576]{0:T(1024)(128)(4,1)S(1)}, s32[]{:S(2)}) async-start(s8[5242880]{0:T(1024)(128)(4,1)} %bitcast.279), calls=%async_computation.1 | async-start | bytes 2097152
  125.4 37.7 %collective-permute-start.8 = (f32[2,2,2,2,2,2,2,8,640]{8,7,6,5,4,3,2,1,0:T(8,128)S(1)}, f32[2,2,2,2,2,2,2,8,640]{8,7,6,5,4,3,2,1,0:T(8,128)S(1)}, u32[]{:S(2)}, u32[]{:S(2)}) collective-permute-start(f32[2,2,2,2,2,2,2,8,640]{8,7,6,5,4,3,2,1,0:T(8,128)S(1)} %add_bitcast_fusion.2), channel_id=1, source_target_pairs={{0,20},{16,4},{4,16},{20,0},{8,24},{24,8},{12,28},{28,12},{1,21},{... | collective-permute-start | bytes 7864328 | tf_op jit(solution)/shard_map/ppermute | solution.py:248
  141.6 35.3 %collective-permute-start.11 = (f32[2,2,2,2,2,2,2,8,640]{8,7,6,5,4,3,2,1,0:T(8,128)}, f32[2,2,2,2,2,2,2,8,640]{8,7,6,5,4,3,2,1,0:T(8,128)}, u32[]{:S(2)}, u32[]{:S(2)}) collective-permute-start(f32[2,2,2,2,2,2,2,8,640]{8,7,6,5,4,3,2,1,0:T(8,128)} %add_bitcast_fusion.1), channel_id=1, source_target_pairs={{0,96},{32,64},{64,32},{96,0},{8,40},{40,8},{72,104},{104,72},{1,9... | collective-permute-start | bytes 7864328 | tf_op jit(solution)/shard_map/ppermute | solution.py:248
  159.3 8.5 %collective-permute-start.7 = (f32[2,2,8,2,2,8,384]{6,5,4,3,2,1,0:T(8,128)S(1)}, f32[2,2,8,2,2,8,384]{6,5,4,3,2,1,0:T(8,128)S(1)}, u32[]{:S(2)}, u32[]{:S(2)}) collective-permute-start(f32[2,2,8,2,2,8,384]{6,5,4,3,2,1,0:T(8,128)S(1)} %get-tuple-element.90), channel_id=1, source_target_pairs={{0,8},{8,0},{1,9},{9,1},{2,10},{10,2},{3,11},{11,3},{4,12},{12,4},... | collective-permute-start | bytes 4718600 | tf_op jit(solution)/shard_map/ppermute | solution.py:252
  165.0 20.1 %collective-permute-start.10 = (f32[2,2,2,2,2,2,8,640]{7,6,5,4,3,2,1,0:T(8,128)}, f32[2,2,2,2,2,2,8,640]{7,6,5,4,3,2,1,0:T(8,128)}, u32[]{:S(2)}, u32[]{:S(2)}) collective-permute-start(f32[2,2,2,2,2,2,8,640]{7,6,5,4,3,2,1,0:T(8,128)} %get-tuple-element.93), channel_id=1, source_target_pairs={{0,32},{32,0},{64,96},{96,64},{8,104},{40,72},{72,40},{104,8},{1,3... | collective-permute-start | bytes 3932168 | tf_op jit(solution)/shard_map/ppermute | solution.py:248
  167.8 1.2 copy-start.8
  172.2 20.6 %collective-permute-start.9 = (f32[2,2,2,2,2,2,2,8,384]{8,7,6,4,5,3,2,1,0:T(8,128)S(1)}, f32[2,2,2,2,2,2,2,8,384]{8,7,6,4,5,3,2,1,0:T(8,128)S(1)}, u32[]{:S(2)}, u32[]{:S(2)}) collective-permute-start(f32[2,2,2,2,2,2,2,8,384]{8,7,6,4,5,3,2,1,0:T(8,128)S(1)} %copy.55), channel_id=1, source_target_pairs={{0,16},{16,0},{4,20},{20,4},{8,28},{24,12},{12,24},{28,8},{1,17},{... | collective-permute-start | bytes 4718600 | tf_op jit(solution)/shard_map/ppermute | solution.py:248
  176.9 8.2 %copy-start.2 = (f32[1,2,2,2,2,2,2,8,640]{8,7,6,5,4,3,2,1,0:T(8,128)S(1)}, f32[1,2,2,2,2,2,2,8,640]{8,7,6,5,4,3,2,1,0:T(8,128)}, u32[]{:S(2)}) copy-start(f32[1,2,2,2,2,2,2,8,640]{8,7,6,5,4,3,2,1,0:T(8,128)} %get-tuple-element.94) | copy-start | bytes 3932164
  179.1 18.3 %collective-permute-start.14 = (f32[2,2,2,2,2,2,8,640]{7,6,5,4,3,2,1,0:T(8,128)S(1)}, f32[2,2,2,2,2,2,8,640]{7,6,5,4,3,2,1,0:T(8,128)S(1)}, u32[]{:S(2)}, u32[]{:S(2)}) collective-permute-start(f32[2,2,2,2,2,2,8,640]{7,6,5,4,3,2,1,0:T(8,128)S(1)} %get-tuple-element.92), channel_id=1, source_target_pairs={{0,1},{1,0},{2,3},{3,2},{8,11},{9,10},{10,9},{11,8},{4,5},{5,4},{6... | collective-permute-start | bytes 3932168 | tf_op jit(solution)/shard_map/ppermute | solution.py:248
  186.6 11.9 %collective-permute-start.13 = (f32[2,2,2,2,2,8,640]{6,5,4,3,2,1,0:T(8,128)S(1)}, f32[2,2,2,2,2,8,640]{6,5,4,3,2,1,0:T(8,128)S(1)}, u32[]{:S(2)}, u32[]{:S(2)}) collective-permute-start(f32[2,2,2,2,2,8,640]{6,5,4,3,2,1,0:T(8,128)S(1)} %get-tuple-element.99), channel_id=1, source_target_pairs={{0,96},{32,64},{64,32},{96,0},{8,40},{40,8},{72,104},{104,72},{1,9... | collective-permute-start | bytes 1966088 | tf_op jit(solution)/shard_map/ppermute | solution.py:248
  193.0 11.3 %collective-permute-start.12 = (f32[2,2,2,2,2,2,8,384]{7,6,5,3,4,2,1,0:T(8,128)S(1)}, f32[2,2,2,2,2,2,8,384]{7,6,5,3,4,2,1,0:T(8,128)S(1)}, u32[]{:S(2)}, u32[]{:S(2)}) collective-permute-start(f32[2,2,2,2,2,2,8,384]{7,6,5,3,4,2,1,0:T(8,128)S(1)} %get-tuple-element.96), channel_id=1, source_target_pairs={{0,20},{16,4},{4,16},{20,0},{8,24},{24,8},{12,28},{28,12},{1,21},{... | collective-permute-start | bytes 2359304 | tf_op jit(solution)/shard_map/ppermute | solution.py:248
  198.5 10.4 %collective-permute-start.16 = (f32[2,2,2,2,2,8,640]{6,5,4,3,2,1,0:T(8,128)}, f32[2,2,2,2,2,8,640]{6,5,4,3,2,1,0:T(8,128)}, u32[]{:S(2)}, u32[]{:S(2)}) collective-permute-start(f32[2,2,2,2,2,8,640]{6,5,4,3,2,1,0:T(8,128)} %get-tuple-element.98), channel_id=1, source_target_pairs={{0,3},{1,2},{2,1},{3,0},{8,9},{9,8},{10,11},{11,10},{4,7},{5,6},{6... | collective-permute-start | bytes 1966088 | tf_op jit(solution)/shard_map/ppermute | solution.py:248
  205.3 8.2 %collective-permute-start.15 = (f32[2,2,2,2,2,8,384]{6,5,4,2,3,1,0:T(8,128)}, f32[2,2,2,2,2,8,384]{6,5,4,2,3,1,0:T(8,128)}, u32[]{:S(2)}, u32[]{:S(2)}) collective-permute-start(f32[2,2,2,2,2,8,384]{6,5,4,2,3,1,0:T(8,128)} %get-tuple-element.101), channel_id=1, source_target_pairs={{0,32},{32,0},{64,96},{96,64},{8,104},{40,72},{72,40},{104,8},{1,3... | collective-permute-start | bytes 1179656 | tf_op jit(solution)/shard_map/ppermute | solution.py:248
  205.3 9.3 %copy-start.4 = (f32[1,2,2,2,2,8,640]{6,5,4,3,2,1,0:T(8,128)S(1)}, f32[1,2,2,2,2,8,640]{6,5,4,3,2,1,0:T(8,128)}, u32[]{:S(2)}) copy-start(f32[1,2,2,2,2,8,640]{6,5,4,3,2,1,0:T(8,128)} %get-tuple-element.106) | copy-start | bytes 983044
  205.3 13.8 %copy-start.3 = (f32[1,2,2,2,2,2,8,384]{7,6,5,3,4,2,1,0:T(8,128)S(1)}, f32[1,2,2,2,2,2,8,384]{7,6,5,3,4,2,1,0:T(8,128)}, u32[]{:S(2)}) copy-start(f32[1,2,2,2,2,2,8,384]{7,6,5,3,4,2,1,0:T(8,128)} %get-tuple-element.102) | copy-start | bytes 1179652
  205.3 9.3 %collective-permute-start.19 = (f32[2,2,2,2,8,640]{5,4,3,2,1,0:T(8,128)}, f32[2,2,2,2,8,640]{5,4,3,2,1,0:T(8,128)S(1)}, u32[]{:S(2)}, u32[]{:S(2)}) collective-permute-start(f32[2,2,2,2,8,640]{5,4,3,2,1,0:T(8,128)} %get-tuple-element.105), channel_id=1, source_target_pairs={{0,1},{1,0},{2,3},{3,2},{8,11},{9,10},{10,9},{11,8},{4,5},{5,4},{6... | collective-permute-start | bytes 983048 | tf_op jit(solution)/shard_map/ppermute | solution.py:248
  210.0 7.2 %collective-permute-start.18 = (f32[2,2,2,2,8,640]{5,4,3,2,1,0:T(8,128)S(1)}, f32[2,2,2,2,8,640]{5,4,3,2,1,0:T(8,128)S(1)}, u32[]{:S(2)}, u32[]{:S(2)}) collective-permute-start(f32[2,2,2,2,8,640]{5,4,3,2,1,0:T(8,128)S(1)} %get-tuple-element.104), channel_id=1, source_target_pairs={{0,16},{16,0},{4,20},{20,4},{8,28},{24,12},{12,24},{28,8},{1,17},{... | collective-permute-start | bytes 983048 | tf_op jit(solution)/shard_map/ppermute | solution.py:248
  214.5 4.6 %collective-permute-start.17 = (f32[2,2,2,2,8,384]{5,4,3,1,2,0:T(8,128)S(1)}, f32[2,2,2,2,8,384]{5,4,3,1,2,0:T(8,128)S(1)}, u32[]{:S(2)}, u32[]{:S(2)}) collective-permute-start(f32[2,2,2,2,8,384]{5,4,3,1,2,0:T(8,128)S(1)} %fusion.29), channel_id=1, source_target_pairs={{0,96},{32,64},{64,32},{96,0},{8,40},{40,8},{72,104},{104,72},{1,9... | collective-permute-start | bytes 589832 | tf_op jit(solution)/shard_map/ppermute | solution.py:248
  214.7 5.5 %collective-permute-start.20 = (f32[2,2,2,8,640]{4,3,2,1,0:T(8,128)S(1)}, f32[2,2,2,8,640]{4,3,2,1,0:T(8,128)S(1)}, u32[]{:S(2)}, u32[]{:S(2)}) collective-permute-start(f32[2,2,2,8,640]{4,3,2,1,0:T(8,128)S(1)} %fusion.40), channel_id=1, source_target_pairs={{0,3},{1,2},{2,1},{3,0},{8,9},{9,8},{10,11},{11,10},{4,7},{5,6},{6... | collective-permute-start | bytes 491528 | tf_op jit(solution)/shard_map/ppermute | solution.py:248
  217.2 4.5 %collective-permute-start.21 = (f32[2,2,2,8,640]{4,3,2,1,0:T(8,128)S(1)}, f32[2,2,2,8,640]{4,3,2,1,0:T(8,128)S(1)}, u32[]{:S(2)}, u32[]{:S(2)}) collective-permute-start(f32[2,2,2,8,640]{4,3,2,1,0:T(8,128)S(1)} %fusion.42), channel_id=1, source_target_pairs={{0,20},{16,4},{4,16},{20,0},{8,24},{24,8},{12,28},{28,12},{1,21},{... | collective-permute-start | bytes 491528 | tf_op jit(solution)/shard_map/ppermute | solution.py:248
  221.9 7.0 %collective-permute-start.23 = (f32[2,2,8,640]{3,2,1,0:T(8,128)S(1)}, f32[2,2,8,640]{3,2,1,0:T(8,128)S(1)}, u32[]{:S(2)}, u32[]{:S(2)}) collective-permute-start(f32[2,2,8,640]{3,2,1,0:T(8,128)S(1)} %get-tuple-element.116), channel_id=1, source_target_pairs={{0,8},{8,0},{1,9},{9,1},{2,10},{10,2},{3,11},{11,3},{4,12},{12,4},... | collective-permute-start | bytes 245768 | tf_op jit(solution)/shard_map/ppermute | solution.py:252
  227.6 1.3 collective-permute-start.24
  227.7 1.4 collective-permute-start.22

commit v3 on v2

--- a/solution.py
+++ b/solution.py
@@ -45,8 +45,11 @@
     return 2 * high + (low ^ high)
 
 
-def widen_kernel(where_ref, own_ref, out_ref):
-    out_ref[...] = own_ref[:, 0].astype(jnp.float32)
+def widen_kernel(part, where_ref, wide_ref, narrow_ref, out_ref):
+    sources = (wide_ref, narrow_ref) if part == "x" else (narrow_ref, wide_ref)
+    cut = sources[0].shape[-1]
+    out_ref[..., :cut] = sources[0][:, 0].astype(jnp.float32)
+    out_ref[..., cut:] = sources[1][:, 0].astype(jnp.float32)
 
 
 def spread(table_ref, wide_ref):
@@ -185,25 +188,31 @@
     )
 
 
-def own_spec(part, flip, block_of):
+def own_spec(part, block_of):
     def place(t, w):
         mode, block = block_place(part, block_of(t))
-        return (0, 2 * (w[0] ^ flip) + mode, 0, 0, block)
+        return (0, 2 * w[0] + mode, 0, 0, block)
 
     return pl.BlockSpec((16, 1, 2, 64, BLOCK), place)
 
 
 def widened(part, where, own):
+    def spec(blocks, mode):
+        lanes = blocks * BLOCK
+        at = 1 if blocks == 3 else 3
+        return pl.BlockSpec((4, 1, 2, 64, lanes), lambda r, w: (r, 2 * (w[0] ^ 1) + mode, 0, 0, at))
+
+    first = 0 if part == "x" else 1
     return kernel_call(
-        widen_kernel,
+        lambda *refs: widen_kernel(part, *refs),
         where,
-        (own,),
-        [own_spec(part, 1, lambda t: t)],
+        (own, own),
+        [spec(3, first), spec(2, 1 - first)],
         1,
         (16, 2, 64, BLOCKS * BLOCK),
-        (16, 2, 64, BLOCK),
-        lambda t, w: (0, 0, 0, t),
-        BLOCKS,
+        (4, 2, 64, BLOCKS * BLOCK),
+        lambda r, w: (r, 0, 0, 0),
+        4,
         [],
     )[0]
 
@@ -216,8 +225,8 @@
         [
             pl.BlockSpec((256, 256), lambda t, w: (0, 0)),
             pl.BlockSpec((32, 32), lambda t, w: (0, 0)),
-            own_spec(part, 0, lambda t: 2 * t),
-            own_spec(part, 0, lambda t: jnp.minimum(2 * t + 1, BLOCKS - 1)),
+            own_spec(part, lambda t: 2 * t),
+            own_spec(part, lambda t: jnp.minimum(2 * t + 1, BLOCKS - 1)),
             pl.BlockSpec((16, 2, 64, 2 * BLOCK), lambda t, w: (0, 0, 0, t)),
         ],
         2,
@@ -365,13 +374,13 @@
 
     (own,) = after(others, own)
     got_x = widened("x", where, own)
-    (wk,) = after(got_x, wk)
+    (later,) = after(got_x, own)
     got_x = swap(got_x)
+    got_y = widened("y", where, later)
+    (wk,) = after(got_y, wk)
+    got_y = swap(got_y)
     begin("z", electron_sums(where, wk, own))
-    (later,) = after(keep["z"], own)
-    got_y = widened("y", where, later)
-    wq, got_x = after(got_y, wq, got_x)
-    got_y = swap(got_y)
+    wq, got_x = after(keep["z"], wq, got_x)
     begin("x", partial_sums("x", where, wq, wk, own, got_x))
     wq, got_y = after(keep["x"], wq, got_y)
     begin("y", partial_sums("y", where, wq, wk, own, got_y))

time: 233 us -> 230 us (0.987)
    unnamed x31 -> x37, local copies, waits for them, and re-layouts: 24.4 us -> 24.4 us
  transfers between devices with their start and end apart: 25 -> 25, of which waited for: 14 -> 14; matrix products, arithmetic and copies ran while one was open for 29% -> 28% of each run, Pallas kernels for 16% -> 16%
where the time goes in v3:
time: 230 us; the launch traced here: 229 us
  waiting for transfers between devices  76.1 us (33%)
  Pallas kernels  45 us (20%)
  local copies, waits for them, and re-layouts  38.3 us (17%)
  starting transfers between devices  35.2 us (15%)
  other arithmetic  33.4 us (15%)
    ppermute x18, waiting for transfers between devices, exchange(): return lax.ppermute(value, names, pairs)  75.2 us
    pallas_call x6, Pallas kernels, kernel_call(): pl.pallas_call(kernel, grid_spec=pltpu.PrefetchScalarGridSpec(num_scalar_...  41.9 us
    ppermute x18, starting transfers between devices, exchange(): return lax.ppermute(value, names, pairs)  25.1 us
    unnamed x37, local copies, waits for them, and re-layouts  24.4 us
    add x10, other arithmetic, body(): latest = send[part] = keep[part][1] + arrived[part][1]  15.7 us
    mul x4, local copies, waits for them, and re-layouts, rotation_tables(): right = right * jnp.eye(8, dtype=jnp.float32)[:, None, :, None]  11.9 us
    ppermute x7, starting transfers between devices, swap(): return lax.ppermute(value, 'c', [(0, 1), (1, 0)])  10 us
    add x3, other arithmetic, body(): keep[part] = held[0] + came[0]  6.75 us
  transfers between devices with their start and end apart: 25, of which 14 were waited for; matrix products, arithmetic and copies ran while one was open for 28% of the time, Pallas kernels for 16%

profile of v3, /device:TPU:1, one launch (start us, length us, event | category | flops | bytes accessed | tf_op | source)
XLA Modules:
  0.0 228.6 jit_solution(3760829259911372054)
XLA Ops:
  0.0 0.7 add_convert_fusion
  0.7 1.5 collective-permute-start
  2.2 18.6 %copy.67 = bf16[16,64,4,2,1024]{4,1,3,2,0:T(8,128)(2,1)} copy(bf16[16,64,4,2,1024]{4,3,2,1,0:T(2,128)(2,1)} %param.9) | data formatting | bytes 33554432 | tf_op args[0]
  20.9 5.2 %shard_map.91 = f32[16,2,64,640]{3,2,1,0:T(8,128)} custom-call(s32[5]{0:T(128)S(1)} %stack.92.refs_0_.where_ref, bf16[16,4,2,64,1024]{4,3,2,1,0:T(8,128)(2,1)} %bitcast.283, bf16[16,4,2,64,1024]{4,3,2,1,0:T(8,128)(2,1)} %bitcast.284), custom_call_target="tpu_custom_call" | custom-call | flops 2147483648 | bytes 38797312 | tf_op jit(solution)/shard_map/pallas_call | solution.py:140
  26.2 5.2 %shard_map.92 = f32[16,2,64,640]{3,2,1,0:T(8,128)} custom-call(s32[5]{0:T(128)S(1)} %stack.92.refs_0_.where_ref, bf16[16,4,2,64,1024]{4,3,2,1,0:T(8,128)(2,1)} %bitcast.285, bf16[16,4,2,64,1024]{4,3,2,1,0:T(8,128)(2,1)} %bitcast.286), custom_call_target="tpu_custom_call" | custom-call | flops 2147483648 | bytes 38797312 | tf_op jit(solution)/shard_map/pallas_call | solution.py:140
  31.4 0.5 collective-permute-start.2
  32.6 9.7 %shard_map.93 = (f32[2,2,2,2,8,2,2,8,384]{8,7,6,5,4,3,2,1,0:T(8,128)}, f32[2,2,2,2,8,2,2,8,384]{8,7,6,5,4,3,2,1,0:T(8,128)}) custom-call(s32[5]{0:T(128)S(1)} %stack.92.refs_0_.where_ref, bf16[32,32]{1,0:T(8,128)(2,1)S(1)} %reshape.653.wk_ref.refs_2_, bf16[16,4,2,64,1024]{4,3,2,1,0:T(8,128)(2,1)} %bitcast.287), custom_call_target="tpu_custom_call" | custom-call | flops 2147483648 | bytes 29362176 | tf_op jit(solution)/shard_map/pallas_call | solution.py:140
  42.4 3.8 %collective-permute-start.3 = (f32[2,2,2,2,8,2,2,8,384]{8,7,6,5,4,3,2,1,0:T(8,128)}, f32[2,2,2,2,8,2,2,8,384]{8,7,6,5,4,3,2,1,0:T(8,128)}, u32[]{:S(2)}, u32[]{:S(2)}) collective-permute-start(f32[2,2,2,2,8,2,2,8,384]{8,7,6,5,4,3,2,1,0:T(8,128)} %get-tuple-element.55), channel_id=1, source_target_pairs={{0,1},{1,0},{2,3},{3,2},{8,11},{9,10},{10,9},{11,8},{4,5},{5,4},{6... | collective-permute-start | bytes 18874376 | tf_op jit(solution)/shard_map/ppermute | solution.py:257
  46.3 0.6 fusion.47
  46.8 0.6 multiply_convert_fusion.2
  47.6 9.4 %shard_map.94 = (f32[2,2,2,2,2,2,2,2,8,640]{9,8,7,6,5,4,3,2,1,0:T(8,128)S(1)}, f32[2,2,2,2,2,2,2,2,8,640]{9,8,7,6,5,4,3,2,1,0:T(8,128)}) custom-call(s32[5]{0:T(128)S(1)} %stack.92.refs_0_.where_ref, bf16[256,256]{1,0:T(8,128)(2,1)S(1)} %maximum_maximum_fusion.refs_1_.wq_ref, bf16[32,32]{1,0:T(8,128)(2,1)S(1)} %reshape.653.wk_ref.refs_2_, ...), custom_call_target="tpu_custom_call" | custom-call | flops 2147483648 | bytes 49416192 | tf_op jit(solution)/shard_map/pallas_call | solution.py:140
  57.0 2.3 copy-done.1
  59.2 2.5 %collective-permute-start.6 = (f32[2,2,2,2,2,2,2,2,8,640]{9,8,7,6,5,4,3,2,1,0:T(8,128)}, f32[2,2,2,2,2,2,2,2,8,640]{9,8,7,6,5,4,3,2,1,0:T(8,128)}, u32[]{:S(2)}, u32[]{:S(2)}) collective-permute-start(f32[2,2,2,2,2,2,2,2,8,640]{9,8,7,6,5,4,3,2,1,0:T(8,128)} %get-tuple-element.64), channel_id=1, source_target_pairs={{0,16},{16,0},{4,20},{20,4},{8,28},{24,12},{12,24},{28,8},{1,17},{... | collective-permute-start | bytes 15728648 | tf_op jit(solution)/shard_map/ppermute | solution.py:257
  62.2 9.4 %shard_map.95 = (f32[2,2,2,2,2,2,2,2,8,640]{9,8,7,6,5,4,3,2,1,0:T(8,128)S(1)}, f32[2,2,2,2,2,2,2,2,8,640]{9,8,7,6,5,4,3,2,1,0:T(8,128)}) custom-call(s32[5]{0:T(128)S(1)} %stack.92.refs_0_.where_ref, bf16[256,256]{1,0:T(8,128)(2,1)S(1)} %maximum_maximum_fusion.refs_1_.wq_ref, bf16[32,32]{1,0:T(8,128)(2,1)S(1)} %reshape.653.wk_ref.refs_2_, ...), custom_call_target="tpu_custom_call" | custom-call | flops 2147483648 | bytes 49416192 | tf_op jit(solution)/shard_map/pallas_call | solution.py:140
  71.6 2.3 copy-done
  73.9 2.7 %collective-permute-start.5 = (f32[2,2,2,2,2,2,2,2,8,640]{9,8,7,6,5,4,3,2,1,0:T(8,128)}, f32[2,2,2,2,2,2,2,2,8,640]{9,8,7,6,5,4,3,2,1,0:T(8,128)}, u32[]{:S(2)}, u32[]{:S(2)}) collective-permute-start(f32[2,2,2,2,2,2,2,2,8,640]{9,8,7,6,5,4,3,2,1,0:T(8,128)} %get-tuple-element.63), channel_id=1, source_target_pairs={{0,32},{32,0},{64,96},{96,64},{8,104},{40,72},{72,40},{104,8},{1,3... | collective-permute-start | bytes 15728648 | tf_op jit(solution)/shard_map/ppermute | solution.py:257
  76.7 4.4 %mul.351 = f32[2,2,2,8,32,8,32]{6,5,4,3,2,1,0:T(8,128)} broadcast(f32[2,2,2,32,32]{4,3,2,1,0:T(8,128)S(1)} %copy.51), dimensions={0,1,2,4,6} | broadcast | bytes 2129920 | tf_op jit(solution)/shard_map/mul | solution.py:270
  81.0 7.1 %mul.352 = f32[2,2,2,256,256]{4,3,2,1,0:T(8,128)} reshape(f32[2,2,2,8,32,8,32]{6,5,4,3,2,1,0:T(8,128)} %mul.351) | data formatting | bytes 4194304 | tf_op jit(solution)/shard_map/mul | solution.py:270
  88.5 0.6 copy.53
  89.1 0.6 reshape.654.left_ref
  89.7 1.9 broadcast_multiply_fusion.right_ref
  91.7 23.2 %collective-permute-done.3 = f32[2,2,2,2,8,2,2,8,384]{8,7,6,5,4,3,2,1,0:T(8,128)} collective-permute-done((f32[2,2,2,2,8,2,2,8,384]{8,7,6,5,4,3,2,1,0:T(8,128)}, f32[2,2,2,2,8,2,2,8,384]{8,7,6,5,4,3,2,1,0:T(8,128)}, u32[]{:S(2)}, u32[]{:S(2)}) %collective-permute-start.3) | collective-permute-done | bytes 6291488 | tf_op jit(solution)/shard_map/ppermute | solution.py:257
  114.9 3.5 %add_bitcast_fusion = f32[2,2,2,8,2,2,8,384]{7,6,5,4,3,2,1,0:T(8,128)S(1)} fusion(f32[2,2,2,2,8,2,2,8,384]{8,7,6,5,4,3,2,1,0:T(8,128)} %collective-permute-done.3, f32[2,2,2,2,8,2,2,8,384]{8,7,6,5,4,3,2,1,0:T(8,128)} %get-tuple-element.61), kind=kLoop, calls=%fused_computation.2 | loop fusion | flops 786432 | bytes 9437184 | tf_op jit(solution)/shard_map/add | solution.py:395
  118.5 0.9 collective-permute-done.6
  119.4 2.3 %add_bitcast_fusion.2 = f32[2,2,2,2,2,2,2,8,640]{8,7,6,5,4,3,2,1,0:T(8,128)S(1)} fusion(f32[2,2,2,2,2,2,2,2,8,640]{9,8,7,6,5,4,3,2,1,0:T(8,128)} %collective-permute-done.6, f32[2,2,2,2,2,2,2,2,8,640]{9,8,7,6,5,4,3,2,1,0:T(8,128)S(1)} %bitcast.282), kind=kLoop, calls=%fused_computation.6 | loop fusion | flops 655360 | bytes 7864320 | tf_op jit(solution)/shard_map/add | solution.py:395
  121.7 0.4 collective-permute-start.8
  122.1 2.5 %slice_add_fusion = f32[1,2,2,2,8,2,2,8,384]{8,7,6,5,4,3,2,1,0:T(8,128)S(1)} fusion(f32[2,2,2,2,8,2,2,8,384]{8,7,6,5,4,3,2,1,0:T(8,128)} %collective-permute-done.3, f32[2,2,2,2,8,2,2,8,384]{8,7,6,5,4,3,2,1,0:T(8,128)S(1)} %bitcast.293), kind=kLoop, calls=%fused_computation.1 | loop fusion | flops 786432 | bytes 9437184 | tf_op jit(solution)/shard_map/add | solution.py:398
  124.6 9.6 %collective-permute-done.5 = f32[2,2,2,2,2,2,2,2,8,640]{9,8,7,6,5,4,3,2,1,0:T(8,128)} collective-permute-done((f32[2,2,2,2,2,2,2,2,8,640]{9,8,7,6,5,4,3,2,1,0:T(8,128)}, f32[2,2,2,2,2,2,2,2,8,640]{9,8,7,6,5,4,3,2,1,0:T(8,128)}, u32[]{:S(2)}, u32[]{:S(2)}) %collective-permute-start.5) | collective-permute-done | bytes 5242912 | tf_op jit(solution)/shard_map/ppermute | solution.py:257
  134.2 3.6 %add_bitcast_fusion.1 = f32[2,2,2,2,2,2,2,8,640]{8,7,6,5,4,3,2,1,0:T(8,128)} fusion(f32[2,2,2,2,2,2,2,2,8,640]{9,8,7,6,5,4,3,2,1,0:T(8,128)} %collective-permute-done.5, f32[2,2,2,2,2,2,2,2,8,640]{9,8,7,6,5,4,3,2,1,0:T(8,128)S(1)} %bitcast.280), kind=kLoop, calls=%fused_computation.5 | loop fusion | flops 655360 | bytes 7864320 | tf_op jit(solution)/shard_map/add | solution.py:395
  137.9 17.1 %collective-permute-done.4 = f32[2,2,2,8,2,2,8,384]{7,6,5,4,3,2,1,0:T(8,128)S(1)} collective-permute-done((f32[2,2,2,8,2,2,8,384]{7,6,5,4,3,2,1,0:T(8,128)S(1)}, f32[2,2,2,8,2,2,8,384]{7,6,5,4,3,2,1,0:T(8,128)S(1)}, u32[]{:S(2)}, u32[]{:S(2)}) %collective-permute-start.4) | collective-permute-done | bytes 3145760 | tf_op jit(solution)/shard_map/ppermute | solution.py:257
  155.0 0.6 fusion.3
  155.6 1.7 collective-permute-start.7
  157.3 2.1 slice_add_fusion.2
  159.4 1.9 fusion.9
  161.3 2.7 %collective-permute-start.10 = (f32[2,2,2,2,2,2,8,640]{7,6,5,4,3,2,1,0:T(8,128)}, f32[2,2,2,2,2,2,8,640]{7,6,5,4,3,2,1,0:T(8,128)}, u32[]{:S(2)}, u32[]{:S(2)}) collective-permute-start(f32[2,2,2,2,2,2,8,640]{7,6,5,4,3,2,1,0:T(8,128)} %get-tuple-element.93), channel_id=1, source_target_pairs={{0,32},{32,0},{64,96},{96,64},{8,104},{40,72},{72,40},{104,8},{1,3... | collective-permute-start | bytes 3932168 | tf_op jit(solution)/shard_map/ppermute | solution.py:257
  164.1 1.1 copy-done.10
  165.2 3.1 %shard_map.96 = (f32[2,2,2,2,2,2,2,8,384]{8,7,6,5,4,3,2,1,0:T(8,128)S(1)}, f32[2,2,2,2,2,2,2,8,384]{8,7,6,5,4,3,2,1,0:T(8,128)S(1)}) custom-call(s32[5]{0:T(128)S(1)} %stack.92.refs_0_.where_ref, bf16[256,256]{1,0:T(8,128)(2,1)S(1)} %maximum_maximum_fusion.refs_1_.wq_ref, f32[2,2,8,2,2,8,384]{6,5,4,3,2,1,0:T(8,128)S(1)} %get-tuple-element.89.own_ref, ...), custom_call_target="tpu_custom_call" | custom-call | flops 2147483648 | bytes 6422528 | tf_op jit(solution)/shard_map/pallas_call | solution.py:140
  168.5 2.6 %collective-permute-start.9 = (f32[2,2,2,2,2,2,2,8,384]{8,7,6,4,5,3,2,1,0:T(8,128)S(1)}, f32[2,2,2,2,2,2,2,8,384]{8,7,6,4,5,3,2,1,0:T(8,128)S(1)}, u32[]{:S(2)}, u32[]{:S(2)}) collective-permute-start(f32[2,2,2,2,2,2,2,8,384]{8,7,6,4,5,3,2,1,0:T(8,128)S(1)} %copy.55), channel_id=1, source_target_pairs={{0,16},{16,0},{4,20},{20,4},{8,28},{24,12},{12,24},{28,8},{1,17},{... | collective-permute-start | bytes 4718600 | tf_op jit(solution)/shard_map/ppermute | solution.py:257
  171.0 2.1 slice_add_fusion.1
  173.2 2.2 fusion.4
  175.4 3.0 %collective-permute-start.14 = (f32[2,2,2,2,2,2,8,640]{7,6,5,4,3,2,1,0:T(8,128)S(1)}, f32[2,2,2,2,2,2,8,640]{7,6,5,4,3,2,1,0:T(8,128)S(1)}, u32[]{:S(2)}, u32[]{:S(2)}) collective-permute-start(f32[2,2,2,2,2,2,8,640]{7,6,5,4,3,2,1,0:T(8,128)S(1)} %get-tuple-element.92), channel_id=1, source_target_pairs={{0,1},{1,0},{2,3},{3,2},{8,11},{9,10},{10,9},{11,8},{4,5},{5,4},{6... | collective-permute-start | bytes 3932168 | tf_op jit(solution)/shard_map/ppermute | solution.py:257
  178.4 3.0 %collective-permute-done.10 = f32[2,2,2,2,2,2,8,640]{7,6,5,4,3,2,1,0:T(8,128)} collective-permute-done((f32[2,2,2,2,2,2,8,640]{7,6,5,4,3,2,1,0:T(8,128)}, f32[2,2,2,2,2,2,8,640]{7,6,5,4,3,2,1,0:T(8,128)}, u32[]{:S(2)}, u32[]{:S(2)}) %collective-permute-start.10) | collective-permute-done | bytes 1310752 | tf_op jit(solution)/shard_map/ppermute | solution.py:257
  181.4 1.4 fusion.16
  182.8 0.5 collective-permute-start.13
  183.3 5.7 %collective-permute-done.9 = f32[2,2,2,2,2,2,2,8,384]{8,7,6,4,5,3,2,1,0:T(8,128)S(1)} collective-permute-done((f32[2,2,2,2,2,2,2,8,384]{8,7,6,4,5,3,2,1,0:T(8,128)S(1)}, f32[2,2,2,2,2,2,2,8,384]{8,7,6,4,5,3,2,1,0:T(8,128)S(1)}, u32[]{:S(2)}, u32[]{:S(2)}) %collective-permute-start.9) | collective-permute-done | bytes 1572896 | tf_op jit(solution)/shard_map/ppermute | solution.py:257
  189.3 0.4 collective-permute-start.12
  189.7 4.0 %collective-permute-done.14 = f32[2,2,2,2,2,2,8,640]{7,6,5,4,3,2,1,0:T(8,128)S(1)} collective-permute-done((f32[2,2,2,2,2,2,8,640]{7,6,5,4,3,2,1,0:T(8,128)S(1)}, f32[2,2,2,2,2,2,8,640]{7,6,5,4,3,2,1,0:T(8,128)S(1)}, u32[]{:S(2)}, u32[]{:S(2)}) %collective-permute-start.14) | collective-permute-done | bytes 1310752 | tf_op jit(solution)/shard_map/ppermute | solution.py:257
  193.7 1.0 fusion.11
  194.7 0.9 fusion.25
  195.7 4.9 %collective-permute-done.12 = f32[2,2,2,2,2,2,8,384]{7,6,5,3,4,2,1,0:T(8,128)S(1)} collective-permute-done((f32[2,2,2,2,2,2,8,384]{7,6,5,3,4,2,1,0:T(8,128)S(1)}, f32[2,2,2,2,2,2,8,384]{7,6,5,3,4,2,1,0:T(8,128)S(1)}, u32[]{:S(2)}, u32[]{:S(2)}) %collective-permute-start.12) | collective-permute-done | bytes 786464 | tf_op jit(solution)/shard_map/ppermute | solution.py:257
  200.6 1.0 fusion.18
  201.6 3.5 %collective-permute-start.19 = (f32[2,2,2,2,8,640]{5,4,3,2,1,0:T(8,128)}, f32[2,2,2,2,8,640]{5,4,3,2,1,0:T(8,128)S(1)}, u32[]{:S(2)}, u32[]{:S(2)}) collective-permute-start(f32[2,2,2,2,8,640]{5,4,3,2,1,0:T(8,128)} %get-tuple-element.105), channel_id=1, source_target_pairs={{0,1},{1,0},{2,3},{3,2},{8,11},{9,10},{10,9},{11,8},{4,5},{5,4},{6... | collective-permute-start | bytes 983048 | tf_op jit(solution)/shard_map/ppermute | solution.py:257
  205.1 1.1 fusion.21
  206.3 2.6 %collective-permute-start.18 = (f32[2,2,2,2,8,640]{5,4,3,2,1,0:T(8,128)S(1)}, f32[2,2,2,2,8,640]{5,4,3,2,1,0:T(8,128)S(1)}, u32[]{:S(2)}, u32[]{:S(2)}) collective-permute-start(f32[2,2,2,2,8,640]{5,4,3,2,1,0:T(8,128)S(1)} %get-tuple-element.104), channel_id=1, source_target_pairs={{0,16},{16,0},{4,20},{20,4},{8,28},{24,12},{12,24},{28,8},{1,17},{... | collective-permute-start | bytes 983048 | tf_op jit(solution)/shard_map/ppermute | solution.py:257
  208.8 0.9 collective-permute-done.15
  209.7 1.0 fusion.29
  211.0 2.5 %collective-permute-done.18 = f32[2,2,2,2,8,640]{5,4,3,2,1,0:T(8,128)S(1)} collective-permute-done((f32[2,2,2,2,8,640]{5,4,3,2,1,0:T(8,128)S(1)}, f32[2,2,2,2,8,640]{5,4,3,2,1,0:T(8,128)S(1)}, u32[]{:S(2)}, u32[]{:S(2)}) %collective-permute-start.18) | collective-permute-done | bytes 327712 | tf_op jit(solution)/shard_map/ppermute | solution.py:257
  213.6 1.8 collective-permute-done.17
  215.4 1.0 fusion.32
  216.4 1.6 collective-permute-done.21
  218.2 5.7 %collective-permute-start.23 = (f32[2,2,8,640]{3,2,1,0:T(8,128)S(1)}, f32[2,2,8,640]{3,2,1,0:T(8,128)S(1)}, u32[]{:S(2)}, u32[]{:S(2)}) collective-permute-start(f32[2,2,8,640]{3,2,1,0:T(8,128)S(1)} %get-tuple-element.116), channel_id=1, source_target_pairs={{0,8},{8,0},{1,9},{9,1},{2,10},{10,2},{3,11},{11,3},{4,12},{12,4},... | collective-permute-start | bytes 245768 | tf_op jit(solution)/shard_map/ppermute | solution.py:261
  224.0 0.4 collective-permute-start.22
  224.5 0.7 collective-permute-done.24
  225.5 3.1 %shard_map.97 = f32[2,8,4,2,1024]{4,3,2,1,0:T(2,128)} custom-call(f32[2,2,4,8,1024]{4,3,2,1,0:T(8,128)S(1)} %pad_maximum_fusion.sum_ref, f32[2,2,2,256,256]{4,3,2,1,0:T(8,128)S(1)} %broadcast_multiply_fusion.right_ref, f32[2,8,64,64]{3,2,1,0:T(8,128)S(1)} %reshape.654.left_ref), custom_call_target="tpu_custom_call" | custom-call | flops 268435456 | bytes 4194304 | tf_op jit(solution)/shard_map/pallas_call | solution.py:328
  (110 shorter events, 3.4 us)
Async XLA Ops:
  0.7 20.2 %collective-permute-start = (f32[4,64]{1,0:T(4,128)S(1)}, f32[4,64]{1,0:T(4,128)S(1)}, u32[]{:S(2)}, u32[]{:S(2)}) collective-permute-start(f32[4,64]{1,0:T(4,128)S(1)} %add_convert_fusion), channel_id=1, source_target_pairs={{0,8},{8,0},{1,9},{9,1},{2,10},{10,2},{3,11},{11,3},{4,12},{12,4},... | collective-permute-start | bytes 3080 | tf_op jit(solution)/shard_map/ppermute | solution.py:261
  26.1 5.8 %copy-start.7 = (s32[3,16]{1,0:T(4,128)S(1)}, s32[3,16]{1,0:T(4,128)}, u32[]{:S(2)}) copy-start(s32[3,16]{1,0:T(4,128)} %param.10) | copy-start | bytes 580
  26.1 5.8 %copy-start.11 = (s32[16]{0:T(128)S(1)}, s32[16]{0:T(128)}, u32[]{:S(2)}) copy-start(s32[16]{0:T(128)} %param.12) | copy-start | bytes 196
  26.1 5.8 %copy-start.9 = (f32[3,16]{1,0:T(4,128)S(1)}, f32[3,16]{1,0:T(4,128)}, u32[]{:S(2)}) copy-start(f32[3,16]{1,0:T(4,128)} %param.14) | copy-start | bytes 580
  26.1 21.5 %collective-permute-start.1 = (f32[16,2,64,640]{3,2,1,0:T(8,128)}, f32[16,2,64,640]{3,2,1,0:T(8,128)}, u32[]{:S(2)}, u32[]{:S(2)}) collective-permute-start(f32[16,2,64,640]{3,2,1,0:T(8,128)} %shard_map.91), channel_id=1, source_target_pairs={{0,8},{8,0},{1,9},{9,1},{2,10},{10,2},{3,11},{11,3},{4,12},{12,4},... | collective-permute-start | bytes 15728648 | tf_op jit(solution)/shard_map/ppermute | solution.py:261
  31.4 30.8 %collective-permute-start.2 = (f32[16,2,64,640]{3,2,1,0:T(8,128)}, f32[16,2,64,640]{3,2,1,0:T(8,128)}, u32[]{:S(2)}, u32[]{:S(2)}) collective-permute-start(f32[16,2,64,640]{3,2,1,0:T(8,128)} %shard_map.92), channel_id=1, source_target_pairs={{0,8},{8,0},{1,9},{9,1},{2,10},{10,2},{3,11},{11,3},{4,12},{12,4},... | collective-permute-start | bytes 15728648 | tf_op jit(solution)/shard_map/ppermute | solution.py:261
  32.6 13.6 %copy-start.8 = (f32[3,128]{1,0:T(4,128)S(1)}, f32[3,128]{1,0:T(4,128)}, u32[]{:S(2)}) copy-start(f32[3,128]{1,0:T(4,128)} %param.15) | copy-start | bytes 4612
  42.4 72.5 %collective-permute-start.3 = (f32[2,2,2,2,8,2,2,8,384]{8,7,6,5,4,3,2,1,0:T(8,128)}, f32[2,2,2,2,8,2,2,8,384]{8,7,6,5,4,3,2,1,0:T(8,128)}, u32[]{:S(2)}, u32[]{:S(2)}) collective-permute-start(f32[2,2,2,2,8,2,2,8,384]{8,7,6,5,4,3,2,1,0:T(8,128)} %get-tuple-element.55), channel_id=1, source_target_pairs={{0,1},{1,0},{2,3},{3,2},{8,11},{9,10},{10,9},{11,8},{4,5},{5,4},{6... | collective-permute-start | bytes 18874376 | tf_op jit(solution)/shard_map/ppermute | solution.py:257
  57.0 2.3 copy-start.1
  59.2 60.1 %collective-permute-start.6 = (f32[2,2,2,2,2,2,2,2,8,640]{9,8,7,6,5,4,3,2,1,0:T(8,128)}, f32[2,2,2,2,2,2,2,2,8,640]{9,8,7,6,5,4,3,2,1,0:T(8,128)}, u32[]{:S(2)}, u32[]{:S(2)}) collective-permute-start(f32[2,2,2,2,2,2,2,2,8,640]{9,8,7,6,5,4,3,2,1,0:T(8,128)} %get-tuple-element.64), channel_id=1, source_target_pairs={{0,16},{16,0},{4,20},{20,4},{8,28},{24,12},{12,24},{28,8},{1,17},{... | collective-permute-start | bytes 15728648 | tf_op jit(solution)/shard_map/ppermute | solution.py:257
  62.2 14.4 %copy-start.6 = (f32[2,2,32,32]{3,2,1,0:T(8,128)S(1)}, f32[2,2,32,32]{3,2,1,0:T(8,128)}, u32[]{:S(2)}) copy-start(f32[2,2,32,32]{3,2,1,0:T(8,128)} %param.16) | copy-start | bytes 49156
  71.6 2.3 copy-start
  73.9 60.4 %collective-permute-start.5 = (f32[2,2,2,2,2,2,2,2,8,640]{9,8,7,6,5,4,3,2,1,0:T(8,128)}, f32[2,2,2,2,2,2,2,2,8,640]{9,8,7,6,5,4,3,2,1,0:T(8,128)}, u32[]{:S(2)}, u32[]{:S(2)}) collective-permute-start(f32[2,2,2,2,2,2,2,2,8,640]{9,8,7,6,5,4,3,2,1,0:T(8,128)} %get-tuple-element.63), channel_id=1, source_target_pairs={{0,32},{32,0},{64,96},{96,64},{8,104},{40,72},{72,40},{104,8},{1,3... | collective-permute-start | bytes 15728648 | tf_op jit(solution)/shard_map/ppermute | solution.py:257
  81.0 7.1 %copy-start.5 = (f32[2,8,2,32,32]{4,3,2,1,0:T(8,128)S(1)}, f32[2,8,2,32,32]{4,3,2,1,0:T(8,128)}, u32[]{:S(2)}) copy-start(f32[2,8,2,32,32]{4,3,2,1,0:T(8,128)} %param.17) | copy-start | bytes 393220
  89.7 29.7 %slice-start.2 = ((s8[5242880]{0:T(1024)(128)(4,1)}), s8[4194304]{0:T(1024)(128)(4,1)S(1)}, s32[]{:S(2)}) async-start(s8[5242880]{0:T(1024)(128)(4,1)} %bitcast.281), calls=%async_computation.2 | async-start | bytes 8388608
  89.7 32.4 %slice-start.4 = ((s8[6291456]{0:T(1024)(128)(4,1)}), s8[4194304]{0:T(1024)(128)(4,1)S(1)}, s32[]{:S(2)}) async-start(s8[6291456]{0:T(1024)(128)(4,1)} %bitcast.292), calls=%async_computation.4 | async-start | bytes 8388608
  91.6 27.7 %slice-start.3 = ((s8[5242880]{0:T(1024)(128)(4,1)}), s8[1048576]{0:T(1024)(128)(4,1)S(1)}, s32[]{:S(2)}) async-start(s8[5242880]{0:T(1024)(128)(4,1)} %bitcast.281), calls=%async_computation.3 | async-start | bytes 2097152
  91.7 30.5 %slice-start.5 = ((s8[6291456]{0:T(1024)(128)(4,1)}), s8[2097152]{0:T(1024)(128)(4,1)S(1)}, s32[]{:S(2)}) async-start(s8[6291456]{0:T(1024)(128)(4,1)} %bitcast.292), calls=%async_computation.5 | async-start | bytes 4194304
  118.4 36.6 %collective-permute-start.4 = (f32[2,2,2,8,2,2,8,384]{7,6,5,4,3,2,1,0:T(8,128)S(1)}, f32[2,2,2,8,2,2,8,384]{7,6,5,4,3,2,1,0:T(8,128)S(1)}, u32[]{:S(2)}, u32[]{:S(2)}) collective-permute-start(f32[2,2,2,8,2,2,8,384]{7,6,5,4,3,2,1,0:T(8,128)S(1)} %add_bitcast_fusion), channel_id=1, source_target_pairs={{0,3},{1,2},{2,1},{3,0},{8,9},{9,8},{10,11},{11,10},{4,7},{5,6},{6... | collective-permute-start | bytes 9437192 | tf_op jit(solution)/shard_map/ppermute | solution.py:257
  119.3 14.9 %slice-start = ((s8[5242880]{0:T(1024)(128)(4,1)}), s8[4194304]{0:T(1024)(128)(4,1)S(1)}, s32[]{:S(2)}) async-start(s8[5242880]{0:T(1024)(128)(4,1)} %bitcast.279), calls=%async_computation | async-start | bytes 8388608
  121.7 12.6 %slice-start.1 = ((s8[5242880]{0:T(1024)(128)(4,1)}), s8[1048576]{0:T(1024)(128)(4,1)S(1)}, s32[]{:S(2)}) async-start(s8[5242880]{0:T(1024)(128)(4,1)} %bitcast.279), calls=%async_computation.1 | async-start | bytes 2097152
  121.7 37.7 %collective-permute-start.8 = (f32[2,2,2,2,2,2,2,8,640]{8,7,6,5,4,3,2,1,0:T(8,128)S(1)}, f32[2,2,2,2,2,2,2,8,640]{8,7,6,5,4,3,2,1,0:T(8,128)S(1)}, u32[]{:S(2)}, u32[]{:S(2)}) collective-permute-start(f32[2,2,2,2,2,2,2,8,640]{8,7,6,5,4,3,2,1,0:T(8,128)S(1)} %add_bitcast_fusion.2), channel_id=1, source_target_pairs={{0,20},{16,4},{4,16},{20,0},{8,24},{24,8},{12,28},{28,12},{1,21},{... | collective-permute-start | bytes 7864328 | tf_op jit(solution)/shard_map/ppermute | solution.py:257
  137.9 35.3 %collective-permute-start.11 = (f32[2,2,2,2,2,2,2,8,640]{8,7,6,5,4,3,2,1,0:T(8,128)}, f32[2,2,2,2,2,2,2,8,640]{8,7,6,5,4,3,2,1,0:T(8,128)}, u32[]{:S(2)}, u32[]{:S(2)}) collective-permute-start(f32[2,2,2,2,2,2,2,8,640]{8,7,6,5,4,3,2,1,0:T(8,128)} %add_bitcast_fusion.1), channel_id=1, source_target_pairs={{0,96},{32,64},{64,32},{96,0},{8,40},{40,8},{72,104},{104,72},{1,9... | collective-permute-start | bytes 7864328 | tf_op jit(solution)/shard_map/ppermute | solution.py:257
  155.6 8.5 %collective-permute-start.7 = (f32[2,2,8,2,2,8,384]{6,5,4,3,2,1,0:T(8,128)S(1)}, f32[2,2,8,2,2,8,384]{6,5,4,3,2,1,0:T(8,128)S(1)}, u32[]{:S(2)}, u32[]{:S(2)}) collective-permute-start(f32[2,2,8,2,2,8,384]{6,5,4,3,2,1,0:T(8,128)S(1)} %get-tuple-element.90), channel_id=1, source_target_pairs={{0,8},{8,0},{1,9},{9,1},{2,10},{10,2},{3,11},{11,3},{4,12},{12,4},... | collective-permute-start | bytes 4718600 | tf_op jit(solution)/shard_map/ppermute | solution.py:261
  161.3 20.0 %collective-permute-start.10 = (f32[2,2,2,2,2,2,8,640]{7,6,5,4,3,2,1,0:T(8,128)}, f32[2,2,2,2,2,2,8,640]{7,6,5,4,3,2,1,0:T(8,128)}, u32[]{:S(2)}, u32[]{:S(2)}) collective-permute-start(f32[2,2,2,2,2,2,8,640]{7,6,5,4,3,2,1,0:T(8,128)} %get-tuple-element.93), channel_id=1, source_target_pairs={{0,32},{32,0},{64,96},{96,64},{8,104},{40,72},{72,40},{104,8},{1,3... | collective-permute-start | bytes 3932168 | tf_op jit(solution)/shard_map/ppermute | solution.py:257
  164.1 1.1 copy-start.10
  168.5 20.6 %collective-permute-start.9 = (f32[2,2,2,2,2,2,2,8,384]{8,7,6,4,5,3,2,1,0:T(8,128)S(1)}, f32[2,2,2,2,2,2,2,8,384]{8,7,6,4,5,3,2,1,0:T(8,128)S(1)}, u32[]{:S(2)}, u32[]{:S(2)}) collective-permute-start(f32[2,2,2,2,2,2,2,8,384]{8,7,6,4,5,3,2,1,0:T(8,128)S(1)} %copy.55), channel_id=1, source_target_pairs={{0,16},{16,0},{4,20},{20,4},{8,28},{24,12},{12,24},{28,8},{1,17},{... | collective-permute-start | bytes 4718600 | tf_op jit(solution)/shard_map/ppermute | solution.py:257
  173.2 8.2 %copy-start.2 = (f32[1,2,2,2,2,2,2,8,640]{8,7,6,5,4,3,2,1,0:T(8,128)S(1)}, f32[1,2,2,2,2,2,2,8,640]{8,7,6,5,4,3,2,1,0:T(8,128)}, u32[]{:S(2)}) copy-start(f32[1,2,2,2,2,2,2,8,640]{8,7,6,5,4,3,2,1,0:T(8,128)} %get-tuple-element.94) | copy-start | bytes 3932164
  175.4 18.3 %collective-permute-start.14 = (f32[2,2,2,2,2,2,8,640]{7,6,5,4,3,2,1,0:T(8,128)S(1)}, f32[2,2,2,2,2,2,8,640]{7,6,5,4,3,2,1,0:T(8,128)S(1)}, u32[]{:S(2)}, u32[]{:S(2)}) collective-permute-start(f32[2,2,2,2,2,2,8,640]{7,6,5,4,3,2,1,0:T(8,128)S(1)} %get-tuple-element.92), channel_id=1, source_target_pairs={{0,1},{1,0},{2,3},{3,2},{8,11},{9,10},{10,9},{11,8},{4,5},{5,4},{6... | collective-permute-start | bytes 3932168 | tf_op jit(solution)/shard_map/ppermute | solution.py:257
  182.8 11.9 %collective-permute-start.13 = (f32[2,2,2,2,2,8,640]{6,5,4,3,2,1,0:T(8,128)S(1)}, f32[2,2,2,2,2,8,640]{6,5,4,3,2,1,0:T(8,128)S(1)}, u32[]{:S(2)}, u32[]{:S(2)}) collective-permute-start(f32[2,2,2,2,2,8,640]{6,5,4,3,2,1,0:T(8,128)S(1)} %get-tuple-element.99), channel_id=1, source_target_pairs={{0,96},{32,64},{64,32},{96,0},{8,40},{40,8},{72,104},{104,72},{1,9... | collective-permute-start | bytes 1966088 | tf_op jit(solution)/shard_map/ppermute | solution.py:257
  189.3 11.3 %collective-permute-start.12 = (f32[2,2,2,2,2,2,8,384]{7,6,5,3,4,2,1,0:T(8,128)S(1)}, f32[2,2,2,2,2,2,8,384]{7,6,5,3,4,2,1,0:T(8,128)S(1)}, u32[]{:S(2)}, u32[]{:S(2)}) collective-permute-start(f32[2,2,2,2,2,2,8,384]{7,6,5,3,4,2,1,0:T(8,128)S(1)} %get-tuple-element.96), channel_id=1, source_target_pairs={{0,20},{16,4},{4,16},{20,0},{8,24},{24,8},{12,28},{28,12},{1,21},{... | collective-permute-start | bytes 2359304 | tf_op jit(solution)/shard_map/ppermute | solution.py:257
  194.7 10.4 %collective-permute-start.16 = (f32[2,2,2,2,2,8,640]{6,5,4,3,2,1,0:T(8,128)}, f32[2,2,2,2,2,8,640]{6,5,4,3,2,1,0:T(8,128)}, u32[]{:S(2)}, u32[]{:S(2)}) collective-permute-start(f32[2,2,2,2,2,8,640]{6,5,4,3,2,1,0:T(8,128)} %get-tuple-element.98), channel_id=1, source_target_pairs={{0,3},{1,2},{2,1},{3,0},{8,9},{9,8},{10,11},{11,10},{4,7},{5,6},{6... | collective-permute-start | bytes 1966088 | tf_op jit(solution)/shard_map/ppermute | solution.py:257
  201.6 8.2 %collective-permute-start.15 = (f32[2,2,2,2,2,8,384]{6,5,4,2,3,1,0:T(8,128)}, f32[2,2,2,2,2,8,384]{6,5,4,2,3,1,0:T(8,128)}, u32[]{:S(2)}, u32[]{:S(2)}) collective-permute-start(f32[2,2,2,2,2,8,384]{6,5,4,2,3,1,0:T(8,128)} %get-tuple-element.101), channel_id=1, source_target_pairs={{0,32},{32,0},{64,96},{96,64},{8,104},{40,72},{72,40},{104,8},{1,3... | collective-permute-start | bytes 1179656 | tf_op jit(solution)/shard_map/ppermute | solution.py:257
  201.6 9.3 %copy-start.4 = (f32[1,2,2,2,2,8,640]{6,5,4,3,2,1,0:T(8,128)S(1)}, f32[1,2,2,2,2,8,640]{6,5,4,3,2,1,0:T(8,128)}, u32[]{:S(2)}) copy-start(f32[1,2,2,2,2,8,640]{6,5,4,3,2,1,0:T(8,128)} %get-tuple-element.106) | copy-start | bytes 983044
  201.6 13.8 %copy-start.3 = (f32[1,2,2,2,2,2,8,384]{7,6,5,3,4,2,1,0:T(8,128)S(1)}, f32[1,2,2,2,2,2,8,384]{7,6,5,3,4,2,1,0:T(8,128)}, u32[]{:S(2)}) copy-start(f32[1,2,2,2,2,2,8,384]{7,6,5,3,4,2,1,0:T(8,128)} %get-tuple-element.102) | copy-start | bytes 1179652
  201.6 9.3 %collective-permute-start.19 = (f32[2,2,2,2,8,640]{5,4,3,2,1,0:T(8,128)}, f32[2,2,2,2,8,640]{5,4,3,2,1,0:T(8,128)S(1)}, u32[]{:S(2)}, u32[]{:S(2)}) collective-permute-start(f32[2,2,2,2,8,640]{5,4,3,2,1,0:T(8,128)} %get-tuple-element.105), channel_id=1, source_target_pairs={{0,1},{1,0},{2,3},{3,2},{8,11},{9,10},{10,9},{11,8},{4,5},{5,4},{6... | collective-permute-start | bytes 983048 | tf_op jit(solution)/shard_map/ppermute | solution.py:257
  206.3 7.2 %collective-permute-start.18 = (f32[2,2,2,2,8,640]{5,4,3,2,1,0:T(8,128)S(1)}, f32[2,2,2,2,8,640]{5,4,3,2,1,0:T(8,128)S(1)}, u32[]{:S(2)}, u32[]{:S(2)}) collective-permute-start(f32[2,2,2,2,8,640]{5,4,3,2,1,0:T(8,128)S(1)} %get-tuple-element.104), channel_id=1, source_target_pairs={{0,16},{16,0},{4,20},{20,4},{8,28},{24,12},{12,24},{28,8},{1,17},{... | collective-permute-start | bytes 983048 | tf_op jit(solution)/shard_map/ppermute | solution.py:257
  210.8 4.6 %collective-permute-start.17 = (f32[2,2,2,2,8,384]{5,4,3,1,2,0:T(8,128)S(1)}, f32[2,2,2,2,8,384]{5,4,3,1,2,0:T(8,128)S(1)}, u32[]{:S(2)}, u32[]{:S(2)}) collective-permute-start(f32[2,2,2,2,8,384]{5,4,3,1,2,0:T(8,128)S(1)} %fusion.29), channel_id=1, source_target_pairs={{0,96},{32,64},{64,32},{96,0},{8,40},{40,8},{72,104},{104,72},{1,9... | collective-permute-start | bytes 589832 | tf_op jit(solution)/shard_map/ppermute | solution.py:257
  210.9 5.5 %collective-permute-start.20 = (f32[2,2,2,8,640]{4,3,2,1,0:T(8,128)S(1)}, f32[2,2,2,8,640]{4,3,2,1,0:T(8,128)S(1)}, u32[]{:S(2)}, u32[]{:S(2)}) collective-permute-start(f32[2,2,2,8,640]{4,3,2,1,0:T(8,128)S(1)} %fusion.40), channel_id=1, source_target_pairs={{0,3},{1,2},{2,1},{3,0},{8,9},{9,8},{10,11},{11,10},{4,7},{5,6},{6... | collective-permute-start | bytes 491528 | tf_op jit(solution)/shard_map/ppermute | solution.py:257
  213.5 4.5 %collective-permute-start.21 = (f32[2,2,2,8,640]{4,3,2,1,0:T(8,128)S(1)}, f32[2,2,2,8,640]{4,3,2,1,0:T(8,128)S(1)}, u32[]{:S(2)}, u32[]{:S(2)}) collective-permute-start(f32[2,2,2,8,640]{4,3,2,1,0:T(8,128)S(1)} %fusion.42), channel_id=1, source_target_pairs={{0,20},{16,4},{4,16},{20,0},{8,24},{24,8},{12,28},{28,12},{1,21},{... | collective-permute-start | bytes 491528 | tf_op jit(solution)/shard_map/ppermute | solution.py:257
  218.2 7.0 %collective-permute-start.23 = (f32[2,2,8,640]{3,2,1,0:T(8,128)S(1)}, f32[2,2,8,640]{3,2,1,0:T(8,128)S(1)}, u32[]{:S(2)}, u32[]{:S(2)}) collective-permute-start(f32[2,2,8,640]{3,2,1,0:T(8,128)S(1)} %get-tuple-element.116), channel_id=1, source_target_pairs={{0,8},{8,0},{1,9},{9,1},{2,10},{10,2},{3,11},{11,3},{4,12},{12,4},... | collective-permute-start | bytes 245768 | tf_op jit(solution)/shard_map/ppermute | solution.py:261
  223.9 1.3 collective-permute-start.24
  224.0 1.4 collective-permute-start.22

commit v4 on v3

--- a/solution.py
+++ b/solution.py
@@ -200,7 +200,7 @@
     def spec(blocks, mode):
         lanes = blocks * BLOCK
         at = 1 if blocks == 3 else 3
-        return pl.BlockSpec((4, 1, 2, 64, lanes), lambda r, w: (r, 2 * (w[0] ^ 1) + mode, 0, 0, at))
+        return pl.BlockSpec((8, 1, 2, 64, lanes), lambda r, w: (r, 2 * (w[0] ^ 1) + mode, 0, 0, at))
 
     first = 0 if part == "x" else 1
     return kernel_call(
@@ -210,9 +210,9 @@
         [spec(3, first), spec(2, 1 - first)],
         1,
         (16, 2, 64, BLOCKS * BLOCK),
-        (4, 2, 64, BLOCKS * BLOCK),
+        (8, 2, 64, BLOCKS * BLOCK),
         lambda r, w: (r, 0, 0, 0),
-        4,
+        2,
         [],
     )[0]
 

time: 230 us -> 228 us (level)
  transfers between devices with their start and end apart: 25 -> 25, of which waited for: 14 -> 14; matrix products, arithmetic and copies ran while one was open for 28% -> 29% of each run, Pallas kernels for 16% -> 16%
where the time goes in v4:
time: 228 us; the launch traced here: 227 us
  waiting for transfers between devices  76.1 us (33%)
  Pallas kernels  43.4 us (19%)
  local copies, waits for them, and re-layouts  38.3 us (17%)
  starting transfers between devices  35.2 us (15%)
  other arithmetic  33.4 us (15%)
    ppermute x18, waiting for transfers between devices, exchange(): return lax.ppermute(value, names, pairs)  75.2 us
    pallas_call x6, Pallas kernels, kernel_call(): pl.pallas_call(kernel, grid_spec=pltpu.PrefetchScalarGridSpec(num_scalar_...  40.3 us
    ppermute x18, starting transfers between devices, exchange(): return lax.ppermute(value, names, pairs)  25.1 us
    unnamed x37, local copies, waits for them, and re-layouts  24.4 us
    add x10, other arithmetic, body(): latest = send[part] = keep[part][1] + arrived[part][1]  15.7 us
    mul x4, local copies, waits for them, and re-layouts, rotation_tables(): right = right * jnp.eye(8, dtype=jnp.float32)[:, None, :, None]  11.9 us
    ppermute x7, starting transfers between devices, swap(): return lax.ppermute(value, 'c', [(0, 1), (1, 0)])  10 us
    add x3, other arithmetic, body(): keep[part] = held[0] + came[0]  6.75 us
  transfers between devices with their start and end apart: 25, of which 14 were waited for; matrix products, arithmetic and copies ran while one was open for 29% of the time, Pallas kernels for 16%

profile of v4, /device:TPU:1, one launch (start us, length us, event | category | flops | bytes accessed | tf_op | source)
XLA Modules:
  0.0 227.0 jit_solution(13102303574809913656)
XLA Ops:
  0.0 0.7 add_convert_fusion
  0.7 1.5 collective-permute-start
  2.2 18.6 %copy.67 = bf16[16,64,4,2,1024]{4,1,3,2,0:T(8,128)(2,1)} copy(bf16[16,64,4,2,1024]{4,3,2,1,0:T(2,128)(2,1)} %param.9) | data formatting | bytes 33554432 | tf_op args[0]
  20.9 4.4 %shard_map.91 = f32[16,2,64,640]{3,2,1,0:T(8,128)} custom-call(s32[5]{0:T(128)S(1)} %stack.92.refs_0_.where_ref, bf16[16,4,2,64,1024]{4,3,2,1,0:T(8,128)(2,1)} %bitcast.283, bf16[16,4,2,64,1024]{4,3,2,1,0:T(8,128)(2,1)} %bitcast.284), custom_call_target="tpu_custom_call" | custom-call | flops 2147483648 | bytes 38797312 | tf_op jit(solution)/shard_map/pallas_call | solution.py:140
  25.4 4.3 %shard_map.92 = f32[16,2,64,640]{3,2,1,0:T(8,128)} custom-call(s32[5]{0:T(128)S(1)} %stack.92.refs_0_.where_ref, bf16[16,4,2,64,1024]{4,3,2,1,0:T(8,128)(2,1)} %bitcast.285, bf16[16,4,2,64,1024]{4,3,2,1,0:T(8,128)(2,1)} %bitcast.286), custom_call_target="tpu_custom_call" | custom-call | flops 2147483648 | bytes 38797312 | tf_op jit(solution)/shard_map/pallas_call | solution.py:140
  29.7 0.5 collective-permute-start.2
  31.0 9.7 %shard_map.93 = (f32[2,2,2,2,8,2,2,8,384]{8,7,6,5,4,3,2,1,0:T(8,128)}, f32[2,2,2,2,8,2,2,8,384]{8,7,6,5,4,3,2,1,0:T(8,128)}) custom-call(s32[5]{0:T(128)S(1)} %stack.92.refs_0_.where_ref, bf16[32,32]{1,0:T(8,128)(2,1)S(1)} %reshape.653.wk_ref.refs_2_, bf16[16,4,2,64,1024]{4,3,2,1,0:T(8,128)(2,1)} %bitcast.287), custom_call_target="tpu_custom_call" | custom-call | flops 2147483648 | bytes 29362176 | tf_op jit(solution)/shard_map/pallas_call | solution.py:140
  40.8 3.8 %collective-permute-start.3 = (f32[2,2,2,2,8,2,2,8,384]{8,7,6,5,4,3,2,1,0:T(8,128)}, f32[2,2,2,2,8,2,2,8,384]{8,7,6,5,4,3,2,1,0:T(8,128)}, u32[]{:S(2)}, u32[]{:S(2)}) collective-permute-start(f32[2,2,2,2,8,2,2,8,384]{8,7,6,5,4,3,2,1,0:T(8,128)} %get-tuple-element.55), channel_id=1, source_target_pairs={{0,1},{1,0},{2,3},{3,2},{8,11},{9,10},{10,9},{11,8},{4,5},{5,4},{6... | collective-permute-start | bytes 18874376 | tf_op jit(solution)/shard_map/ppermute | solution.py:257
  44.6 0.6 fusion.47
  45.2 0.6 multiply_convert_fusion.2
  45.9 9.4 %shard_map.94 = (f32[2,2,2,2,2,2,2,2,8,640]{9,8,7,6,5,4,3,2,1,0:T(8,128)S(1)}, f32[2,2,2,2,2,2,2,2,8,640]{9,8,7,6,5,4,3,2,1,0:T(8,128)}) custom-call(s32[5]{0:T(128)S(1)} %stack.92.refs_0_.where_ref, bf16[256,256]{1,0:T(8,128)(2,1)S(1)} %maximum_maximum_fusion.refs_1_.wq_ref, bf16[32,32]{1,0:T(8,128)(2,1)S(1)} %reshape.653.wk_ref.refs_2_, ...), custom_call_target="tpu_custom_call" | custom-call | flops 2147483648 | bytes 49416192 | tf_op jit(solution)/shard_map/pallas_call | solution.py:140
  55.3 2.3 copy-done.1
  57.6 2.5 %collective-permute-start.6 = (f32[2,2,2,2,2,2,2,2,8,640]{9,8,7,6,5,4,3,2,1,0:T(8,128)}, f32[2,2,2,2,2,2,2,2,8,640]{9,8,7,6,5,4,3,2,1,0:T(8,128)}, u32[]{:S(2)}, u32[]{:S(2)}) collective-permute-start(f32[2,2,2,2,2,2,2,2,8,640]{9,8,7,6,5,4,3,2,1,0:T(8,128)} %get-tuple-element.64), channel_id=1, source_target_pairs={{0,16},{16,0},{4,20},{20,4},{8,28},{24,12},{12,24},{28,8},{1,17},{... | collective-permute-start | bytes 15728648 | tf_op jit(solution)/shard_map/ppermute | solution.py:257
  60.6 9.4 %shard_map.95 = (f32[2,2,2,2,2,2,2,2,8,640]{9,8,7,6,5,4,3,2,1,0:T(8,128)S(1)}, f32[2,2,2,2,2,2,2,2,8,640]{9,8,7,6,5,4,3,2,1,0:T(8,128)}) custom-call(s32[5]{0:T(128)S(1)} %stack.92.refs_0_.where_ref, bf16[256,256]{1,0:T(8,128)(2,1)S(1)} %maximum_maximum_fusion.refs_1_.wq_ref, bf16[32,32]{1,0:T(8,128)(2,1)S(1)} %reshape.653.wk_ref.refs_2_, ...), custom_call_target="tpu_custom_call" | custom-call | flops 2147483648 | bytes 49416192 | tf_op jit(solution)/shard_map/pallas_call | solution.py:140
  70.0 2.3 copy-done
  72.2 2.7 %collective-permute-start.5 = (f32[2,2,2,2,2,2,2,2,8,640]{9,8,7,6,5,4,3,2,1,0:T(8,128)}, f32[2,2,2,2,2,2,2,2,8,640]{9,8,7,6,5,4,3,2,1,0:T(8,128)}, u32[]{:S(2)}, u32[]{:S(2)}) collective-permute-start(f32[2,2,2,2,2,2,2,2,8,640]{9,8,7,6,5,4,3,2,1,0:T(8,128)} %get-tuple-element.63), channel_id=1, source_target_pairs={{0,32},{32,0},{64,96},{96,64},{8,104},{40,72},{72,40},{104,8},{1,3... | collective-permute-start | bytes 15728648 | tf_op jit(solution)/shard_map/ppermute | solution.py:257
  75.1 4.4 %mul.351 = f32[2,2,2,8,32,8,32]{6,5,4,3,2,1,0:T(8,128)} broadcast(f32[2,2,2,32,32]{4,3,2,1,0:T(8,128)S(1)} %copy.51), dimensions={0,1,2,4,6} | broadcast | bytes 2129920 | tf_op jit(solution)/shard_map/mul | solution.py:270
  79.4 7.1 %mul.352 = f32[2,2,2,256,256]{4,3,2,1,0:T(8,128)} reshape(f32[2,2,2,8,32,8,32]{6,5,4,3,2,1,0:T(8,128)} %mul.351) | data formatting | bytes 4194304 | tf_op jit(solution)/shard_map/mul | solution.py:270
  86.8 0.6 copy.53
  87.5 0.6 reshape.654.left_ref
  88.1 1.9 broadcast_multiply_fusion.right_ref
  90.0 23.2 %collective-permute-done.3 = f32[2,2,2,2,8,2,2,8,384]{8,7,6,5,4,3,2,1,0:T(8,128)} collective-permute-done((f32[2,2,2,2,8,2,2,8,384]{8,7,6,5,4,3,2,1,0:T(8,128)}, f32[2,2,2,2,8,2,2,8,384]{8,7,6,5,4,3,2,1,0:T(8,128)}, u32[]{:S(2)}, u32[]{:S(2)}) %collective-permute-start.3) | collective-permute-done | bytes 6291488 | tf_op jit(solution)/shard_map/ppermute | solution.py:257
  113.3 3.5 %add_bitcast_fusion = f32[2,2,2,8,2,2,8,384]{7,6,5,4,3,2,1,0:T(8,128)S(1)} fusion(f32[2,2,2,2,8,2,2,8,384]{8,7,6,5,4,3,2,1,0:T(8,128)} %collective-permute-done.3, f32[2,2,2,2,8,2,2,8,384]{8,7,6,5,4,3,2,1,0:T(8,128)} %get-tuple-element.61), kind=kLoop, calls=%fused_computation.2 | loop fusion | flops 786432 | bytes 9437184 | tf_op jit(solution)/shard_map/add | solution.py:395
  116.8 0.9 collective-permute-done.6
  117.7 2.3 %add_bitcast_fusion.2 = f32[2,2,2,2,2,2,2,8,640]{8,7,6,5,4,3,2,1,0:T(8,128)S(1)} fusion(f32[2,2,2,2,2,2,2,2,8,640]{9,8,7,6,5,4,3,2,1,0:T(8,128)} %collective-permute-done.6, f32[2,2,2,2,2,2,2,2,8,640]{9,8,7,6,5,4,3,2,1,0:T(8,128)S(1)} %bitcast.282), kind=kLoop, calls=%fused_computation.6 | loop fusion | flops 655360 | bytes 7864320 | tf_op jit(solution)/shard_map/add | solution.py:395
  120.0 0.4 collective-permute-start.8
  120.5 2.5 %slice_add_fusion = f32[1,2,2,2,8,2,2,8,384]{8,7,6,5,4,3,2,1,0:T(8,128)S(1)} fusion(f32[2,2,2,2,8,2,2,8,384]{8,7,6,5,4,3,2,1,0:T(8,128)} %collective-permute-done.3, f32[2,2,2,2,8,2,2,8,384]{8,7,6,5,4,3,2,1,0:T(8,128)S(1)} %bitcast.293), kind=kLoop, calls=%fused_computation.1 | loop fusion | flops 786432 | bytes 9437184 | tf_op jit(solution)/shard_map/add | solution.py:398
  123.0 9.6 %collective-permute-done.5 = f32[2,2,2,2,2,2,2,2,8,640]{9,8,7,6,5,4,3,2,1,0:T(8,128)} collective-permute-done((f32[2,2,2,2,2,2,2,2,8,640]{9,8,7,6,5,4,3,2,1,0:T(8,128)}, f32[2,2,2,2,2,2,2,2,8,640]{9,8,7,6,5,4,3,2,1,0:T(8,128)}, u32[]{:S(2)}, u32[]{:S(2)}) %collective-permute-start.5) | collective-permute-done | bytes 5242912 | tf_op jit(solution)/shard_map/ppermute | solution.py:257
  132.6 3.6 %add_bitcast_fusion.1 = f32[2,2,2,2,2,2,2,8,640]{8,7,6,5,4,3,2,1,0:T(8,128)} fusion(f32[2,2,2,2,2,2,2,2,8,640]{9,8,7,6,5,4,3,2,1,0:T(8,128)} %collective-permute-done.5, f32[2,2,2,2,2,2,2,2,8,640]{9,8,7,6,5,4,3,2,1,0:T(8,128)S(1)} %bitcast.280), kind=kLoop, calls=%fused_computation.5 | loop fusion | flops 655360 | bytes 7864320 | tf_op jit(solution)/shard_map/add | solution.py:395
  136.3 17.1 %collective-permute-done.4 = f32[2,2,2,8,2,2,8,384]{7,6,5,4,3,2,1,0:T(8,128)S(1)} collective-permute-done((f32[2,2,2,8,2,2,8,384]{7,6,5,4,3,2,1,0:T(8,128)S(1)}, f32[2,2,2,8,2,2,8,384]{7,6,5,4,3,2,1,0:T(8,128)S(1)}, u32[]{:S(2)}, u32[]{:S(2)}) %collective-permute-start.4) | collective-permute-done | bytes 3145760 | tf_op jit(solution)/shard_map/ppermute | solution.py:257
  153.3 0.6 fusion.3
  154.0 1.7 collective-permute-start.7
  155.7 2.1 slice_add_fusion.2
  157.8 1.9 fusion.9
  159.7 2.7 %collective-permute-start.10 = (f32[2,2,2,2,2,2,8,640]{7,6,5,4,3,2,1,0:T(8,128)}, f32[2,2,2,2,2,2,8,640]{7,6,5,4,3,2,1,0:T(8,128)}, u32[]{:S(2)}, u32[]{:S(2)}) collective-permute-start(f32[2,2,2,2,2,2,8,640]{7,6,5,4,3,2,1,0:T(8,128)} %get-tuple-element.93), channel_id=1, source_target_pairs={{0,32},{32,0},{64,96},{96,64},{8,104},{40,72},{72,40},{104,8},{1,3... | collective-permute-start | bytes 3932168 | tf_op jit(solution)/shard_map/ppermute | solution.py:257
  162.5 1.1 copy-done.10
  163.6 3.1 %shard_map.96 = (f32[2,2,2,2,2,2,2,8,384]{8,7,6,5,4,3,2,1,0:T(8,128)S(1)}, f32[2,2,2,2,2,2,2,8,384]{8,7,6,5,4,3,2,1,0:T(8,128)S(1)}) custom-call(s32[5]{0:T(128)S(1)} %stack.92.refs_0_.where_ref, bf16[256,256]{1,0:T(8,128)(2,1)S(1)} %maximum_maximum_fusion.refs_1_.wq_ref, f32[2,2,8,2,2,8,384]{6,5,4,3,2,1,0:T(8,128)S(1)} %get-tuple-element.89.own_ref, ...), custom_call_target="tpu_custom_call" | custom-call | flops 2147483648 | bytes 6422528 | tf_op jit(solution)/shard_map/pallas_call | solution.py:140
  166.8 2.6 %collective-permute-start.9 = (f32[2,2,2,2,2,2,2,8,384]{8,7,6,4,5,3,2,1,0:T(8,128)S(1)}, f32[2,2,2,2,2,2,2,8,384]{8,7,6,4,5,3,2,1,0:T(8,128)S(1)}, u32[]{:S(2)}, u32[]{:S(2)}) collective-permute-start(f32[2,2,2,2,2,2,2,8,384]{8,7,6,4,5,3,2,1,0:T(8,128)S(1)} %copy.55), channel_id=1, source_target_pairs={{0,16},{16,0},{4,20},{20,4},{8,28},{24,12},{12,24},{28,8},{1,17},{... | collective-permute-start | bytes 4718600 | tf_op jit(solution)/shard_map/ppermute | solution.py:257
  169.4 2.1 slice_add_fusion.1
  171.6 2.2 fusion.4
  173.8 3.0 %collective-permute-start.14 = (f32[2,2,2,2,2,2,8,640]{7,6,5,4,3,2,1,0:T(8,128)S(1)}, f32[2,2,2,2,2,2,8,640]{7,6,5,4,3,2,1,0:T(8,128)S(1)}, u32[]{:S(2)}, u32[]{:S(2)}) collective-permute-start(f32[2,2,2,2,2,2,8,640]{7,6,5,4,3,2,1,0:T(8,128)S(1)} %get-tuple-element.92), channel_id=1, source_target_pairs={{0,1},{1,0},{2,3},{3,2},{8,11},{9,10},{10,9},{11,8},{4,5},{5,4},{6... | collective-permute-start | bytes 3932168 | tf_op jit(solution)/shard_map/ppermute | solution.py:257
  176.8 3.0 %collective-permute-done.10 = f32[2,2,2,2,2,2,8,640]{7,6,5,4,3,2,1,0:T(8,128)} collective-permute-done((f32[2,2,2,2,2,2,8,640]{7,6,5,4,3,2,1,0:T(8,128)}, f32[2,2,2,2,2,2,8,640]{7,6,5,4,3,2,1,0:T(8,128)}, u32[]{:S(2)}, u32[]{:S(2)}) %collective-permute-start.10) | collective-permute-done | bytes 1310752 | tf_op jit(solution)/shard_map/ppermute | solution.py:257
  179.7 1.4 fusion.16
  181.2 0.5 collective-permute-start.13
  181.7 5.7 %collective-permute-done.9 = f32[2,2,2,2,2,2,2,8,384]{8,7,6,4,5,3,2,1,0:T(8,128)S(1)} collective-permute-done((f32[2,2,2,2,2,2,2,8,384]{8,7,6,4,5,3,2,1,0:T(8,128)S(1)}, f32[2,2,2,2,2,2,2,8,384]{8,7,6,4,5,3,2,1,0:T(8,128)S(1)}, u32[]{:S(2)}, u32[]{:S(2)}) %collective-permute-start.9) | collective-permute-done | bytes 1572896 | tf_op jit(solution)/shard_map/ppermute | solution.py:257
  187.7 0.4 collective-permute-start.12
  188.0 4.0 %collective-permute-done.14 = f32[2,2,2,2,2,2,8,640]{7,6,5,4,3,2,1,0:T(8,128)S(1)} collective-permute-done((f32[2,2,2,2,2,2,8,640]{7,6,5,4,3,2,1,0:T(8,128)S(1)}, f32[2,2,2,2,2,2,8,640]{7,6,5,4,3,2,1,0:T(8,128)S(1)}, u32[]{:S(2)}, u32[]{:S(2)}) %collective-permute-start.14) | collective-permute-done | bytes 1310752 | tf_op jit(solution)/shard_map/ppermute | solution.py:257
  192.1 1.0 fusion.11
  193.1 0.9 fusion.25
  194.1 4.9 %collective-permute-done.12 = f32[2,2,2,2,2,2,8,384]{7,6,5,3,4,2,1,0:T(8,128)S(1)} collective-permute-done((f32[2,2,2,2,2,2,8,384]{7,6,5,3,4,2,1,0:T(8,128)S(1)}, f32[2,2,2,2,2,2,8,384]{7,6,5,3,4,2,1,0:T(8,128)S(1)}, u32[]{:S(2)}, u32[]{:S(2)}) %collective-permute-start.12) | collective-permute-done | bytes 786464 | tf_op jit(solution)/shard_map/ppermute | solution.py:257
  199.0 1.0 fusion.18
  200.0 3.5 %collective-permute-start.19 = (f32[2,2,2,2,8,640]{5,4,3,2,1,0:T(8,128)}, f32[2,2,2,2,8,640]{5,4,3,2,1,0:T(8,128)S(1)}, u32[]{:S(2)}, u32[]{:S(2)}) collective-permute-start(f32[2,2,2,2,8,640]{5,4,3,2,1,0:T(8,128)} %get-tuple-element.105), channel_id=1, source_target_pairs={{0,1},{1,0},{2,3},{3,2},{8,11},{9,10},{10,9},{11,8},{4,5},{5,4},{6... | collective-permute-start | bytes 983048 | tf_op jit(solution)/shard_map/ppermute | solution.py:257
  203.5 1.1 fusion.21
  204.7 2.6 %collective-permute-start.18 = (f32[2,2,2,2,8,640]{5,4,3,2,1,0:T(8,128)S(1)}, f32[2,2,2,2,8,640]{5,4,3,2,1,0:T(8,128)S(1)}, u32[]{:S(2)}, u32[]{:S(2)}) collective-permute-start(f32[2,2,2,2,8,640]{5,4,3,2,1,0:T(8,128)S(1)} %get-tuple-element.104), channel_id=1, source_target_pairs={{0,16},{16,0},{4,20},{20,4},{8,28},{24,12},{12,24},{28,8},{1,17},{... | collective-permute-start | bytes 983048 | tf_op jit(solution)/shard_map/ppermute | solution.py:257
  207.2 0.9 collective-permute-done.15
  208.1 1.0 fusion.29
  209.4 2.5 %collective-permute-done.18 = f32[2,2,2,2,8,640]{5,4,3,2,1,0:T(8,128)S(1)} collective-permute-done((f32[2,2,2,2,8,640]{5,4,3,2,1,0:T(8,128)S(1)}, f32[2,2,2,2,8,640]{5,4,3,2,1,0:T(8,128)S(1)}, u32[]{:S(2)}, u32[]{:S(2)}) %collective-permute-start.18) | collective-permute-done | bytes 327712 | tf_op jit(solution)/shard_map/ppermute | solution.py:257
  212.0 1.8 collective-permute-done.17
  213.8 1.0 fusion.32
  214.8 1.6 collective-permute-done.21
  216.5 5.7 %collective-permute-start.23 = (f32[2,2,8,640]{3,2,1,0:T(8,128)S(1)}, f32[2,2,8,640]{3,2,1,0:T(8,128)S(1)}, u32[]{:S(2)}, u32[]{:S(2)}) collective-permute-start(f32[2,2,8,640]{3,2,1,0:T(8,128)S(1)} %get-tuple-element.116), channel_id=1, source_target_pairs={{0,8},{8,0},{1,9},{9,1},{2,10},{10,2},{3,11},{11,3},{4,12},{12,4},... | collective-permute-start | bytes 245768 | tf_op jit(solution)/shard_map/ppermute | solution.py:261
  222.4 0.4 collective-permute-start.22
  222.8 0.7 collective-permute-done.24
  223.9 3.1 %shard_map.97 = f32[2,8,4,2,1024]{4,3,2,1,0:T(2,128)} custom-call(f32[2,2,4,8,1024]{4,3,2,1,0:T(8,128)S(1)} %pad_maximum_fusion.sum_ref, f32[2,2,2,256,256]{4,3,2,1,0:T(8,128)S(1)} %broadcast_multiply_fusion.right_ref, f32[2,8,64,64]{3,2,1,0:T(8,128)S(1)} %reshape.654.left_ref), custom_call_target="tpu_custom_call" | custom-call | flops 268435456 | bytes 4194304 | tf_op jit(solution)/shard_map/pallas_call | solution.py:328
  (110 shorter events, 3.4 us)
Async XLA Ops:
  0.7 20.2 %collective-permute-start = (f32[4,64]{1,0:T(4,128)S(1)}, f32[4,64]{1,0:T(4,128)S(1)}, u32[]{:S(2)}, u32[]{:S(2)}) collective-permute-start(f32[4,64]{1,0:T(4,128)S(1)} %add_convert_fusion), channel_id=1, source_target_pairs={{0,8},{8,0},{1,9},{9,1},{2,10},{10,2},{3,11},{11,3},{4,12},{12,4},... | collective-permute-start | bytes 3080 | tf_op jit(solution)/shard_map/ppermute | solution.py:261
  25.3 4.9 %copy-start.7 = (s32[3,16]{1,0:T(4,128)S(1)}, s32[3,16]{1,0:T(4,128)}, u32[]{:S(2)}) copy-start(s32[3,16]{1,0:T(4,128)} %param.10) | copy-start | bytes 580
  25.3 4.9 %copy-start.11 = (s32[16]{0:T(128)S(1)}, s32[16]{0:T(128)}, u32[]{:S(2)}) copy-start(s32[16]{0:T(128)} %param.12) | copy-start | bytes 196
  25.3 4.9 %copy-start.9 = (f32[3,16]{1,0:T(4,128)S(1)}, f32[3,16]{1,0:T(4,128)}, u32[]{:S(2)}) copy-start(f32[3,16]{1,0:T(4,128)} %param.14) | copy-start | bytes 580
  25.3 20.6 %collective-permute-start.1 = (f32[16,2,64,640]{3,2,1,0:T(8,128)}, f32[16,2,64,640]{3,2,1,0:T(8,128)}, u32[]{:S(2)}, u32[]{:S(2)}) collective-permute-start(f32[16,2,64,640]{3,2,1,0:T(8,128)} %shard_map.91), channel_id=1, source_target_pairs={{0,8},{8,0},{1,9},{9,1},{2,10},{10,2},{3,11},{11,3},{4,12},{12,4},... | collective-permute-start | bytes 15728648 | tf_op jit(solution)/shard_map/ppermute | solution.py:261
  29.7 30.8 %collective-permute-start.2 = (f32[16,2,64,640]{3,2,1,0:T(8,128)}, f32[16,2,64,640]{3,2,1,0:T(8,128)}, u32[]{:S(2)}, u32[]{:S(2)}) collective-permute-start(f32[16,2,64,640]{3,2,1,0:T(8,128)} %shard_map.92), channel_id=1, source_target_pairs={{0,8},{8,0},{1,9},{9,1},{2,10},{10,2},{3,11},{11,3},{4,12},{12,4},... | collective-permute-start | bytes 15728648 | tf_op jit(solution)/shard_map/ppermute | solution.py:261
  31.0 13.6 %copy-start.8 = (f32[3,128]{1,0:T(4,128)S(1)}, f32[3,128]{1,0:T(4,128)}, u32[]{:S(2)}) copy-start(f32[3,128]{1,0:T(4,128)} %param.15) | copy-start | bytes 4612
  40.8 72.5 %collective-permute-start.3 = (f32[2,2,2,2,8,2,2,8,384]{8,7,6,5,4,3,2,1,0:T(8,128)}, f32[2,2,2,2,8,2,2,8,384]{8,7,6,5,4,3,2,1,0:T(8,128)}, u32[]{:S(2)}, u32[]{:S(2)}) collective-permute-start(f32[2,2,2,2,8,2,2,8,384]{8,7,6,5,4,3,2,1,0:T(8,128)} %get-tuple-element.55), channel_id=1, source_target_pairs={{0,1},{1,0},{2,3},{3,2},{8,11},{9,10},{10,9},{11,8},{4,5},{5,4},{6... | collective-permute-start | bytes 18874376 | tf_op jit(solution)/shard_map/ppermute | solution.py:257
  55.3 2.3 copy-start.1
  57.6 60.1 %collective-permute-start.6 = (f32[2,2,2,2,2,2,2,2,8,640]{9,8,7,6,5,4,3,2,1,0:T(8,128)}, f32[2,2,2,2,2,2,2,2,8,640]{9,8,7,6,5,4,3,2,1,0:T(8,128)}, u32[]{:S(2)}, u32[]{:S(2)}) collective-permute-start(f32[2,2,2,2,2,2,2,2,8,640]{9,8,7,6,5,4,3,2,1,0:T(8,128)} %get-tuple-element.64), channel_id=1, source_target_pairs={{0,16},{16,0},{4,20},{20,4},{8,28},{24,12},{12,24},{28,8},{1,17},{... | collective-permute-start | bytes 15728648 | tf_op jit(solution)/shard_map/ppermute | solution.py:257
  60.6 14.4 %copy-start.6 = (f32[2,2,32,32]{3,2,1,0:T(8,128)S(1)}, f32[2,2,32,32]{3,2,1,0:T(8,128)}, u32[]{:S(2)}) copy-start(f32[2,2,32,32]{3,2,1,0:T(8,128)} %param.16) | copy-start | bytes 49156
  70.0 2.3 copy-start
  72.2 60.4 %collective-permute-start.5 = (f32[2,2,2,2,2,2,2,2,8,640]{9,8,7,6,5,4,3,2,1,0:T(8,128)}, f32[2,2,2,2,2,2,2,2,8,640]{9,8,7,6,5,4,3,2,1,0:T(8,128)}, u32[]{:S(2)}, u32[]{:S(2)}) collective-permute-start(f32[2,2,2,2,2,2,2,2,8,640]{9,8,7,6,5,4,3,2,1,0:T(8,128)} %get-tuple-element.63), channel_id=1, source_target_pairs={{0,32},{32,0},{64,96},{96,64},{8,104},{40,72},{72,40},{104,8},{1,3... | collective-permute-start | bytes 15728648 | tf_op jit(solution)/shard_map/ppermute | solution.py:257
  79.4 7.1 %copy-start.5 = (f32[2,8,2,32,32]{4,3,2,1,0:T(8,128)S(1)}, f32[2,8,2,32,32]{4,3,2,1,0:T(8,128)}, u32[]{:S(2)}) copy-start(f32[2,8,2,32,32]{4,3,2,1,0:T(8,128)} %param.17) | copy-start | bytes 393220
  88.1 29.7 %slice-start.2 = ((s8[5242880]{0:T(1024)(128)(4,1)}), s8[4194304]{0:T(1024)(128)(4,1)S(1)}, s32[]{:S(2)}) async-start(s8[5242880]{0:T(1024)(128)(4,1)} %bitcast.281), calls=%async_computation.2 | async-start | bytes 8388608
  88.1 32.4 %slice-start.4 = ((s8[6291456]{0:T(1024)(128)(4,1)}), s8[4194304]{0:T(1024)(128)(4,1)S(1)}, s32[]{:S(2)}) async-start(s8[6291456]{0:T(1024)(128)(4,1)} %bitcast.292), calls=%async_computation.4 | async-start | bytes 8388608
  90.0 27.7 %slice-start.3 = ((s8[5242880]{0:T(1024)(128)(4,1)}), s8[1048576]{0:T(1024)(128)(4,1)S(1)}, s32[]{:S(2)}) async-start(s8[5242880]{0:T(1024)(128)(4,1)} %bitcast.281), calls=%async_computation.3 | async-start | bytes 2097152
  90.0 30.5 %slice-start.5 = ((s8[6291456]{0:T(1024)(128)(4,1)}), s8[2097152]{0:T(1024)(128)(4,1)S(1)}, s32[]{:S(2)}) async-start(s8[6291456]{0:T(1024)(128)(4,1)} %bitcast.292), calls=%async_computation.5 | async-start | bytes 4194304
  116.7 36.6 %collective-permute-start.4 = (f32[2,2,2,8,2,2,8,384]{7,6,5,4,3,2,1,0:T(8,128)S(1)}, f32[2,2,2,8,2,2,8,384]{7,6,5,4,3,2,1,0:T(8,128)S(1)}, u32[]{:S(2)}, u32[]{:S(2)}) collective-permute-start(f32[2,2,2,8,2,2,8,384]{7,6,5,4,3,2,1,0:T(8,128)S(1)} %add_bitcast_fusion), channel_id=1, source_target_pairs={{0,3},{1,2},{2,1},{3,0},{8,9},{9,8},{10,11},{11,10},{4,7},{5,6},{6... | collective-permute-start | bytes 9437192 | tf_op jit(solution)/shard_map/ppermute | solution.py:257
  117.7 14.9 %slice-start = ((s8[5242880]{0:T(1024)(128)(4,1)}), s8[4194304]{0:T(1024)(128)(4,1)S(1)}, s32[]{:S(2)}) async-start(s8[5242880]{0:T(1024)(128)(4,1)} %bitcast.279), calls=%async_computation | async-start | bytes 8388608
  120.0 12.6 %slice-start.1 = ((s8[5242880]{0:T(1024)(128)(4,1)}), s8[1048576]{0:T(1024)(128)(4,1)S(1)}, s32[]{:S(2)}) async-start(s8[5242880]{0:T(1024)(128)(4,1)} %bitcast.279), calls=%async_computation.1 | async-start | bytes 2097152
  120.0 37.7 %collective-permute-start.8 = (f32[2,2,2,2,2,2,2,8,640]{8,7,6,5,4,3,2,1,0:T(8,128)S(1)}, f32[2,2,2,2,2,2,2,8,640]{8,7,6,5,4,3,2,1,0:T(8,128)S(1)}, u32[]{:S(2)}, u32[]{:S(2)}) collective-permute-start(f32[2,2,2,2,2,2,2,8,640]{8,7,6,5,4,3,2,1,0:T(8,128)S(1)} %add_bitcast_fusion.2), channel_id=1, source_target_pairs={{0,20},{16,4},{4,16},{20,0},{8,24},{24,8},{12,28},{28,12},{1,21},{... | collective-permute-start | bytes 7864328 | tf_op jit(solution)/shard_map/ppermute | solution.py:257
  136.2 35.3 %collective-permute-start.11 = (f32[2,2,2,2,2,2,2,8,640]{8,7,6,5,4,3,2,1,0:T(8,128)}, f32[2,2,2,2,2,2,2,8,640]{8,7,6,5,4,3,2,1,0:T(8,128)}, u32[]{:S(2)}, u32[]{:S(2)}) collective-permute-start(f32[2,2,2,2,2,2,2,8,640]{8,7,6,5,4,3,2,1,0:T(8,128)} %add_bitcast_fusion.1), channel_id=1, source_target_pairs={{0,96},{32,64},{64,32},{96,0},{8,40},{40,8},{72,104},{104,72},{1,9... | collective-permute-start | bytes 7864328 | tf_op jit(solution)/shard_map/ppermute | solution.py:257
  154.0 8.5 %collective-permute-start.7 = (f32[2,2,8,2,2,8,384]{6,5,4,3,2,1,0:T(8,128)S(1)}, f32[2,2,8,2,2,8,384]{6,5,4,3,2,1,0:T(8,128)S(1)}, u32[]{:S(2)}, u32[]{:S(2)}) collective-permute-start(f32[2,2,8,2,2,8,384]{6,5,4,3,2,1,0:T(8,128)S(1)} %get-tuple-element.90), channel_id=1, source_target_pairs={{0,8},{8,0},{1,9},{9,1},{2,10},{10,2},{3,11},{11,3},{4,12},{12,4},... | collective-permute-start | bytes 4718600 | tf_op jit(solution)/shard_map/ppermute | solution.py:261
  159.7 20.0 %collective-permute-start.10 = (f32[2,2,2,2,2,2,8,640]{7,6,5,4,3,2,1,0:T(8,128)}, f32[2,2,2,2,2,2,8,640]{7,6,5,4,3,2,1,0:T(8,128)}, u32[]{:S(2)}, u32[]{:S(2)}) collective-permute-start(f32[2,2,2,2,2,2,8,640]{7,6,5,4,3,2,1,0:T(8,128)} %get-tuple-element.93), channel_id=1, source_target_pairs={{0,32},{32,0},{64,96},{96,64},{8,104},{40,72},{72,40},{104,8},{1,3... | collective-permute-start | bytes 3932168 | tf_op jit(solution)/shard_map/ppermute | solution.py:257
  162.5 1.1 copy-start.10
  166.8 20.6 %collective-permute-start.9 = (f32[2,2,2,2,2,2,2,8,384]{8,7,6,4,5,3,2,1,0:T(8,128)S(1)}, f32[2,2,2,2,2,2,2,8,384]{8,7,6,4,5,3,2,1,0:T(8,128)S(1)}, u32[]{:S(2)}, u32[]{:S(2)}) collective-permute-start(f32[2,2,2,2,2,2,2,8,384]{8,7,6,4,5,3,2,1,0:T(8,128)S(1)} %copy.55), channel_id=1, source_target_pairs={{0,16},{16,0},{4,20},{20,4},{8,28},{24,12},{12,24},{28,8},{1,17},{... | collective-permute-start | bytes 4718600 | tf_op jit(solution)/shard_map/ppermute | solution.py:257
  171.6 8.2 %copy-start.2 = (f32[1,2,2,2,2,2,2,8,640]{8,7,6,5,4,3,2,1,0:T(8,128)S(1)}, f32[1,2,2,2,2,2,2,8,640]{8,7,6,5,4,3,2,1,0:T(8,128)}, u32[]{:S(2)}) copy-start(f32[1,2,2,2,2,2,2,8,640]{8,7,6,5,4,3,2,1,0:T(8,128)} %get-tuple-element.94) | copy-start | bytes 3932164
  173.8 18.3 %collective-permute-start.14 = (f32[2,2,2,2,2,2,8,640]{7,6,5,4,3,2,1,0:T(8,128)S(1)}, f32[2,2,2,2,2,2,8,640]{7,6,5,4,3,2,1,0:T(8,128)S(1)}, u32[]{:S(2)}, u32[]{:S(2)}) collective-permute-start(f32[2,2,2,2,2,2,8,640]{7,6,5,4,3,2,1,0:T(8,128)S(1)} %get-tuple-element.92), channel_id=1, source_target_pairs={{0,1},{1,0},{2,3},{3,2},{8,11},{9,10},{10,9},{11,8},{4,5},{5,4},{6... | collective-permute-start | bytes 3932168 | tf_op jit(solution)/shard_map/ppermute | solution.py:257
  181.2 11.9 %collective-permute-start.13 = (f32[2,2,2,2,2,8,640]{6,5,4,3,2,1,0:T(8,128)S(1)}, f32[2,2,2,2,2,8,640]{6,5,4,3,2,1,0:T(8,128)S(1)}, u32[]{:S(2)}, u32[]{:S(2)}) collective-permute-start(f32[2,2,2,2,2,8,640]{6,5,4,3,2,1,0:T(8,128)S(1)} %get-tuple-element.99), channel_id=1, source_target_pairs={{0,96},{32,64},{64,32},{96,0},{8,40},{40,8},{72,104},{104,72},{1,9... | collective-permute-start | bytes 1966088 | tf_op jit(solution)/shard_map/ppermute | solution.py:257
  187.7 11.3 %collective-permute-start.12 = (f32[2,2,2,2,2,2,8,384]{7,6,5,3,4,2,1,0:T(8,128)S(1)}, f32[2,2,2,2,2,2,8,384]{7,6,5,3,4,2,1,0:T(8,128)S(1)}, u32[]{:S(2)}, u32[]{:S(2)}) collective-permute-start(f32[2,2,2,2,2,2,8,384]{7,6,5,3,4,2,1,0:T(8,128)S(1)} %get-tuple-element.96), channel_id=1, source_target_pairs={{0,20},{16,4},{4,16},{20,0},{8,24},{24,8},{12,28},{28,12},{1,21},{... | collective-permute-start | bytes 2359304 | tf_op jit(solution)/shard_map/ppermute | solution.py:257
  193.1 10.4 %collective-permute-start.16 = (f32[2,2,2,2,2,8,640]{6,5,4,3,2,1,0:T(8,128)}, f32[2,2,2,2,2,8,640]{6,5,4,3,2,1,0:T(8,128)}, u32[]{:S(2)}, u32[]{:S(2)}) collective-permute-start(f32[2,2,2,2,2,8,640]{6,5,4,3,2,1,0:T(8,128)} %get-tuple-element.98), channel_id=1, source_target_pairs={{0,3},{1,2},{2,1},{3,0},{8,9},{9,8},{10,11},{11,10},{4,7},{5,6},{6... | collective-permute-start | bytes 1966088 | tf_op jit(solution)/shard_map/ppermute | solution.py:257
  200.0 8.2 %collective-permute-start.15 = (f32[2,2,2,2,2,8,384]{6,5,4,2,3,1,0:T(8,128)}, f32[2,2,2,2,2,8,384]{6,5,4,2,3,1,0:T(8,128)}, u32[]{:S(2)}, u32[]{:S(2)}) collective-permute-start(f32[2,2,2,2,2,8,384]{6,5,4,2,3,1,0:T(8,128)} %get-tuple-element.101), channel_id=1, source_target_pairs={{0,32},{32,0},{64,96},{96,64},{8,104},{40,72},{72,40},{104,8},{1,3... | collective-permute-start | bytes 1179656 | tf_op jit(solution)/shard_map/ppermute | solution.py:257
  200.0 9.3 %copy-start.4 = (f32[1,2,2,2,2,8,640]{6,5,4,3,2,1,0:T(8,128)S(1)}, f32[1,2,2,2,2,8,640]{6,5,4,3,2,1,0:T(8,128)}, u32[]{:S(2)}) copy-start(f32[1,2,2,2,2,8,640]{6,5,4,3,2,1,0:T(8,128)} %get-tuple-element.106) | copy-start | bytes 983044
  200.0 13.8 %copy-start.3 = (f32[1,2,2,2,2,2,8,384]{7,6,5,3,4,2,1,0:T(8,128)S(1)}, f32[1,2,2,2,2,2,8,384]{7,6,5,3,4,2,1,0:T(8,128)}, u32[]{:S(2)}) copy-start(f32[1,2,2,2,2,2,8,384]{7,6,5,3,4,2,1,0:T(8,128)} %get-tuple-element.102) | copy-start | bytes 1179652
  200.0 9.3 %collective-permute-start.19 = (f32[2,2,2,2,8,640]{5,4,3,2,1,0:T(8,128)}, f32[2,2,2,2,8,640]{5,4,3,2,1,0:T(8,128)S(1)}, u32[]{:S(2)}, u32[]{:S(2)}) collective-permute-start(f32[2,2,2,2,8,640]{5,4,3,2,1,0:T(8,128)} %get-tuple-element.105), channel_id=1, source_target_pairs={{0,1},{1,0},{2,3},{3,2},{8,11},{9,10},{10,9},{11,8},{4,5},{5,4},{6... | collective-permute-start | bytes 983048 | tf_op jit(solution)/shard_map/ppermute | solution.py:257
  204.7 7.2 %collective-permute-start.18 = (f32[2,2,2,2,8,640]{5,4,3,2,1,0:T(8,128)S(1)}, f32[2,2,2,2,8,640]{5,4,3,2,1,0:T(8,128)S(1)}, u32[]{:S(2)}, u32[]{:S(2)}) collective-permute-start(f32[2,2,2,2,8,640]{5,4,3,2,1,0:T(8,128)S(1)} %get-tuple-element.104), channel_id=1, source_target_pairs={{0,16},{16,0},{4,20},{20,4},{8,28},{24,12},{12,24},{28,8},{1,17},{... | collective-permute-start | bytes 983048 | tf_op jit(solution)/shard_map/ppermute | solution.py:257
  209.2 4.6 %collective-permute-start.17 = (f32[2,2,2,2,8,384]{5,4,3,1,2,0:T(8,128)S(1)}, f32[2,2,2,2,8,384]{5,4,3,1,2,0:T(8,128)S(1)}, u32[]{:S(2)}, u32[]{:S(2)}) collective-permute-start(f32[2,2,2,2,8,384]{5,4,3,1,2,0:T(8,128)S(1)} %fusion.29), channel_id=1, source_target_pairs={{0,96},{32,64},{64,32},{96,0},{8,40},{40,8},{72,104},{104,72},{1,9... | collective-permute-start | bytes 589832 | tf_op jit(solution)/shard_map/ppermute | solution.py:257
  209.3 5.5 %collective-permute-start.20 = (f32[2,2,2,8,640]{4,3,2,1,0:T(8,128)S(1)}, f32[2,2,2,8,640]{4,3,2,1,0:T(8,128)S(1)}, u32[]{:S(2)}, u32[]{:S(2)}) collective-permute-start(f32[2,2,2,8,640]{4,3,2,1,0:T(8,128)S(1)} %fusion.40), channel_id=1, source_target_pairs={{0,3},{1,2},{2,1},{3,0},{8,9},{9,8},{10,11},{11,10},{4,7},{5,6},{6... | collective-permute-start | bytes 491528 | tf_op jit(solution)/shard_map/ppermute | solution.py:257
  211.9 4.5 %collective-permute-start.21 = (f32[2,2,2,8,640]{4,3,2,1,0:T(8,128)S(1)}, f32[2,2,2,8,640]{4,3,2,1,0:T(8,128)S(1)}, u32[]{:S(2)}, u32[]{:S(2)}) collective-permute-start(f32[2,2,2,8,640]{4,3,2,1,0:T(8,128)S(1)} %fusion.42), channel_id=1, source_target_pairs={{0,20},{16,4},{4,16},{20,0},{8,24},{24,8},{12,28},{28,12},{1,21},{... | collective-permute-start | bytes 491528 | tf_op jit(solution)/shard_map/ppermute | solution.py:257
  216.5 7.0 %collective-permute-start.23 = (f32[2,2,8,640]{3,2,1,0:T(8,128)S(1)}, f32[2,2,8,640]{3,2,1,0:T(8,128)S(1)}, u32[]{:S(2)}, u32[]{:S(2)}) collective-permute-start(f32[2,2,8,640]{3,2,1,0:T(8,128)S(1)} %get-tuple-element.116), channel_id=1, source_target_pairs={{0,8},{8,0},{1,9},{9,1},{2,10},{10,2},{3,11},{11,3},{4,12},{12,4},... | collective-permute-start | bytes 245768 | tf_op jit(solution)/shard_map/ppermute | solution.py:261
  222.3 1.3 collective-permute-start.24
  222.4 1.4 collective-permute-start.22

commit v5 on v4

--- a/solution.py
+++ b/solution.py
@@ -135,7 +135,7 @@
                 (keep_ref, send_ref)[xf][xs, yf, ys, other, i, 0] = summed_ref[h, i, :, g]
 
 
-def kernel_call(kernel, where, inputs, in_specs, count, out, block, place, grid, scratch):
+def kernel_call(kernel, where, inputs, in_specs, count, out, block, place, grid, scratch, vmem=48):
     read = sum(v.size * v.dtype.itemsize for v in inputs)
     return pl.pallas_call(
         kernel,
@@ -147,7 +147,7 @@
             scratch_shapes=scratch,
         ),
         out_shape=[jax.ShapeDtypeStruct(out, jnp.float32)] * count,
-        compiler_params=pltpu.CompilerParams(vmem_limit_bytes=48 * 1024 * 1024),
+        compiler_params=pltpu.CompilerParams(vmem_limit_bytes=vmem * 1024 * 1024),
         cost_estimate=pl.CostEstimate(
             flops=2**31, bytes_accessed=read + 4 * count * math.prod(out), transcendentals=0
         ),
@@ -239,6 +239,7 @@
             pltpu.VMEM((2, 256, 256), jnp.bfloat16),
             pltpu.VMEM((8, 32, 256), jnp.bfloat16),
         ],
+        vmem=57,
     )
 
 

time: 228 us -> 228 us (level)
  local copies, waits for them, and re-layouts: 38.3 us -> 33.9 us
  Pallas kernels: 43.4 us -> 46.4 us
    unnamed x37 -> x43, local copies, waits for them, and re-layouts: 24.4 us -> 19.9 us
    pallas_call x6, Pallas kernels: 40.3 us -> 43.2 us  [kernel_call(): pl.pallas_call(kernel, grid_spec=pltpu.PrefetchScalarGridSpec(num_scalar_...]
  transfers between devices with their start and end apart: 25 -> 25, of which waited for: 14 -> 14; matrix products, arithmetic and copies ran while one was open for 29% -> 29% of each run, Pallas kernels for 16% -> 17%
where the time goes in v5:
time: 228 us; the launch traced here: 227 us
  waiting for transfers between devices  76.6 us (34%)
  Pallas kernels  46.4 us (20%)
  starting transfers between devices  35 us (15%)
  other arithmetic  34.6 us (15%)
  local copies, waits for them, and re-layouts  33.9 us (15%)
    ppermute x18, waiting for transfers between devices, exchange(): return lax.ppermute(value, names, pairs)  75.7 us
    pallas_call x6, Pallas kernels, kernel_call(): pl.pallas_call(kernel, grid_spec=pltpu.PrefetchScalarGridSpec(num_scalar_...  43.2 us
    ppermute x18, starting transfers between devices, exchange(): return lax.ppermute(value, names, pairs)  24.9 us
    unnamed x43, local copies, waits for them, and re-layouts  19.9 us
    add x10, other arithmetic, body(): latest = send[part] = keep[part][1] + arrived[part][1]  16.3 us
    mul x4, local copies, waits for them, and re-layouts, rotation_tables(): right = right * jnp.eye(8, dtype=jnp.float32)[:, None, :, None]  11.9 us
    ppermute x7, starting transfers between devices, swap(): return lax.ppermute(value, 'c', [(0, 1), (1, 0)])  10.1 us
    add x3, other arithmetic, body(): keep[part] = held[0] + came[0]  6.71 us
  transfers between devices with their start and end apart: 25, of which 14 were waited for; matrix products, arithmetic and copies ran while one was open for 29% of the time, Pallas kernels for 17%

profile of v5, /device:TPU:1, one launch (start us, length us, event | category | flops | bytes accessed | tf_op | source)
XLA Modules:
  0.0 227.1 jit_solution(5771908372057448217)
XLA Ops:
  0.0 0.7 add_convert_fusion
  0.7 1.5 collective-permute-start
  2.2 18.6 %copy.67 = bf16[16,64,4,2,1024]{4,1,3,2,0:T(8,128)(2,1)} copy(bf16[16,64,4,2,1024]{4,3,2,1,0:T(2,128)(2,1)} %param.9) | data formatting | bytes 33554432 | tf_op args[0]
  20.9 4.4 %shard_map.91 = f32[16,2,64,640]{3,2,1,0:T(8,128)} custom-call(s32[5]{0:T(128)S(1)} %stack.92.refs_0_.where_ref, bf16[16,4,2,64,1024]{4,3,2,1,0:T(8,128)(2,1)} %bitcast.279, bf16[16,4,2,64,1024]{4,3,2,1,0:T(8,128)(2,1)} %bitcast.280), custom_call_target="tpu_custom_call" | custom-call | flops 2147483648 | bytes 38797312 | tf_op jit(solution)/shard_map/pallas_call | solution.py:140
  25.5 4.3 %shard_map.92 = f32[16,2,64,640]{3,2,1,0:T(8,128)} custom-call(s32[5]{0:T(128)S(1)} %stack.92.refs_0_.where_ref, bf16[16,4,2,64,1024]{4,3,2,1,0:T(8,128)(2,1)} %bitcast.281, bf16[16,4,2,64,1024]{4,3,2,1,0:T(8,128)(2,1)} %bitcast.282), custom_call_target="tpu_custom_call" | custom-call | flops 2147483648 | bytes 38797312 | tf_op jit(solution)/shard_map/pallas_call | solution.py:140
  29.8 0.5 collective-permute-start.2
  30.6 0.3 copy.49
  31.1 9.7 %shard_map.93 = (f32[2,2,2,2,8,2,2,8,384]{8,7,6,5,4,3,2,1,0:T(8,128)}, f32[2,2,2,2,8,2,2,8,384]{8,7,6,5,4,3,2,1,0:T(8,128)}) custom-call(s32[5]{0:T(128)S(1)} %stack.92.refs_0_.where_ref, bf16[32,32]{1,0:T(8,128)(2,1)S(1)} %reshape.653.wk_ref.refs_2_, bf16[16,4,2,64,1024]{4,3,2,1,0:T(8,128)(2,1)} %bitcast.283), custom_call_target="tpu_custom_call" | custom-call | flops 2147483648 | bytes 29362176 | tf_op jit(solution)/shard_map/pallas_call | solution.py:140
  40.8 3.8 %collective-permute-start.3 = (f32[2,2,2,2,8,2,2,8,384]{8,7,6,5,4,3,2,1,0:T(8,128)}, f32[2,2,2,2,8,2,2,8,384]{8,7,6,5,4,3,2,1,0:T(8,128)}, u32[]{:S(2)}, u32[]{:S(2)}) collective-permute-start(f32[2,2,2,2,8,2,2,8,384]{8,7,6,5,4,3,2,1,0:T(8,128)} %get-tuple-element.55), channel_id=1, source_target_pairs={{0,1},{1,0},{2,3},{3,2},{8,11},{9,10},{10,9},{11,8},{4,5},{5,4},{6... | collective-permute-start | bytes 18874376 | tf_op jit(solution)/shard_map/ppermute | solution.py:258
  44.7 0.6 fusion.47
  45.2 0.6 multiply_convert_fusion.2
  45.8 0.8 maximum_maximum_fusion.refs_1_.wq_ref
  46.6 10.6 %shard_map.94 = (f32[2,2,2,2,2,2,2,2,8,640]{9,8,7,6,5,4,3,2,1,0:T(8,128)}, f32[2,2,2,2,2,2,2,2,8,640]{9,8,7,6,5,4,3,2,1,0:T(8,128)}) custom-call(s32[5]{0:T(128)} %copy-done.2, bf16[256,256]{1,0:T(8,128)(2,1)} %maximum_maximum_fusion.refs_1_.wq_ref, bf16[32,32]{1,0:T(8,128)(2,1)} %copy-done.1, bf16[16,4,2,64,1024]{4,3,2,1,0:T(8,128)(2,1)} %bitcast.284, ...), custom_call_target="tpu_custom_call" | custom-call | flops 2147483648 | bytes 49416192 | tf_op jit(solution)/shard_map/pallas_call | solution.py:140
  57.2 2.5 %collective-permute-start.6 = (f32[2,2,2,2,2,2,2,2,8,640]{9,8,7,6,5,4,3,2,1,0:T(8,128)}, f32[2,2,2,2,2,2,2,2,8,640]{9,8,7,6,5,4,3,2,1,0:T(8,128)}, u32[]{:S(2)}, u32[]{:S(2)}) collective-permute-start(f32[2,2,2,2,2,2,2,2,8,640]{9,8,7,6,5,4,3,2,1,0:T(8,128)} %get-tuple-element.64), channel_id=1, source_target_pairs={{0,16},{16,0},{4,20},{20,4},{8,28},{24,12},{12,24},{28,8},{1,17},{... | collective-permute-start | bytes 15728648 | tf_op jit(solution)/shard_map/ppermute | solution.py:258
  59.9 0.3 mul.354
  60.2 10.8 %shard_map.95 = (f32[2,2,2,2,2,2,2,2,8,640]{9,8,7,6,5,4,3,2,1,0:T(8,128)}, f32[2,2,2,2,2,2,2,2,8,640]{9,8,7,6,5,4,3,2,1,0:T(8,128)}) custom-call(s32[5]{0:T(128)} %copy-done.2, bf16[256,256]{1,0:T(8,128)(2,1)} %maximum_maximum_fusion.refs_1_.wq_ref, bf16[32,32]{1,0:T(8,128)(2,1)} %copy-done.1, bf16[16,4,2,64,1024]{4,3,2,1,0:T(8,128)(2,1)} %bitcast.286, ...), custom_call_target="tpu_custom_call" | custom-call | flops 2147483648 | bytes 49416192 | tf_op jit(solution)/shard_map/pallas_call | solution.py:140
  71.0 2.7 %collective-permute-start.5 = (f32[2,2,2,2,2,2,2,2,8,640]{9,8,7,6,5,4,3,2,1,0:T(8,128)}, f32[2,2,2,2,2,2,2,2,8,640]{9,8,7,6,5,4,3,2,1,0:T(8,128)}, u32[]{:S(2)}, u32[]{:S(2)}) collective-permute-start(f32[2,2,2,2,2,2,2,2,8,640]{9,8,7,6,5,4,3,2,1,0:T(8,128)} %get-tuple-element.63), channel_id=1, source_target_pairs={{0,32},{32,0},{64,96},{96,64},{8,104},{40,72},{72,40},{104,8},{1,3... | collective-permute-start | bytes 15728648 | tf_op jit(solution)/shard_map/ppermute | solution.py:258
  73.8 4.4 %mul.351 = f32[2,2,2,8,32,8,32]{6,5,4,3,2,1,0:T(8,128)} broadcast(f32[2,2,2,32,32]{4,3,2,1,0:T(8,128)S(1)} %copy.51), dimensions={0,1,2,4,6} | broadcast | bytes 2129920 | tf_op jit(solution)/shard_map/mul | solution.py:271
  78.2 7.1 %mul.352 = f32[2,2,2,256,256]{4,3,2,1,0:T(8,128)} reshape(f32[2,2,2,8,32,8,32]{6,5,4,3,2,1,0:T(8,128)} %mul.351) | data formatting | bytes 4194304 | tf_op jit(solution)/shard_map/mul | solution.py:271
  85.7 0.6 copy.53
  86.3 0.6 reshape.654.left_ref
  86.9 2.0 broadcast_multiply_fusion.right_ref
  88.9 24.4 %collective-permute-done.3 = f32[2,2,2,2,8,2,2,8,384]{8,7,6,5,4,3,2,1,0:T(8,128)} collective-permute-done((f32[2,2,2,2,8,2,2,8,384]{8,7,6,5,4,3,2,1,0:T(8,128)}, f32[2,2,2,2,8,2,2,8,384]{8,7,6,5,4,3,2,1,0:T(8,128)}, u32[]{:S(2)}, u32[]{:S(2)}) %collective-permute-start.3) | collective-permute-done | bytes 6291488 | tf_op jit(solution)/shard_map/ppermute | solution.py:258
  113.3 3.5 %add_bitcast_fusion = f32[2,2,2,8,2,2,8,384]{7,6,5,4,3,2,1,0:T(8,128)S(1)} fusion(f32[2,2,2,2,8,2,2,8,384]{8,7,6,5,4,3,2,1,0:T(8,128)} %collective-permute-done.3, f32[2,2,2,2,8,2,2,8,384]{8,7,6,5,4,3,2,1,0:T(8,128)} %get-tuple-element.61), kind=kLoop, calls=%fused_computation.2 | loop fusion | flops 786432 | bytes 9437184 | tf_op jit(solution)/shard_map/add | solution.py:396
  116.9 0.5 collective-permute-done.6
  117.4 3.1 %add_bitcast_fusion.2 = f32[2,2,2,2,2,2,2,8,640]{8,7,6,5,4,3,2,1,0:T(8,128)S(1)} fusion(f32[2,2,2,2,2,2,2,2,8,640]{9,8,7,6,5,4,3,2,1,0:T(8,128)} %collective-permute-done.6, f32[2,2,2,2,2,2,2,2,8,640]{9,8,7,6,5,4,3,2,1,0:T(8,128)} %get-tuple-element.68), kind=kLoop, calls=%fused_computation.6 | loop fusion | flops 655360 | bytes 7864320 | tf_op jit(solution)/shard_map/add | solution.py:396
  120.5 0.8 collective-permute-start.8
  121.3 2.5 %slice_add_fusion = f32[1,2,2,2,8,2,2,8,384]{8,7,6,5,4,3,2,1,0:T(8,128)S(1)} fusion(f32[2,2,2,2,8,2,2,8,384]{8,7,6,5,4,3,2,1,0:T(8,128)} %collective-permute-done.3, f32[2,2,2,2,8,2,2,8,384]{8,7,6,5,4,3,2,1,0:T(8,128)S(1)} %bitcast.289), kind=kLoop, calls=%fused_computation.1 | loop fusion | flops 786432 | bytes 9437184 | tf_op jit(solution)/shard_map/add | solution.py:399
  123.8 7.6 %collective-permute-done.5 = f32[2,2,2,2,2,2,2,2,8,640]{9,8,7,6,5,4,3,2,1,0:T(8,128)} collective-permute-done((f32[2,2,2,2,2,2,2,2,8,640]{9,8,7,6,5,4,3,2,1,0:T(8,128)}, f32[2,2,2,2,2,2,2,2,8,640]{9,8,7,6,5,4,3,2,1,0:T(8,128)}, u32[]{:S(2)}, u32[]{:S(2)}) %collective-permute-start.5) | collective-permute-done | bytes 5242912 | tf_op jit(solution)/shard_map/ppermute | solution.py:258
  131.4 3.8 %add_bitcast_fusion.1 = f32[2,2,2,2,2,2,2,8,640]{8,7,6,5,4,3,2,1,0:T(8,128)} fusion(f32[2,2,2,2,2,2,2,2,8,640]{9,8,7,6,5,4,3,2,1,0:T(8,128)} %collective-permute-done.5, f32[2,2,2,2,2,2,2,2,8,640]{9,8,7,6,5,4,3,2,1,0:T(8,128)S(1)} %bitcast.291), kind=kLoop, calls=%fused_computation.5 | loop fusion | flops 655360 | bytes 7864320 | tf_op jit(solution)/shard_map/add | solution.py:396
  135.2 18.2 %collective-permute-done.4 = f32[2,2,2,8,2,2,8,384]{7,6,5,4,3,2,1,0:T(8,128)S(1)} collective-permute-done((f32[2,2,2,8,2,2,8,384]{7,6,5,4,3,2,1,0:T(8,128)S(1)}, f32[2,2,2,8,2,2,8,384]{7,6,5,4,3,2,1,0:T(8,128)S(1)}, u32[]{:S(2)}, u32[]{:S(2)}) %collective-permute-start.4) | collective-permute-done | bytes 3145760 | tf_op jit(solution)/shard_map/ppermute | solution.py:258
  153.4 0.6 fusion.3
  154.0 1.7 collective-permute-start.7
  155.8 2.1 slice_add_fusion.2
  157.9 1.5 fusion.9
  159.4 2.7 %collective-permute-start.10 = (f32[2,2,2,2,2,2,8,640]{7,6,5,4,3,2,1,0:T(8,128)}, f32[2,2,2,2,2,2,8,640]{7,6,5,4,3,2,1,0:T(8,128)}, u32[]{:S(2)}, u32[]{:S(2)}) collective-permute-start(f32[2,2,2,2,2,2,8,640]{7,6,5,4,3,2,1,0:T(8,128)} %get-tuple-element.93), channel_id=1, source_target_pairs={{0,32},{32,0},{64,96},{96,64},{8,104},{40,72},{72,40},{104,8},{1,3... | collective-permute-start | bytes 3932168 | tf_op jit(solution)/shard_map/ppermute | solution.py:258
  162.2 1.2 copy-done.11
  163.3 3.4 %shard_map.96 = (f32[2,2,2,2,2,2,2,8,384]{8,7,6,5,4,3,2,1,0:T(8,128)S(1)}, f32[2,2,2,2,2,2,2,8,384]{8,7,6,5,4,3,2,1,0:T(8,128)S(1)}) custom-call(s32[5]{0:T(128)S(1)} %copy-done.3, bf16[256,256]{1,0:T(8,128)(2,1)S(1)} %copy-done, f32[2,2,8,2,2,8,384]{6,5,4,3,2,1,0:T(8,128)S(1)} %get-tuple-element.89.own_ref, f32[2,2,8,2,2,8,384]{6,5,4,3,2,1,0:T(8,128)} %copy-done.11), custom_call_target="tpu_custom_call" | custom-call | flops 2147483648 | bytes 6422528 | tf_op jit(solution)/shard_map/pallas_call | solution.py:140
  166.9 2.6 %collective-permute-start.9 = (f32[2,2,2,2,2,2,2,8,384]{8,7,6,4,5,3,2,1,0:T(8,128)S(1)}, f32[2,2,2,2,2,2,2,8,384]{8,7,6,4,5,3,2,1,0:T(8,128)S(1)}, u32[]{:S(2)}, u32[]{:S(2)}) collective-permute-start(f32[2,2,2,2,2,2,2,8,384]{8,7,6,4,5,3,2,1,0:T(8,128)S(1)} %copy.55), channel_id=1, source_target_pairs={{0,16},{16,0},{4,20},{20,4},{8,28},{24,12},{12,24},{28,8},{1,17},{... | collective-permute-start | bytes 4718600 | tf_op jit(solution)/shard_map/ppermute | solution.py:258
  169.4 2.1 slice_add_fusion.1
  171.6 2.1 fusion.4
  173.6 3.0 %collective-permute-start.14 = (f32[2,2,2,2,2,2,8,640]{7,6,5,4,3,2,1,0:T(8,128)S(1)}, f32[2,2,2,2,2,2,8,640]{7,6,5,4,3,2,1,0:T(8,128)S(1)}, u32[]{:S(2)}, u32[]{:S(2)}) collective-permute-start(f32[2,2,2,2,2,2,8,640]{7,6,5,4,3,2,1,0:T(8,128)S(1)} %get-tuple-element.92), channel_id=1, source_target_pairs={{0,1},{1,0},{2,3},{3,2},{8,11},{9,10},{10,9},{11,8},{4,5},{5,4},{6... | collective-permute-start | bytes 3932168 | tf_op jit(solution)/shard_map/ppermute | solution.py:258
  176.7 2.0 collective-permute-done.10
  178.7 1.5 fusion.16
  180.1 0.5 collective-permute-start.13
  180.6 7.1 %collective-permute-done.9 = f32[2,2,2,2,2,2,2,8,384]{8,7,6,4,5,3,2,1,0:T(8,128)S(1)} collective-permute-done((f32[2,2,2,2,2,2,2,8,384]{8,7,6,4,5,3,2,1,0:T(8,128)S(1)}, f32[2,2,2,2,2,2,2,8,384]{8,7,6,4,5,3,2,1,0:T(8,128)S(1)}, u32[]{:S(2)}, u32[]{:S(2)}) %collective-permute-start.9) | collective-permute-done | bytes 1572896 | tf_op jit(solution)/shard_map/ppermute | solution.py:258
  188.1 3.9 %collective-permute-done.14 = f32[2,2,2,2,2,2,8,640]{7,6,5,4,3,2,1,0:T(8,128)S(1)} collective-permute-done((f32[2,2,2,2,2,2,8,640]{7,6,5,4,3,2,1,0:T(8,128)S(1)}, f32[2,2,2,2,2,2,8,640]{7,6,5,4,3,2,1,0:T(8,128)S(1)}, u32[]{:S(2)}, u32[]{:S(2)}) %collective-permute-start.14) | collective-permute-done | bytes 1310752 | tf_op jit(solution)/shard_map/ppermute | solution.py:258
  192.0 1.1 fusion.11
  193.0 0.9 fusion.25
  194.0 5.3 %collective-permute-done.12 = f32[2,2,2,2,2,2,8,384]{7,6,5,3,4,2,1,0:T(8,128)S(1)} collective-permute-done((f32[2,2,2,2,2,2,8,384]{7,6,5,3,4,2,1,0:T(8,128)S(1)}, f32[2,2,2,2,2,2,8,384]{7,6,5,3,4,2,1,0:T(8,128)S(1)}, u32[]{:S(2)}, u32[]{:S(2)}) %collective-permute-start.12) | collective-permute-done | bytes 786464 | tf_op jit(solution)/shard_map/ppermute | solution.py:258
  199.3 1.0 fusion.18
  200.3 3.2 %collective-permute-start.19 = (f32[2,2,2,2,8,640]{5,4,3,2,1,0:T(8,128)}, f32[2,2,2,2,8,640]{5,4,3,2,1,0:T(8,128)S(1)}, u32[]{:S(2)}, u32[]{:S(2)}) collective-permute-start(f32[2,2,2,2,8,640]{5,4,3,2,1,0:T(8,128)} %get-tuple-element.105), channel_id=1, source_target_pairs={{0,1},{1,0},{2,3},{3,2},{8,11},{9,10},{10,9},{11,8},{4,5},{5,4},{6... | collective-permute-start | bytes 983048 | tf_op jit(solution)/shard_map/ppermute | solution.py:258
  203.6 1.1 fusion.21
  204.7 2.6 %collective-permute-start.18 = (f32[2,2,2,2,8,640]{5,4,3,2,1,0:T(8,128)S(1)}, f32[2,2,2,2,8,640]{5,4,3,2,1,0:T(8,128)S(1)}, u32[]{:S(2)}, u32[]{:S(2)}) collective-permute-start(f32[2,2,2,2,8,640]{5,4,3,2,1,0:T(8,128)S(1)} %get-tuple-element.104), channel_id=1, source_target_pairs={{0,16},{16,0},{4,20},{20,4},{8,28},{24,12},{12,24},{28,8},{1,17},{... | collective-permute-start | bytes 983048 | tf_op jit(solution)/shard_map/ppermute | solution.py:258
  207.3 1.2 collective-permute-done.15
  208.5 1.0 fusion.29
  209.7 2.2 collective-permute-done.18
  212.0 2.4 %collective-permute-done.17 = f32[2,2,2,2,8,384]{5,4,3,1,2,0:T(8,128)S(1)} collective-permute-done((f32[2,2,2,2,8,384]{5,4,3,1,2,0:T(8,128)S(1)}, f32[2,2,2,2,8,384]{5,4,3,1,2,0:T(8,128)S(1)}, u32[]{:S(2)}, u32[]{:S(2)}) %collective-permute-start.17) | collective-permute-done | bytes 196640 | tf_op jit(solution)/shard_map/ppermute | solution.py:258
  214.4 1.0 fusion.32
  215.5 1.0 collective-permute-done.21
  216.6 5.8 %collective-permute-start.23 = (f32[2,2,8,640]{3,2,1,0:T(8,128)S(1)}, f32[2,2,8,640]{3,2,1,0:T(8,128)S(1)}, u32[]{:S(2)}, u32[]{:S(2)}) collective-permute-start(f32[2,2,8,640]{3,2,1,0:T(8,128)S(1)} %get-tuple-element.116), channel_id=1, source_target_pairs={{0,8},{8,0},{1,9},{9,1},{2,10},{10,2},{3,11},{11,3},{4,12},{12,4},... | collective-permute-start | bytes 245768 | tf_op jit(solution)/shard_map/ppermute | solution.py:262
  222.4 0.4 collective-permute-start.22
  222.9 0.7 collective-permute-done.24
  223.9 3.1 %shard_map.97 = f32[2,8,4,2,1024]{4,3,2,1,0:T(2,128)} custom-call(f32[2,2,4,8,1024]{4,3,2,1,0:T(8,128)S(1)} %pad_maximum_fusion.sum_ref, f32[2,2,2,256,256]{4,3,2,1,0:T(8,128)S(1)} %broadcast_multiply_fusion.right_ref, f32[2,8,64,64]{3,2,1,0:T(8,128)S(1)} %reshape.654.left_ref), custom_call_target="tpu_custom_call" | custom-call | flops 268435456 | bytes 4194304 | tf_op jit(solution)/shard_map/pallas_call | solution.py:329
  (117 shorter events, 2.8 us)
Async XLA Ops:
  0.7 20.2 %collective-permute-start = (f32[4,64]{1,0:T(4,128)S(1)}, f32[4,64]{1,0:T(4,128)S(1)}, u32[]{:S(2)}, u32[]{:S(2)}) collective-permute-start(f32[4,64]{1,0:T(4,128)S(1)} %add_convert_fusion), channel_id=1, source_target_pairs={{0,8},{8,0},{1,9},{9,1},{2,10},{10,2},{3,11},{11,3},{4,12},{12,4},... | collective-permute-start | bytes 3080 | tf_op jit(solution)/shard_map/ppermute | solution.py:262
  20.9 10.1 %copy-start.2 = (s32[5]{0:T(128)}, s32[5]{0:T(128)S(1)}, u32[]{:S(2)}) copy-start(s32[5]{0:T(128)S(1)} %stack.92.refs_0_.where_ref) | copy-start | bytes 64
  25.3 4.9 %copy-start.8 = (s32[3,16]{1,0:T(4,128)S(1)}, s32[3,16]{1,0:T(4,128)}, u32[]{:S(2)}) copy-start(s32[3,16]{1,0:T(4,128)} %param.10) | copy-start | bytes 580
  25.3 4.9 %copy-start.12 = (s32[16]{0:T(128)S(1)}, s32[16]{0:T(128)}, u32[]{:S(2)}) copy-start(s32[16]{0:T(128)} %param.12) | copy-start | bytes 196
  25.4 4.9 %copy-start.10 = (f32[3,16]{1,0:T(4,128)S(1)}, f32[3,16]{1,0:T(4,128)}, u32[]{:S(2)}) copy-start(f32[3,16]{1,0:T(4,128)} %param.14) | copy-start | bytes 580
  25.4 21.3 %collective-permute-start.1 = (f32[16,2,64,640]{3,2,1,0:T(8,128)}, f32[16,2,64,640]{3,2,1,0:T(8,128)}, u32[]{:S(2)}, u32[]{:S(2)}) collective-permute-start(f32[16,2,64,640]{3,2,1,0:T(8,128)} %shard_map.91), channel_id=1, source_target_pairs={{0,8},{8,0},{1,9},{9,1},{2,10},{10,2},{3,11},{11,3},{4,12},{12,4},... | collective-permute-start | bytes 15728648 | tf_op jit(solution)/shard_map/ppermute | solution.py:262
  29.8 30.4 %collective-permute-start.2 = (f32[16,2,64,640]{3,2,1,0:T(8,128)}, f32[16,2,64,640]{3,2,1,0:T(8,128)}, u32[]{:S(2)}, u32[]{:S(2)}) collective-permute-start(f32[16,2,64,640]{3,2,1,0:T(8,128)} %shard_map.92), channel_id=1, source_target_pairs={{0,8},{8,0},{1,9},{9,1},{2,10},{10,2},{3,11},{11,3},{4,12},{12,4},... | collective-permute-start | bytes 15728648 | tf_op jit(solution)/shard_map/ppermute | solution.py:262
  31.1 9.7 %copy-start.1 = (bf16[32,32]{1,0:T(8,128)(2,1)}, bf16[32,32]{1,0:T(8,128)(2,1)S(1)}, u32[]{:S(2)}) copy-start(bf16[32,32]{1,0:T(8,128)(2,1)S(1)} %reshape.653.wk_ref.refs_2_) | copy-start | bytes 6148
  31.1 13.6 %copy-start.9 = (f32[3,128]{1,0:T(4,128)S(1)}, f32[3,128]{1,0:T(4,128)}, u32[]{:S(2)}) copy-start(f32[3,128]{1,0:T(4,128)} %param.15) | copy-start | bytes 4612
  40.8 72.5 %collective-permute-start.3 = (f32[2,2,2,2,8,2,2,8,384]{8,7,6,5,4,3,2,1,0:T(8,128)}, f32[2,2,2,2,8,2,2,8,384]{8,7,6,5,4,3,2,1,0:T(8,128)}, u32[]{:S(2)}, u32[]{:S(2)}) collective-permute-start(f32[2,2,2,2,8,2,2,8,384]{8,7,6,5,4,3,2,1,0:T(8,128)} %get-tuple-element.55), channel_id=1, source_target_pairs={{0,1},{1,0},{2,3},{3,2},{8,11},{9,10},{10,9},{11,8},{4,5},{5,4},{6... | collective-permute-start | bytes 18874376 | tf_op jit(solution)/shard_map/ppermute | solution.py:258
  57.2 60.1 %collective-permute-start.6 = (f32[2,2,2,2,2,2,2,2,8,640]{9,8,7,6,5,4,3,2,1,0:T(8,128)}, f32[2,2,2,2,2,2,2,2,8,640]{9,8,7,6,5,4,3,2,1,0:T(8,128)}, u32[]{:S(2)}, u32[]{:S(2)}) collective-permute-start(f32[2,2,2,2,2,2,2,2,8,640]{9,8,7,6,5,4,3,2,1,0:T(8,128)} %get-tuple-element.64), channel_id=1, source_target_pairs={{0,16},{16,0},{4,20},{20,4},{8,28},{24,12},{12,24},{28,8},{1,17},{... | collective-permute-start | bytes 15728648 | tf_op jit(solution)/shard_map/ppermute | solution.py:258
  60.2 13.6 %copy-start.7 = (f32[2,2,32,32]{3,2,1,0:T(8,128)S(1)}, f32[2,2,32,32]{3,2,1,0:T(8,128)}, u32[]{:S(2)}) copy-start(f32[2,2,32,32]{3,2,1,0:T(8,128)} %param.16) | copy-start | bytes 49156
  71.0 60.4 %collective-permute-start.5 = (f32[2,2,2,2,2,2,2,2,8,640]{9,8,7,6,5,4,3,2,1,0:T(8,128)}, f32[2,2,2,2,2,2,2,2,8,640]{9,8,7,6,5,4,3,2,1,0:T(8,128)}, u32[]{:S(2)}, u32[]{:S(2)}) collective-permute-start(f32[2,2,2,2,2,2,2,2,8,640]{9,8,7,6,5,4,3,2,1,0:T(8,128)} %get-tuple-element.63), channel_id=1, source_target_pairs={{0,32},{32,0},{64,96},{96,64},{8,104},{40,72},{72,40},{104,8},{1,3... | collective-permute-start | bytes 15728648 | tf_op jit(solution)/shard_map/ppermute | solution.py:258
  78.2 7.1 %copy-start.6 = (f32[2,8,2,32,32]{4,3,2,1,0:T(8,128)S(1)}, f32[2,8,2,32,32]{4,3,2,1,0:T(8,128)}, u32[]{:S(2)}) copy-start(f32[2,8,2,32,32]{4,3,2,1,0:T(8,128)} %param.17) | copy-start | bytes 393220
  86.9 34.4 %slice-start = ((s8[6291456]{0:T(1024)(128)(4,1)}), s8[4194304]{0:T(1024)(128)(4,1)S(1)}, s32[]{:S(2)}) async-start(s8[6291456]{0:T(1024)(128)(4,1)} %bitcast.288), calls=%async_computation | async-start | bytes 8388608
  88.9 32.4 %slice-start.1 = ((s8[6291456]{0:T(1024)(128)(4,1)}), s8[2097152]{0:T(1024)(128)(4,1)S(1)}, s32[]{:S(2)}) async-start(s8[6291456]{0:T(1024)(128)(4,1)} %bitcast.288), calls=%async_computation.1 | async-start | bytes 4194304
  116.8 36.6 %collective-permute-start.4 = (f32[2,2,2,8,2,2,8,384]{7,6,5,4,3,2,1,0:T(8,128)S(1)}, f32[2,2,2,8,2,2,8,384]{7,6,5,4,3,2,1,0:T(8,128)S(1)}, u32[]{:S(2)}, u32[]{:S(2)}) collective-permute-start(f32[2,2,2,8,2,2,8,384]{7,6,5,4,3,2,1,0:T(8,128)S(1)} %add_bitcast_fusion), channel_id=1, source_target_pairs={{0,3},{1,2},{2,1},{3,0},{8,9},{9,8},{10,11},{11,10},{4,7},{5,6},{6... | collective-permute-start | bytes 9437192 | tf_op jit(solution)/shard_map/ppermute | solution.py:258
  117.4 14.0 %slice-start.2 = ((s8[5242880]{0:T(1024)(128)(4,1)}), s8[4194304]{0:T(1024)(128)(4,1)S(1)}, s32[]{:S(2)}) async-start(s8[5242880]{0:T(1024)(128)(4,1)} %bitcast.290), calls=%async_computation.2 | async-start | bytes 8388608
  120.4 10.9 %slice-start.3 = ((s8[5242880]{0:T(1024)(128)(4,1)}), s8[1048576]{0:T(1024)(128)(4,1)S(1)}, s32[]{:S(2)}) async-start(s8[5242880]{0:T(1024)(128)(4,1)} %bitcast.290), calls=%async_computation.3 | async-start | bytes 2097152
  120.5 37.4 %collective-permute-start.8 = (f32[2,2,2,2,2,2,2,8,640]{8,7,6,5,4,3,2,1,0:T(8,128)S(1)}, f32[2,2,2,2,2,2,2,8,640]{8,7,6,5,4,3,2,1,0:T(8,128)S(1)}, u32[]{:S(2)}, u32[]{:S(2)}) collective-permute-start(f32[2,2,2,2,2,2,2,8,640]{8,7,6,5,4,3,2,1,0:T(8,128)S(1)} %add_bitcast_fusion.2), channel_id=1, source_target_pairs={{0,20},{16,4},{4,16},{20,0},{8,24},{24,8},{12,28},{28,12},{1,21},{... | collective-permute-start | bytes 7864328 | tf_op jit(solution)/shard_map/ppermute | solution.py:258
  131.4 24.4 %slice-start.6 = ((s8[5242880]{0:T(1024)(128)(4,1)}), s8[4194304]{0:T(1024)(128)(4,1)S(1)}, s32[]{:S(2)}) async-start(s8[5242880]{0:T(1024)(128)(4,1)} %bitcast.294), calls=%async_computation.6 | async-start | bytes 8388608
  135.2 20.6 %slice-start.7 = ((s8[5242880]{0:T(1024)(128)(4,1)}), s8[1048576]{0:T(1024)(128)(4,1)S(1)}, s32[]{:S(2)}) async-start(s8[5242880]{0:T(1024)(128)(4,1)} %bitcast.294), calls=%async_computation.7 | async-start | bytes 2097152
  135.2 36.4 %collective-permute-start.11 = (f32[2,2,2,2,2,2,2,8,640]{8,7,6,5,4,3,2,1,0:T(8,128)}, f32[2,2,2,2,2,2,2,8,640]{8,7,6,5,4,3,2,1,0:T(8,128)}, u32[]{:S(2)}, u32[]{:S(2)}) collective-permute-start(f32[2,2,2,2,2,2,2,8,640]{8,7,6,5,4,3,2,1,0:T(8,128)} %add_bitcast_fusion.1), channel_id=1, source_target_pairs={{0,96},{32,64},{64,32},{96,0},{8,40},{40,8},{72,104},{104,72},{1,9... | collective-permute-start | bytes 7864328 | tf_op jit(solution)/shard_map/ppermute | solution.py:258
  154.0 8.1 %collective-permute-start.7 = (f32[2,2,8,2,2,8,384]{6,5,4,3,2,1,0:T(8,128)S(1)}, f32[2,2,8,2,2,8,384]{6,5,4,3,2,1,0:T(8,128)S(1)}, u32[]{:S(2)}, u32[]{:S(2)}) collective-permute-start(f32[2,2,8,2,2,8,384]{6,5,4,3,2,1,0:T(8,128)S(1)} %get-tuple-element.90), channel_id=1, source_target_pairs={{0,8},{8,0},{1,9},{9,1},{2,10},{10,2},{3,11},{11,3},{4,12},{12,4},... | collective-permute-start | bytes 4718600 | tf_op jit(solution)/shard_map/ppermute | solution.py:262
  157.8 5.5 %copy-start = (bf16[256,256]{1,0:T(8,128)(2,1)S(1)}, bf16[256,256]{1,0:T(8,128)(2,1)}, u32[]{:S(2)}) copy-start(bf16[256,256]{1,0:T(8,128)(2,1)} %maximum_maximum_fusion.refs_1_.wq_ref) | copy-start | bytes 393220
  157.9 5.5 %copy-start.3 = (s32[5]{0:T(128)S(1)}, s32[5]{0:T(128)}, u32[]{:S(2)}) copy-start(s32[5]{0:T(128)} %copy-done.2) | copy-start | bytes 64
  157.9 11.6 %slice-start.4 = ((s8[5242880]{0:T(1024)(128)(4,1)}), s8[1048576]{0:T(1024)(128)(4,1)S(1)}, s32[]{:S(2)}) async-start(s8[5242880]{0:T(1024)(128)(4,1)} %bitcast.292), calls=%async_computation.4 | async-start | bytes 2097152
  159.4 19.2 %collective-permute-start.10 = (f32[2,2,2,2,2,2,8,640]{7,6,5,4,3,2,1,0:T(8,128)}, f32[2,2,2,2,2,2,8,640]{7,6,5,4,3,2,1,0:T(8,128)}, u32[]{:S(2)}, u32[]{:S(2)}) collective-permute-start(f32[2,2,2,2,2,2,8,640]{7,6,5,4,3,2,1,0:T(8,128)} %get-tuple-element.93), channel_id=1, source_target_pairs={{0,32},{32,0},{64,96},{96,64},{8,104},{40,72},{72,40},{104,8},{1,3... | collective-permute-start | bytes 3932168 | tf_op jit(solution)/shard_map/ppermute | solution.py:258
  162.1 1.2 copy-start.11
  163.3 6.1 %slice-start.5 = ((s8[5242880]{0:T(1024)(128)(4,1)}), s8[4194304]{0:T(1024)(128)(4,1)S(1)}, s32[]{:S(2)}) async-start(s8[5242880]{0:T(1024)(128)(4,1)} %bitcast.292), calls=%async_computation.5 | async-start | bytes 8388608
  166.9 20.9 %collective-permute-start.9 = (f32[2,2,2,2,2,2,2,8,384]{8,7,6,4,5,3,2,1,0:T(8,128)S(1)}, f32[2,2,2,2,2,2,2,8,384]{8,7,6,4,5,3,2,1,0:T(8,128)S(1)}, u32[]{:S(2)}, u32[]{:S(2)}) collective-permute-start(f32[2,2,2,2,2,2,2,8,384]{8,7,6,4,5,3,2,1,0:T(8,128)S(1)} %copy.55), channel_id=1, source_target_pairs={{0,16},{16,0},{4,20},{20,4},{8,28},{24,12},{12,24},{28,8},{1,17},{... | collective-permute-start | bytes 4718600 | tf_op jit(solution)/shard_map/ppermute | solution.py:258
  173.6 18.3 %collective-permute-start.14 = (f32[2,2,2,2,2,2,8,640]{7,6,5,4,3,2,1,0:T(8,128)S(1)}, f32[2,2,2,2,2,2,8,640]{7,6,5,4,3,2,1,0:T(8,128)S(1)}, u32[]{:S(2)}, u32[]{:S(2)}) collective-permute-start(f32[2,2,2,2,2,2,8,640]{7,6,5,4,3,2,1,0:T(8,128)S(1)} %get-tuple-element.92), channel_id=1, source_target_pairs={{0,1},{1,0},{2,3},{3,2},{8,11},{9,10},{10,9},{11,8},{4,5},{5,4},{6... | collective-permute-start | bytes 3932168 | tf_op jit(solution)/shard_map/ppermute | solution.py:258
  180.1 12.9 %collective-permute-start.13 = (f32[2,2,2,2,2,8,640]{6,5,4,3,2,1,0:T(8,128)S(1)}, f32[2,2,2,2,2,8,640]{6,5,4,3,2,1,0:T(8,128)S(1)}, u32[]{:S(2)}, u32[]{:S(2)}) collective-permute-start(f32[2,2,2,2,2,8,640]{6,5,4,3,2,1,0:T(8,128)S(1)} %get-tuple-element.99), channel_id=1, source_target_pairs={{0,96},{32,64},{64,32},{96,0},{8,40},{40,8},{72,104},{104,72},{1,9... | collective-permute-start | bytes 1966088 | tf_op jit(solution)/shard_map/ppermute | solution.py:258
  188.0 11.3 %collective-permute-start.12 = (f32[2,2,2,2,2,2,8,384]{7,6,5,3,4,2,1,0:T(8,128)S(1)}, f32[2,2,2,2,2,2,8,384]{7,6,5,3,4,2,1,0:T(8,128)S(1)}, u32[]{:S(2)}, u32[]{:S(2)}) collective-permute-start(f32[2,2,2,2,2,2,8,384]{7,6,5,3,4,2,1,0:T(8,128)S(1)} %get-tuple-element.96), channel_id=1, source_target_pairs={{0,20},{16,4},{4,16},{20,0},{8,24},{24,8},{12,28},{28,12},{1,21},{... | collective-permute-start | bytes 2359304 | tf_op jit(solution)/shard_map/ppermute | solution.py:258
  193.0 10.5 %collective-permute-start.16 = (f32[2,2,2,2,2,8,640]{6,5,4,3,2,1,0:T(8,128)}, f32[2,2,2,2,2,8,640]{6,5,4,3,2,1,0:T(8,128)}, u32[]{:S(2)}, u32[]{:S(2)}) collective-permute-start(f32[2,2,2,2,2,8,640]{6,5,4,3,2,1,0:T(8,128)} %get-tuple-element.98), channel_id=1, source_target_pairs={{0,3},{1,2},{2,1},{3,0},{8,9},{9,8},{10,11},{11,10},{4,7},{5,6},{6... | collective-permute-start | bytes 1966088 | tf_op jit(solution)/shard_map/ppermute | solution.py:258
  200.3 8.2 %collective-permute-start.15 = (f32[2,2,2,2,2,8,384]{6,5,4,2,3,1,0:T(8,128)}, f32[2,2,2,2,2,8,384]{6,5,4,2,3,1,0:T(8,128)}, u32[]{:S(2)}, u32[]{:S(2)}) collective-permute-start(f32[2,2,2,2,2,8,384]{6,5,4,2,3,1,0:T(8,128)} %get-tuple-element.101), channel_id=1, source_target_pairs={{0,32},{32,0},{64,96},{96,64},{8,104},{40,72},{72,40},{104,8},{1,3... | collective-permute-start | bytes 1179656 | tf_op jit(solution)/shard_map/ppermute | solution.py:258
  200.3 9.3 %copy-start.5 = (f32[1,2,2,2,2,8,640]{6,5,4,3,2,1,0:T(8,128)S(1)}, f32[1,2,2,2,2,8,640]{6,5,4,3,2,1,0:T(8,128)}, u32[]{:S(2)}) copy-start(f32[1,2,2,2,2,8,640]{6,5,4,3,2,1,0:T(8,128)} %get-tuple-element.106) | copy-start | bytes 983044
  200.3 14.1 %copy-start.4 = (f32[1,2,2,2,2,2,8,384]{7,6,5,3,4,2,1,0:T(8,128)S(1)}, f32[1,2,2,2,2,2,8,384]{7,6,5,3,4,2,1,0:T(8,128)}, u32[]{:S(2)}) copy-start(f32[1,2,2,2,2,2,8,384]{7,6,5,3,4,2,1,0:T(8,128)} %get-tuple-element.102) | copy-start | bytes 1179652
  200.3 9.3 %collective-permute-start.19 = (f32[2,2,2,2,8,640]{5,4,3,2,1,0:T(8,128)}, f32[2,2,2,2,8,640]{5,4,3,2,1,0:T(8,128)S(1)}, u32[]{:S(2)}, u32[]{:S(2)}) collective-permute-start(f32[2,2,2,2,8,640]{5,4,3,2,1,0:T(8,128)} %get-tuple-element.105), channel_id=1, source_target_pairs={{0,1},{1,0},{2,3},{3,2},{8,11},{9,10},{10,9},{11,8},{4,5},{5,4},{6... | collective-permute-start | bytes 983048 | tf_op jit(solution)/shard_map/ppermute | solution.py:258
  204.7 7.2 %collective-permute-start.18 = (f32[2,2,2,2,8,640]{5,4,3,2,1,0:T(8,128)S(1)}, f32[2,2,2,2,8,640]{5,4,3,2,1,0:T(8,128)S(1)}, u32[]{:S(2)}, u32[]{:S(2)}) collective-permute-start(f32[2,2,2,2,8,640]{5,4,3,2,1,0:T(8,128)S(1)} %get-tuple-element.104), channel_id=1, source_target_pairs={{0,16},{16,0},{4,20},{20,4},{8,28},{24,12},{12,24},{28,8},{1,17},{... | collective-permute-start | bytes 983048 | tf_op jit(solution)/shard_map/ppermute | solution.py:258
  209.5 4.9 %collective-permute-start.17 = (f32[2,2,2,2,8,384]{5,4,3,1,2,0:T(8,128)S(1)}, f32[2,2,2,2,8,384]{5,4,3,1,2,0:T(8,128)S(1)}, u32[]{:S(2)}, u32[]{:S(2)}) collective-permute-start(f32[2,2,2,2,8,384]{5,4,3,1,2,0:T(8,128)S(1)} %fusion.29), channel_id=1, source_target_pairs={{0,96},{32,64},{64,32},{96,0},{8,40},{40,8},{72,104},{104,72},{1,9... | collective-permute-start | bytes 589832 | tf_op jit(solution)/shard_map/ppermute | solution.py:258
  209.6 5.8 %collective-permute-start.20 = (f32[2,2,2,8,640]{4,3,2,1,0:T(8,128)S(1)}, f32[2,2,2,8,640]{4,3,2,1,0:T(8,128)S(1)}, u32[]{:S(2)}, u32[]{:S(2)}) collective-permute-start(f32[2,2,2,8,640]{4,3,2,1,0:T(8,128)S(1)} %fusion.40), channel_id=1, source_target_pairs={{0,3},{1,2},{2,1},{3,0},{8,9},{9,8},{10,11},{11,10},{4,7},{5,6},{6... | collective-permute-start | bytes 491528 | tf_op jit(solution)/shard_map/ppermute | solution.py:258
  211.9 4.5 %collective-permute-start.21 = (f32[2,2,2,8,640]{4,3,2,1,0:T(8,128)S(1)}, f32[2,2,2,8,640]{4,3,2,1,0:T(8,128)S(1)}, u32[]{:S(2)}, u32[]{:S(2)}) collective-permute-start(f32[2,2,2,8,640]{4,3,2,1,0:T(8,128)S(1)} %fusion.42), channel_id=1, source_target_pairs={{0,20},{16,4},{4,16},{20,0},{8,24},{24,8},{12,28},{28,12},{1,21},{... | collective-permute-start | bytes 491528 | tf_op jit(solution)/shard_map/ppermute | solution.py:258
  216.6 7.0 %collective-permute-start.23 = (f32[2,2,8,640]{3,2,1,0:T(8,128)S(1)}, f32[2,2,8,640]{3,2,1,0:T(8,128)S(1)}, u32[]{:S(2)}, u32[]{:S(2)}) collective-permute-start(f32[2,2,8,640]{3,2,1,0:T(8,128)S(1)} %get-tuple-element.116), channel_id=1, source_target_pairs={{0,8},{8,0},{1,9},{9,1},{2,10},{10,2},{3,11},{11,3},{4,12},{12,4},... | collective-permute-start | bytes 245768 | tf_op jit(solution)/shard_map/ppermute | solution.py:262
  222.3 1.3 collective-permute-start.24
  222.4 1.4 collective-permute-start.22

commit v6 on v5

--- a/solution.py
+++ b/solution.py
@@ -16,7 +16,7 @@
 EVENTS = (
     *("z0", "x0", "y0", "z1", "x1", "zk"),
     *("y1", "x2", "z2", "y2", "x3", "z3"),
-    *("y3", "z4", "x4", "y4", "z5", "x5", "y5"),
+    *("x4", "y3", "z4", "x5", "y4", "z5", "y5"),
 )
 
 

time: 228 us -> 228 us (level)
    ppermute x18, starting transfers between devices: 24.9 us -> 22.5 us  [exchange(): return lax.ppermute(value, names, pairs)]
    add x5 -> x6, other arithmetic: 5.17 us -> 7.54 us  [body(): keep[part] = keep[part][0] + arrived[part][0]]
    add x10 -> x9, other arithmetic: 16.3 us -> 15 us  [body(): latest = send[part] = keep[part][1] + arrived[part][1]]
  transfers between devices with their start and end apart: 25 -> 25, of which waited for: 14 -> 17; matrix products, arithmetic and copies ran while one was open for 29% -> 30% of each run, Pallas kernels for 17% -> 17%
where the time goes in v6:
time: 228 us; the launch traced here: 227 us
  waiting for transfers between devices  77.6 us (34%)
  Pallas kernels  46.3 us (20%)
  other arithmetic  35.8 us (16%)
  local copies, waits for them, and re-layouts  33.9 us (15%)
  starting transfers between devices  33.1 us (15%)
    ppermute x18, waiting for transfers between devices, exchange(): return lax.ppermute(value, names, pairs)  75.7 us
    pallas_call x6, Pallas kernels, kernel_call(): pl.pallas_call(kernel, grid_spec=pltpu.PrefetchScalarGridSpec(num_scalar_...  43.2 us
    ppermute x18, starting transfers between devices, exchange(): return lax.ppermute(value, names, pairs)  22.5 us
    unnamed x43, local copies, waits for them, and re-layouts  19.9 us
    add x9, other arithmetic, body(): latest = send[part] = keep[part][1] + arrived[part][1]  15 us
    mul x4, local copies, waits for them, and re-layouts, rotation_tables(): right = right * jnp.eye(8, dtype=jnp.float32)[:, None, :, None]  11.9 us
    ppermute x7, starting transfers between devices, swap(): return lax.ppermute(value, 'c', [(0, 1), (1, 0)])  10.5 us
    add x6, other arithmetic, body(): keep[part] = keep[part][0] + arrived[part][0]  7.54 us
  transfers between devices with their start and end apart: 25, of which 17 were waited for; matrix products, arithmetic and copies ran while one was open for 30% of the time, Pallas kernels for 17%

profile of v6, /device:TPU:1, one launch (start us, length us, event | category | flops | bytes accessed | tf_op | source)
XLA Modules:
  0.0 227.3 jit_solution(5108948752238183577)
XLA Ops:
  0.0 0.7 add_convert_fusion
  0.7 1.5 collective-permute-start
  2.2 18.6 %copy.67 = bf16[16,64,4,2,1024]{4,1,3,2,0:T(8,128)(2,1)} copy(bf16[16,64,4,2,1024]{4,3,2,1,0:T(2,128)(2,1)} %param.9) | data formatting | bytes 33554432 | tf_op args[0]
  20.9 4.4 %shard_map.91 = f32[16,2,64,640]{3,2,1,0:T(8,128)} custom-call(s32[5]{0:T(128)S(1)} %stack.92.refs_0_.where_ref, bf16[16,4,2,64,1024]{4,3,2,1,0:T(8,128)(2,1)} %bitcast.279, bf16[16,4,2,64,1024]{4,3,2,1,0:T(8,128)(2,1)} %bitcast.280), custom_call_target="tpu_custom_call" | custom-call | flops 2147483648 | bytes 38797312 | tf_op jit(solution)/shard_map/pallas_call | solution.py:140
  25.5 4.3 %shard_map.92 = f32[16,2,64,640]{3,2,1,0:T(8,128)} custom-call(s32[5]{0:T(128)S(1)} %stack.92.refs_0_.where_ref, bf16[16,4,2,64,1024]{4,3,2,1,0:T(8,128)(2,1)} %bitcast.281, bf16[16,4,2,64,1024]{4,3,2,1,0:T(8,128)(2,1)} %bitcast.282), custom_call_target="tpu_custom_call" | custom-call | flops 2147483648 | bytes 38797312 | tf_op jit(solution)/shard_map/pallas_call | solution.py:140
  29.8 0.5 collective-permute-start.2
  31.1 9.7 %shard_map.93 = (f32[2,2,2,2,8,2,2,8,384]{8,7,6,5,4,3,2,1,0:T(8,128)}, f32[2,2,2,2,8,2,2,8,384]{8,7,6,5,4,3,2,1,0:T(8,128)}) custom-call(s32[5]{0:T(128)S(1)} %stack.92.refs_0_.where_ref, bf16[32,32]{1,0:T(8,128)(2,1)S(1)} %reshape.653.wk_ref.refs_2_, bf16[16,4,2,64,1024]{4,3,2,1,0:T(8,128)(2,1)} %bitcast.283), custom_call_target="tpu_custom_call" | custom-call | flops 2147483648 | bytes 29362176 | tf_op jit(solution)/shard_map/pallas_call | solution.py:140
  40.8 3.8 %collective-permute-start.3 = (f32[2,2,2,2,8,2,2,8,384]{8,7,6,5,4,3,2,1,0:T(8,128)}, f32[2,2,2,2,8,2,2,8,384]{8,7,6,5,4,3,2,1,0:T(8,128)}, u32[]{:S(2)}, u32[]{:S(2)}) collective-permute-start(f32[2,2,2,2,8,2,2,8,384]{8,7,6,5,4,3,2,1,0:T(8,128)} %get-tuple-element.55), channel_id=1, source_target_pairs={{0,1},{1,0},{2,3},{3,2},{8,11},{9,10},{10,9},{11,8},{4,5},{5,4},{6... | collective-permute-start | bytes 18874376 | tf_op jit(solution)/shard_map/ppermute | solution.py:258
  44.7 0.6 fusion.47
  45.2 0.6 multiply_convert_fusion.2
  45.8 0.8 maximum_maximum_fusion.refs_1_.wq_ref
  46.6 10.6 %shard_map.94 = (f32[2,2,2,2,2,2,2,2,8,640]{9,8,7,6,5,4,3,2,1,0:T(8,128)}, f32[2,2,2,2,2,2,2,2,8,640]{9,8,7,6,5,4,3,2,1,0:T(8,128)}) custom-call(s32[5]{0:T(128)} %copy-done.2, bf16[256,256]{1,0:T(8,128)(2,1)} %maximum_maximum_fusion.refs_1_.wq_ref, bf16[32,32]{1,0:T(8,128)(2,1)} %copy-done.1, bf16[16,4,2,64,1024]{4,3,2,1,0:T(8,128)(2,1)} %bitcast.284, ...), custom_call_target="tpu_custom_call" | custom-call | flops 2147483648 | bytes 49416192 | tf_op jit(solution)/shard_map/pallas_call | solution.py:140
  57.2 2.5 %collective-permute-start.6 = (f32[2,2,2,2,2,2,2,2,8,640]{9,8,7,6,5,4,3,2,1,0:T(8,128)}, f32[2,2,2,2,2,2,2,2,8,640]{9,8,7,6,5,4,3,2,1,0:T(8,128)}, u32[]{:S(2)}, u32[]{:S(2)}) collective-permute-start(f32[2,2,2,2,2,2,2,2,8,640]{9,8,7,6,5,4,3,2,1,0:T(8,128)} %get-tuple-element.64), channel_id=1, source_target_pairs={{0,16},{16,0},{4,20},{20,4},{8,28},{24,12},{12,24},{28,8},{1,17},{... | collective-permute-start | bytes 15728648 | tf_op jit(solution)/shard_map/ppermute | solution.py:258
  59.7 10.8 %shard_map.95 = (f32[2,2,2,2,2,2,2,2,8,640]{9,8,7,6,5,4,3,2,1,0:T(8,128)}, f32[2,2,2,2,2,2,2,2,8,640]{9,8,7,6,5,4,3,2,1,0:T(8,128)}) custom-call(s32[5]{0:T(128)} %copy-done.2, bf16[256,256]{1,0:T(8,128)(2,1)} %maximum_maximum_fusion.refs_1_.wq_ref, bf16[32,32]{1,0:T(8,128)(2,1)} %copy-done.1, bf16[16,4,2,64,1024]{4,3,2,1,0:T(8,128)(2,1)} %bitcast.286, ...), custom_call_target="tpu_custom_call" | custom-call | flops 2147483648 | bytes 49416192 | tf_op jit(solution)/shard_map/pallas_call | solution.py:140
  70.5 2.7 %collective-permute-start.5 = (f32[2,2,2,2,2,2,2,2,8,640]{9,8,7,6,5,4,3,2,1,0:T(8,128)}, f32[2,2,2,2,2,2,2,2,8,640]{9,8,7,6,5,4,3,2,1,0:T(8,128)}, u32[]{:S(2)}, u32[]{:S(2)}) collective-permute-start(f32[2,2,2,2,2,2,2,2,8,640]{9,8,7,6,5,4,3,2,1,0:T(8,128)} %get-tuple-element.63), channel_id=1, source_target_pairs={{0,32},{32,0},{64,96},{96,64},{8,104},{40,72},{72,40},{104,8},{1,3... | collective-permute-start | bytes 15728648 | tf_op jit(solution)/shard_map/ppermute | solution.py:258
  73.8 4.4 %mul.351 = f32[2,2,2,8,32,8,32]{6,5,4,3,2,1,0:T(8,128)} broadcast(f32[2,2,2,32,32]{4,3,2,1,0:T(8,128)S(1)} %copy.51), dimensions={0,1,2,4,6} | broadcast | bytes 2129920 | tf_op jit(solution)/shard_map/mul | solution.py:271
  78.2 7.1 %mul.352 = f32[2,2,2,256,256]{4,3,2,1,0:T(8,128)} reshape(f32[2,2,2,8,32,8,32]{6,5,4,3,2,1,0:T(8,128)} %mul.351) | data formatting | bytes 4194304 | tf_op jit(solution)/shard_map/mul | solution.py:271
  85.7 0.6 copy.53
  86.3 0.6 reshape.654.left_ref
  86.9 2.0 broadcast_multiply_fusion.right_ref
  88.9 24.4 %collective-permute-done.3 = f32[2,2,2,2,8,2,2,8,384]{8,7,6,5,4,3,2,1,0:T(8,128)} collective-permute-done((f32[2,2,2,2,8,2,2,8,384]{8,7,6,5,4,3,2,1,0:T(8,128)}, f32[2,2,2,2,8,2,2,8,384]{8,7,6,5,4,3,2,1,0:T(8,128)}, u32[]{:S(2)}, u32[]{:S(2)}) %collective-permute-start.3) | collective-permute-done | bytes 6291488 | tf_op jit(solution)/shard_map/ppermute | solution.py:258
  113.3 3.5 %add_bitcast_fusion = f32[2,2,2,8,2,2,8,384]{7,6,5,4,3,2,1,0:T(8,128)S(1)} fusion(f32[2,2,2,2,8,2,2,8,384]{8,7,6,5,4,3,2,1,0:T(8,128)} %collective-permute-done.3, f32[2,2,2,2,8,2,2,8,384]{8,7,6,5,4,3,2,1,0:T(8,128)} %get-tuple-element.61), kind=kLoop, calls=%fused_computation.2 | loop fusion | flops 786432 | bytes 9437184 | tf_op jit(solution)/shard_map/add | solution.py:396
  116.9 0.5 collective-permute-done.6
  117.4 3.1 %add_bitcast_fusion.2 = f32[2,2,2,2,2,2,2,8,640]{8,7,6,5,4,3,2,1,0:T(8,128)S(1)} fusion(f32[2,2,2,2,2,2,2,2,8,640]{9,8,7,6,5,4,3,2,1,0:T(8,128)} %collective-permute-done.6, f32[2,2,2,2,2,2,2,2,8,640]{9,8,7,6,5,4,3,2,1,0:T(8,128)} %get-tuple-element.68), kind=kLoop, calls=%fused_computation.6 | loop fusion | flops 655360 | bytes 7864320 | tf_op jit(solution)/shard_map/add | solution.py:396
  120.5 0.8 collective-permute-start.8
  121.3 9.6 %collective-permute-done.5 = f32[2,2,2,2,2,2,2,2,8,640]{9,8,7,6,5,4,3,2,1,0:T(8,128)} collective-permute-done((f32[2,2,2,2,2,2,2,2,8,640]{9,8,7,6,5,4,3,2,1,0:T(8,128)}, f32[2,2,2,2,2,2,2,2,8,640]{9,8,7,6,5,4,3,2,1,0:T(8,128)}, u32[]{:S(2)}, u32[]{:S(2)}) %collective-permute-start.5) | collective-permute-done | bytes 5242912 | tf_op jit(solution)/shard_map/ppermute | solution.py:258
  130.9 3.6 %add_bitcast_fusion.1 = f32[2,2,2,2,2,2,2,8,640]{8,7,6,5,4,3,2,1,0:T(8,128)} fusion(f32[2,2,2,2,2,2,2,2,8,640]{9,8,7,6,5,4,3,2,1,0:T(8,128)} %collective-permute-done.5, f32[2,2,2,2,2,2,2,2,8,640]{9,8,7,6,5,4,3,2,1,0:T(8,128)S(1)} %bitcast.291), kind=kLoop, calls=%fused_computation.5 | loop fusion | flops 655360 | bytes 7864320 | tf_op jit(solution)/shard_map/add | solution.py:396
  134.6 2.7 %slice_add_fusion = f32[1,2,2,2,8,2,2,8,384]{8,7,6,5,4,3,2,1,0:T(8,128)S(1)} fusion(f32[2,2,2,2,8,2,2,8,384]{8,7,6,5,4,3,2,1,0:T(8,128)} %collective-permute-done.3, f32[2,2,2,2,8,2,2,8,384]{8,7,6,5,4,3,2,1,0:T(8,128)S(1)} %bitcast.289), kind=kLoop, calls=%fused_computation.1 | loop fusion | flops 786432 | bytes 9437184 | tf_op jit(solution)/shard_map/add | solution.py:399
  137.2 16.1 %collective-permute-done.4 = f32[2,2,2,8,2,2,8,384]{7,6,5,4,3,2,1,0:T(8,128)S(1)} collective-permute-done((f32[2,2,2,8,2,2,8,384]{7,6,5,4,3,2,1,0:T(8,128)S(1)}, f32[2,2,2,8,2,2,8,384]{7,6,5,4,3,2,1,0:T(8,128)S(1)}, u32[]{:S(2)}, u32[]{:S(2)}) %collective-permute-start.4) | collective-permute-done | bytes 3145760 | tf_op jit(solution)/shard_map/ppermute | solution.py:258
  153.4 0.6 fusion.3
  154.0 1.7 collective-permute-start.7
  155.8 2.1 slice_add_fusion.2
  157.9 1.4 fusion.9
  159.3 2.7 %collective-permute-start.10 = (f32[2,2,2,2,2,2,8,640]{7,6,5,4,3,2,1,0:T(8,128)}, f32[2,2,2,2,2,2,8,640]{7,6,5,4,3,2,1,0:T(8,128)}, u32[]{:S(2)}, u32[]{:S(2)}) collective-permute-start(f32[2,2,2,2,2,2,8,640]{7,6,5,4,3,2,1,0:T(8,128)} %get-tuple-element.93), channel_id=1, source_target_pairs={{0,32},{32,0},{64,96},{96,64},{8,104},{40,72},{72,40},{104,8},{1,3... | collective-permute-start | bytes 3932168 | tf_op jit(solution)/shard_map/ppermute | solution.py:258
  162.1 1.2 copy-done.11
  163.2 3.4 %shard_map.96 = (f32[2,2,2,2,2,2,2,8,384]{8,7,6,5,4,3,2,1,0:T(8,128)S(1)}, f32[2,2,2,2,2,2,2,8,384]{8,7,6,5,4,3,2,1,0:T(8,128)S(1)}) custom-call(s32[5]{0:T(128)S(1)} %copy-done.3, bf16[256,256]{1,0:T(8,128)(2,1)S(1)} %copy-done, f32[2,2,8,2,2,8,384]{6,5,4,3,2,1,0:T(8,128)S(1)} %get-tuple-element.89.own_ref, f32[2,2,8,2,2,8,384]{6,5,4,3,2,1,0:T(8,128)} %copy-done.11), custom_call_target="tpu_custom_call" | custom-call | flops 2147483648 | bytes 6422528 | tf_op jit(solution)/shard_map/pallas_call | solution.py:140
  166.8 2.6 %collective-permute-start.9 = (f32[2,2,2,2,2,2,2,8,384]{8,7,6,4,5,3,2,1,0:T(8,128)S(1)}, f32[2,2,2,2,2,2,2,8,384]{8,7,6,4,5,3,2,1,0:T(8,128)S(1)}, u32[]{:S(2)}, u32[]{:S(2)}) collective-permute-start(f32[2,2,2,2,2,2,2,8,384]{8,7,6,4,5,3,2,1,0:T(8,128)S(1)} %copy.55), channel_id=1, source_target_pairs={{0,16},{16,0},{4,20},{20,4},{8,28},{24,12},{12,24},{28,8},{1,17},{... | collective-permute-start | bytes 4718600 | tf_op jit(solution)/shard_map/ppermute | solution.py:258
  169.3 2.1 slice_add_fusion.1
  171.5 2.1 fusion.4
  173.5 3.0 %collective-permute-start.14 = (f32[2,2,2,2,2,2,8,640]{7,6,5,4,3,2,1,0:T(8,128)S(1)}, f32[2,2,2,2,2,2,8,640]{7,6,5,4,3,2,1,0:T(8,128)S(1)}, u32[]{:S(2)}, u32[]{:S(2)}) collective-permute-start(f32[2,2,2,2,2,2,8,640]{7,6,5,4,3,2,1,0:T(8,128)S(1)} %get-tuple-element.92), channel_id=1, source_target_pairs={{0,1},{1,0},{2,3},{3,2},{8,11},{9,10},{10,9},{11,8},{4,5},{5,4},{6... | collective-permute-start | bytes 3932168 | tf_op jit(solution)/shard_map/ppermute | solution.py:258
  176.6 1.4 collective-permute-done.10
  178.0 1.5 fusion.16
  179.5 0.5 collective-permute-start.13
  179.9 7.7 %collective-permute-done.9 = f32[2,2,2,2,2,2,2,8,384]{8,7,6,4,5,3,2,1,0:T(8,128)S(1)} collective-permute-done((f32[2,2,2,2,2,2,2,8,384]{8,7,6,4,5,3,2,1,0:T(8,128)S(1)}, f32[2,2,2,2,2,2,2,8,384]{8,7,6,4,5,3,2,1,0:T(8,128)S(1)}, u32[]{:S(2)}, u32[]{:S(2)}) %collective-permute-start.9) | collective-permute-done | bytes 1572896 | tf_op jit(solution)/shard_map/ppermute | solution.py:258
  187.6 1.2 slice_add_fusion.4
  188.8 3.0 %collective-permute-done.14 = f32[2,2,2,2,2,2,8,640]{7,6,5,4,3,2,1,0:T(8,128)S(1)} collective-permute-done((f32[2,2,2,2,2,2,8,640]{7,6,5,4,3,2,1,0:T(8,128)S(1)}, f32[2,2,2,2,2,2,8,640]{7,6,5,4,3,2,1,0:T(8,128)S(1)}, u32[]{:S(2)}, u32[]{:S(2)}) %collective-permute-start.14) | collective-permute-done | bytes 1310752 | tf_op jit(solution)/shard_map/ppermute | solution.py:258
  191.9 1.3 fusion.11
  193.1 0.9 fusion.25
  194.1 2.4 %collective-permute-start.17 = (f32[2,2,2,2,8,640]{5,4,3,2,1,0:T(8,128)}, f32[2,2,2,2,8,640]{5,4,3,2,1,0:T(8,128)}, u32[]{:S(2)}, u32[]{:S(2)}) collective-permute-start(f32[2,2,2,2,8,640]{5,4,3,2,1,0:T(8,128)} %get-tuple-element.105), channel_id=1, source_target_pairs={{0,1},{1,0},{2,3},{3,2},{8,11},{9,10},{10,9},{11,8},{4,5},{5,4},{6... | collective-permute-start | bytes 983048 | tf_op jit(solution)/shard_map/ppermute | solution.py:258
  196.4 3.8 %collective-permute-done.12 = f32[2,2,2,2,2,2,8,384]{7,6,5,3,4,2,1,0:T(8,128)} collective-permute-done((f32[2,2,2,2,2,2,8,384]{7,6,5,3,4,2,1,0:T(8,128)}, f32[2,2,2,2,2,2,8,384]{7,6,5,3,4,2,1,0:T(8,128)}, u32[]{:S(2)}, u32[]{:S(2)}) %collective-permute-start.12) | collective-permute-done | bytes 786464 | tf_op jit(solution)/shard_map/ppermute | solution.py:258
  200.3 1.3 fusion.19
  201.6 3.8 %collective-permute-done.17 = f32[2,2,2,2,8,640]{5,4,3,2,1,0:T(8,128)} collective-permute-done((f32[2,2,2,2,8,640]{5,4,3,2,1,0:T(8,128)}, f32[2,2,2,2,8,640]{5,4,3,2,1,0:T(8,128)}, u32[]{:S(2)}, u32[]{:S(2)}) %collective-permute-start.17) | collective-permute-done | bytes 327712 | tf_op jit(solution)/shard_map/ppermute | solution.py:258
  205.4 1.0 fusion.42
  206.6 1.1 fusion.20
  207.7 1.0 collective-permute-start.19
  208.8 0.7 collective-permute-done.15
  209.6 1.1 collective-permute-done.20
  210.7 0.9 fusion.38
  211.6 3.5 %collective-permute-start.23 = (f32[2,2,8,640]{3,2,1,0:T(8,128)S(1)}, f32[2,2,8,640]{3,2,1,0:T(8,128)S(1)}, u32[]{:S(2)}, u32[]{:S(2)}) collective-permute-start(f32[2,2,8,640]{3,2,1,0:T(8,128)S(1)} %get-tuple-element.116), channel_id=1, source_target_pairs={{0,8},{8,0},{1,9},{9,1},{2,10},{10,2},{3,11},{11,3},{4,12},{12,4},... | collective-permute-start | bytes 245768 | tf_op jit(solution)/shard_map/ppermute | solution.py:262
  215.4 0.7 collective-permute-done.23
  216.2 3.4 %collective-permute-done.21 = f32[2,2,2,8,640]{4,3,2,1,0:T(8,128)S(1)} collective-permute-done((f32[2,2,2,8,640]{4,3,2,1,0:T(8,128)S(1)}, f32[2,2,2,8,640]{4,3,2,1,0:T(8,128)S(1)}, u32[]{:S(2)}, u32[]{:S(2)}) %collective-permute-start.21) | collective-permute-done | bytes 163872 | tf_op jit(solution)/shard_map/ppermute | solution.py:258
  219.6 3.1 %collective-permute-start.24 = (f32[2,2,8,640]{3,2,1,0:T(8,128)S(1)}, f32[2,2,8,640]{3,2,1,0:T(8,128)S(1)}, u32[]{:S(2)}, u32[]{:S(2)}) collective-permute-start(f32[2,2,8,640]{3,2,1,0:T(8,128)S(1)} %get-tuple-element.114), channel_id=1, source_target_pairs={{0,8},{8,0},{1,9},{9,1},{2,10},{10,2},{3,11},{11,3},{4,12},{12,4},... | collective-permute-start | bytes 245768 | tf_op jit(solution)/shard_map/ppermute | solution.py:262
  222.9 0.8 collective-permute-done.24
  224.2 3.1 %shard_map.97 = f32[2,8,4,2,1024]{4,3,2,1,0:T(2,128)} custom-call(f32[2,2,4,8,1024]{4,3,2,1,0:T(8,128)S(1)} %pad_maximum_fusion.sum_ref, f32[2,2,2,256,256]{4,3,2,1,0:T(8,128)S(1)} %broadcast_multiply_fusion.right_ref, f32[2,8,64,64]{3,2,1,0:T(8,128)S(1)} %reshape.654.left_ref), custom_call_target="tpu_custom_call" | custom-call | flops 268435456 | bytes 4194304 | tf_op jit(solution)/shard_map/pallas_call | solution.py:329
  (117 shorter events, 3.5 us)
Async XLA Ops:
  0.7 20.2 %collective-permute-start = (f32[4,64]{1,0:T(4,128)S(1)}, f32[4,64]{1,0:T(4,128)S(1)}, u32[]{:S(2)}, u32[]{:S(2)}) collective-permute-start(f32[4,64]{1,0:T(4,128)S(1)} %add_convert_fusion), channel_id=1, source_target_pairs={{0,8},{8,0},{1,9},{9,1},{2,10},{10,2},{3,11},{11,3},{4,12},{12,4},... | collective-permute-start | bytes 3080 | tf_op jit(solution)/shard_map/ppermute | solution.py:262
  20.9 10.1 %copy-start.2 = (s32[5]{0:T(128)}, s32[5]{0:T(128)S(1)}, u32[]{:S(2)}) copy-start(s32[5]{0:T(128)S(1)} %stack.92.refs_0_.where_ref) | copy-start | bytes 64
  25.3 4.9 %copy-start.8 = (s32[3,16]{1,0:T(4,128)S(1)}, s32[3,16]{1,0:T(4,128)}, u32[]{:S(2)}) copy-start(s32[3,16]{1,0:T(4,128)} %param.10) | copy-start | bytes 580
  25.3 4.9 %copy-start.12 = (s32[16]{0:T(128)S(1)}, s32[16]{0:T(128)}, u32[]{:S(2)}) copy-start(s32[16]{0:T(128)} %param.12) | copy-start | bytes 196
  25.4 4.9 %copy-start.10 = (f32[3,16]{1,0:T(4,128)S(1)}, f32[3,16]{1,0:T(4,128)}, u32[]{:S(2)}) copy-start(f32[3,16]{1,0:T(4,128)} %param.14) | copy-start | bytes 580
  25.4 21.3 %collective-permute-start.1 = (f32[16,2,64,640]{3,2,1,0:T(8,128)}, f32[16,2,64,640]{3,2,1,0:T(8,128)}, u32[]{:S(2)}, u32[]{:S(2)}) collective-permute-start(f32[16,2,64,640]{3,2,1,0:T(8,128)} %shard_map.91), channel_id=1, source_target_pairs={{0,8},{8,0},{1,9},{9,1},{2,10},{10,2},{3,11},{11,3},{4,12},{12,4},... | collective-permute-start | bytes 15728648 | tf_op jit(solution)/shard_map/ppermute | solution.py:262
  29.8 29.9 %collective-permute-start.2 = (f32[16,2,64,640]{3,2,1,0:T(8,128)}, f32[16,2,64,640]{3,2,1,0:T(8,128)}, u32[]{:S(2)}, u32[]{:S(2)}) collective-permute-start(f32[16,2,64,640]{3,2,1,0:T(8,128)} %shard_map.92), channel_id=1, source_target_pairs={{0,8},{8,0},{1,9},{9,1},{2,10},{10,2},{3,11},{11,3},{4,12},{12,4},... | collective-permute-start | bytes 15728648 | tf_op jit(solution)/shard_map/ppermute | solution.py:262
  31.1 9.7 %copy-start.1 = (bf16[32,32]{1,0:T(8,128)(2,1)}, bf16[32,32]{1,0:T(8,128)(2,1)S(1)}, u32[]{:S(2)}) copy-start(bf16[32,32]{1,0:T(8,128)(2,1)S(1)} %reshape.653.wk_ref.refs_2_) | copy-start | bytes 6148
  31.1 13.6 %copy-start.9 = (f32[3,128]{1,0:T(4,128)S(1)}, f32[3,128]{1,0:T(4,128)}, u32[]{:S(2)}) copy-start(f32[3,128]{1,0:T(4,128)} %param.15) | copy-start | bytes 4612
  40.8 72.5 %collective-permute-start.3 = (f32[2,2,2,2,8,2,2,8,384]{8,7,6,5,4,3,2,1,0:T(8,128)}, f32[2,2,2,2,8,2,2,8,384]{8,7,6,5,4,3,2,1,0:T(8,128)}, u32[]{:S(2)}, u32[]{:S(2)}) collective-permute-start(f32[2,2,2,2,8,2,2,8,384]{8,7,6,5,4,3,2,1,0:T(8,128)} %get-tuple-element.55), channel_id=1, source_target_pairs={{0,1},{1,0},{2,3},{3,2},{8,11},{9,10},{10,9},{11,8},{4,5},{5,4},{6... | collective-permute-start | bytes 18874376 | tf_op jit(solution)/shard_map/ppermute | solution.py:258
  57.2 60.1 %collective-permute-start.6 = (f32[2,2,2,2,2,2,2,2,8,640]{9,8,7,6,5,4,3,2,1,0:T(8,128)}, f32[2,2,2,2,2,2,2,2,8,640]{9,8,7,6,5,4,3,2,1,0:T(8,128)}, u32[]{:S(2)}, u32[]{:S(2)}) collective-permute-start(f32[2,2,2,2,2,2,2,2,8,640]{9,8,7,6,5,4,3,2,1,0:T(8,128)} %get-tuple-element.64), channel_id=1, source_target_pairs={{0,16},{16,0},{4,20},{20,4},{8,28},{24,12},{12,24},{28,8},{1,17},{... | collective-permute-start | bytes 15728648 | tf_op jit(solution)/shard_map/ppermute | solution.py:258
  59.7 14.0 %copy-start.7 = (f32[2,2,32,32]{3,2,1,0:T(8,128)S(1)}, f32[2,2,32,32]{3,2,1,0:T(8,128)}, u32[]{:S(2)}) copy-start(f32[2,2,32,32]{3,2,1,0:T(8,128)} %param.16) | copy-start | bytes 49156
  70.5 60.4 %collective-permute-start.5 = (f32[2,2,2,2,2,2,2,2,8,640]{9,8,7,6,5,4,3,2,1,0:T(8,128)}, f32[2,2,2,2,2,2,2,2,8,640]{9,8,7,6,5,4,3,2,1,0:T(8,128)}, u32[]{:S(2)}, u32[]{:S(2)}) collective-permute-start(f32[2,2,2,2,2,2,2,2,8,640]{9,8,7,6,5,4,3,2,1,0:T(8,128)} %get-tuple-element.63), channel_id=1, source_target_pairs={{0,32},{32,0},{64,96},{96,64},{8,104},{40,72},{72,40},{104,8},{1,3... | collective-permute-start | bytes 15728648 | tf_op jit(solution)/shard_map/ppermute | solution.py:258
  78.2 7.1 %copy-start.6 = (f32[2,8,2,32,32]{4,3,2,1,0:T(8,128)S(1)}, f32[2,8,2,32,32]{4,3,2,1,0:T(8,128)}, u32[]{:S(2)}) copy-start(f32[2,8,2,32,32]{4,3,2,1,0:T(8,128)} %param.17) | copy-start | bytes 393220
  86.9 44.0 %slice-start.2 = ((s8[5242880]{0:T(1024)(128)(4,1)}), s8[4194304]{0:T(1024)(128)(4,1)S(1)}, s32[]{:S(2)}) async-start(s8[5242880]{0:T(1024)(128)(4,1)} %bitcast.290), calls=%async_computation.2 | async-start | bytes 8388608
  88.9 42.0 %slice-start.3 = ((s8[5242880]{0:T(1024)(128)(4,1)}), s8[1048576]{0:T(1024)(128)(4,1)S(1)}, s32[]{:S(2)}) async-start(s8[5242880]{0:T(1024)(128)(4,1)} %bitcast.290), calls=%async_computation.3 | async-start | bytes 2097152
  116.8 36.6 %collective-permute-start.4 = (f32[2,2,2,8,2,2,8,384]{7,6,5,4,3,2,1,0:T(8,128)S(1)}, f32[2,2,2,8,2,2,8,384]{7,6,5,4,3,2,1,0:T(8,128)S(1)}, u32[]{:S(2)}, u32[]{:S(2)}) collective-permute-start(f32[2,2,2,8,2,2,8,384]{7,6,5,4,3,2,1,0:T(8,128)S(1)} %add_bitcast_fusion), channel_id=1, source_target_pairs={{0,3},{1,2},{2,1},{3,0},{8,9},{9,8},{10,11},{11,10},{4,7},{5,6},{6... | collective-permute-start | bytes 9437192 | tf_op jit(solution)/shard_map/ppermute | solution.py:258
  117.4 17.2 %slice-start = ((s8[6291456]{0:T(1024)(128)(4,1)}), s8[4194304]{0:T(1024)(128)(4,1)S(1)}, s32[]{:S(2)}) async-start(s8[6291456]{0:T(1024)(128)(4,1)} %bitcast.288), calls=%async_computation | async-start | bytes 8388608
  120.4 14.1 %slice-start.1 = ((s8[6291456]{0:T(1024)(128)(4,1)}), s8[2097152]{0:T(1024)(128)(4,1)S(1)}, s32[]{:S(2)}) async-start(s8[6291456]{0:T(1024)(128)(4,1)} %bitcast.288), calls=%async_computation.1 | async-start | bytes 4194304
  120.5 37.4 %collective-permute-start.8 = (f32[2,2,2,2,2,2,2,8,640]{8,7,6,5,4,3,2,1,0:T(8,128)S(1)}, f32[2,2,2,2,2,2,2,8,640]{8,7,6,5,4,3,2,1,0:T(8,128)S(1)}, u32[]{:S(2)}, u32[]{:S(2)}) collective-permute-start(f32[2,2,2,2,2,2,2,8,640]{8,7,6,5,4,3,2,1,0:T(8,128)S(1)} %add_bitcast_fusion.2), channel_id=1, source_target_pairs={{0,20},{16,4},{4,16},{20,0},{8,24},{24,8},{12,28},{28,12},{1,21},{... | collective-permute-start | bytes 7864328 | tf_op jit(solution)/shard_map/ppermute | solution.py:258
  134.5 36.9 %collective-permute-start.11 = (f32[2,2,2,2,2,2,2,8,640]{8,7,6,5,4,3,2,1,0:T(8,128)}, f32[2,2,2,2,2,2,2,8,640]{8,7,6,5,4,3,2,1,0:T(8,128)}, u32[]{:S(2)}, u32[]{:S(2)}) collective-permute-start(f32[2,2,2,2,2,2,2,8,640]{8,7,6,5,4,3,2,1,0:T(8,128)} %add_bitcast_fusion.1), channel_id=1, source_target_pairs={{0,96},{32,64},{64,32},{96,0},{8,40},{40,8},{72,104},{104,72},{1,9... | collective-permute-start | bytes 7864328 | tf_op jit(solution)/shard_map/ppermute | solution.py:258
  134.5 21.2 %slice-start.6 = ((s8[5242880]{0:T(1024)(128)(4,1)}), s8[4194304]{0:T(1024)(128)(4,1)S(1)}, s32[]{:S(2)}) async-start(s8[5242880]{0:T(1024)(128)(4,1)} %bitcast.294), calls=%async_computation.6 | async-start | bytes 8388608
  137.2 18.5 %slice-start.7 = ((s8[5242880]{0:T(1024)(128)(4,1)}), s8[1048576]{0:T(1024)(128)(4,1)S(1)}, s32[]{:S(2)}) async-start(s8[5242880]{0:T(1024)(128)(4,1)} %bitcast.294), calls=%async_computation.7 | async-start | bytes 2097152
  154.0 8.0 %collective-permute-start.7 = (f32[2,2,8,2,2,8,384]{6,5,4,3,2,1,0:T(8,128)S(1)}, f32[2,2,8,2,2,8,384]{6,5,4,3,2,1,0:T(8,128)S(1)}, u32[]{:S(2)}, u32[]{:S(2)}) collective-permute-start(f32[2,2,8,2,2,8,384]{6,5,4,3,2,1,0:T(8,128)S(1)} %get-tuple-element.90), channel_id=1, source_target_pairs={{0,8},{8,0},{1,9},{9,1},{2,10},{10,2},{3,11},{11,3},{4,12},{12,4},... | collective-permute-start | bytes 4718600 | tf_op jit(solution)/shard_map/ppermute | solution.py:262
  157.8 5.4 %copy-start = (bf16[256,256]{1,0:T(8,128)(2,1)S(1)}, bf16[256,256]{1,0:T(8,128)(2,1)}, u32[]{:S(2)}) copy-start(bf16[256,256]{1,0:T(8,128)(2,1)} %maximum_maximum_fusion.refs_1_.wq_ref) | copy-start | bytes 393220
  157.9 5.4 %copy-start.3 = (s32[5]{0:T(128)S(1)}, s32[5]{0:T(128)}, u32[]{:S(2)}) copy-start(s32[5]{0:T(128)} %copy-done.2) | copy-start | bytes 64
  157.9 11.4 %slice-start.4 = ((s8[5242880]{0:T(1024)(128)(4,1)}), s8[1048576]{0:T(1024)(128)(4,1)S(1)}, s32[]{:S(2)}) async-start(s8[5242880]{0:T(1024)(128)(4,1)} %bitcast.292), calls=%async_computation.4 | async-start | bytes 2097152
  159.3 18.7 %collective-permute-start.10 = (f32[2,2,2,2,2,2,8,640]{7,6,5,4,3,2,1,0:T(8,128)}, f32[2,2,2,2,2,2,8,640]{7,6,5,4,3,2,1,0:T(8,128)}, u32[]{:S(2)}, u32[]{:S(2)}) collective-permute-start(f32[2,2,2,2,2,2,8,640]{7,6,5,4,3,2,1,0:T(8,128)} %get-tuple-element.93), channel_id=1, source_target_pairs={{0,32},{32,0},{64,96},{96,64},{8,104},{40,72},{72,40},{104,8},{1,3... | collective-permute-start | bytes 3932168 | tf_op jit(solution)/shard_map/ppermute | solution.py:258
  162.0 1.2 copy-start.11
  163.2 6.1 %slice-start.5 = ((s8[5242880]{0:T(1024)(128)(4,1)}), s8[4194304]{0:T(1024)(128)(4,1)S(1)}, s32[]{:S(2)}) async-start(s8[5242880]{0:T(1024)(128)(4,1)} %bitcast.292), calls=%async_computation.5 | async-start | bytes 8388608
  166.8 20.9 %collective-permute-start.9 = (f32[2,2,2,2,2,2,2,8,384]{8,7,6,4,5,3,2,1,0:T(8,128)S(1)}, f32[2,2,2,2,2,2,2,8,384]{8,7,6,4,5,3,2,1,0:T(8,128)S(1)}, u32[]{:S(2)}, u32[]{:S(2)}) collective-permute-start(f32[2,2,2,2,2,2,2,8,384]{8,7,6,4,5,3,2,1,0:T(8,128)S(1)} %copy.55), channel_id=1, source_target_pairs={{0,16},{16,0},{4,20},{20,4},{8,28},{24,12},{12,24},{28,8},{1,17},{... | collective-permute-start | bytes 4718600 | tf_op jit(solution)/shard_map/ppermute | solution.py:258
  173.5 18.3 %collective-permute-start.14 = (f32[2,2,2,2,2,2,8,640]{7,6,5,4,3,2,1,0:T(8,128)S(1)}, f32[2,2,2,2,2,2,8,640]{7,6,5,4,3,2,1,0:T(8,128)S(1)}, u32[]{:S(2)}, u32[]{:S(2)}) collective-permute-start(f32[2,2,2,2,2,2,8,640]{7,6,5,4,3,2,1,0:T(8,128)S(1)} %get-tuple-element.92), channel_id=1, source_target_pairs={{0,1},{1,0},{2,3},{3,2},{8,11},{9,10},{10,9},{11,8},{4,5},{5,4},{6... | collective-permute-start | bytes 3932168 | tf_op jit(solution)/shard_map/ppermute | solution.py:258
  179.5 13.7 %collective-permute-start.13 = (f32[2,2,2,2,2,8,640]{6,5,4,3,2,1,0:T(8,128)S(1)}, f32[2,2,2,2,2,8,640]{6,5,4,3,2,1,0:T(8,128)S(1)}, u32[]{:S(2)}, u32[]{:S(2)}) collective-permute-start(f32[2,2,2,2,2,8,640]{6,5,4,3,2,1,0:T(8,128)S(1)} %get-tuple-element.99), channel_id=1, source_target_pairs={{0,96},{32,64},{64,32},{96,0},{8,40},{40,8},{72,104},{104,72},{1,9... | collective-permute-start | bytes 1966088 | tf_op jit(solution)/shard_map/ppermute | solution.py:258
  188.8 11.5 %collective-permute-start.12 = (f32[2,2,2,2,2,2,8,384]{7,6,5,3,4,2,1,0:T(8,128)}, f32[2,2,2,2,2,2,8,384]{7,6,5,3,4,2,1,0:T(8,128)}, u32[]{:S(2)}, u32[]{:S(2)}) collective-permute-start(f32[2,2,2,2,2,2,8,384]{7,6,5,3,4,2,1,0:T(8,128)} %get-tuple-element.96), channel_id=1, source_target_pairs={{0,20},{16,4},{4,16},{20,0},{8,24},{24,8},{12,28},{28,12},{1,21},{... | collective-permute-start | bytes 2359304 | tf_op jit(solution)/shard_map/ppermute | solution.py:258
  193.1 13.5 %collective-permute-start.16 = (f32[2,2,2,2,2,8,640]{6,5,4,3,2,1,0:T(8,128)}, f32[2,2,2,2,2,8,640]{6,5,4,3,2,1,0:T(8,128)}, u32[]{:S(2)}, u32[]{:S(2)}) collective-permute-start(f32[2,2,2,2,2,8,640]{6,5,4,3,2,1,0:T(8,128)} %get-tuple-element.98), channel_id=1, source_target_pairs={{0,3},{1,2},{2,1},{3,0},{8,9},{9,8},{10,11},{11,10},{4,7},{5,6},{6... | collective-permute-start | bytes 1966088 | tf_op jit(solution)/shard_map/ppermute | solution.py:258
  194.1 11.3 %collective-permute-start.17 = (f32[2,2,2,2,8,640]{5,4,3,2,1,0:T(8,128)}, f32[2,2,2,2,8,640]{5,4,3,2,1,0:T(8,128)}, u32[]{:S(2)}, u32[]{:S(2)}) collective-permute-start(f32[2,2,2,2,8,640]{5,4,3,2,1,0:T(8,128)} %get-tuple-element.105), channel_id=1, source_target_pairs={{0,1},{1,0},{2,3},{3,2},{8,11},{9,10},{10,9},{11,8},{4,5},{5,4},{6... | collective-permute-start | bytes 983048 | tf_op jit(solution)/shard_map/ppermute | solution.py:258
  196.4 10.1 %copy-start.4 = (f32[1,2,2,2,2,2,8,640]{7,6,5,4,3,2,1,0:T(8,128)S(1)}, f32[1,2,2,2,2,2,8,640]{7,6,5,4,3,2,1,0:T(8,128)}, u32[]{:S(2)}) copy-start(f32[1,2,2,2,2,2,8,640]{7,6,5,4,3,2,1,0:T(8,128)} %get-tuple-element.97) | copy-start | bytes 1966084
  200.3 10.4 %copy-start.5 = (f32[1,2,2,2,2,8,640]{6,5,4,3,2,1,0:T(8,128)S(1)}, f32[1,2,2,2,2,8,640]{6,5,4,3,2,1,0:T(8,128)}, u32[]{:S(2)}) copy-start(f32[1,2,2,2,2,8,640]{6,5,4,3,2,1,0:T(8,128)} %get-tuple-element.106) | copy-start | bytes 983044
  201.5 7.9 %collective-permute-start.15 = (f32[2,2,2,2,2,8,384]{6,5,4,2,3,1,0:T(8,128)S(1)}, f32[2,2,2,2,2,8,384]{6,5,4,2,3,1,0:T(8,128)S(1)}, u32[]{:S(2)}, u32[]{:S(2)}) collective-permute-start(f32[2,2,2,2,2,8,384]{6,5,4,2,3,1,0:T(8,128)S(1)} %get-tuple-element.102), channel_id=1, source_target_pairs={{0,32},{32,0},{64,96},{96,64},{8,104},{40,72},{72,40},{104,8},{1,3... | collective-permute-start | bytes 1179656 | tf_op jit(solution)/shard_map/ppermute | solution.py:258
  206.4 4.2 %collective-permute-start.20 = (f32[2,2,2,8,640]{4,3,2,1,0:T(8,128)S(1)}, f32[2,2,2,8,640]{4,3,2,1,0:T(8,128)S(1)}, u32[]{:S(2)}, u32[]{:S(2)}) collective-permute-start(f32[2,2,2,8,640]{4,3,2,1,0:T(8,128)S(1)} %fusion.42), channel_id=1, source_target_pairs={{0,3},{1,2},{2,1},{3,0},{8,9},{9,8},{10,11},{11,10},{4,7},{5,6},{6... | collective-permute-start | bytes 491528 | tf_op jit(solution)/shard_map/ppermute | solution.py:258
  207.7 7.5 %collective-permute-start.19 = (f32[2,2,2,2,8,640]{5,4,3,2,1,0:T(8,128)S(1)}, f32[2,2,2,2,8,640]{5,4,3,2,1,0:T(8,128)S(1)}, u32[]{:S(2)}, u32[]{:S(2)}) collective-permute-start(f32[2,2,2,2,8,640]{5,4,3,2,1,0:T(8,128)S(1)} %get-tuple-element.104), channel_id=1, source_target_pairs={{0,16},{16,0},{4,20},{20,4},{8,28},{24,12},{12,24},{28,8},{1,17},{... | collective-permute-start | bytes 983048 | tf_op jit(solution)/shard_map/ppermute | solution.py:258
  209.5 6.6 %collective-permute-start.18 = (f32[2,2,2,2,8,384]{5,4,3,1,2,0:T(8,128)S(1)}, f32[2,2,2,2,8,384]{5,4,3,1,2,0:T(8,128)S(1)}, u32[]{:S(2)}, u32[]{:S(2)}) collective-permute-start(f32[2,2,2,2,8,384]{5,4,3,1,2,0:T(8,128)S(1)} %fusion.29), channel_id=1, source_target_pairs={{0,96},{32,64},{64,32},{96,0},{8,40},{40,8},{72,104},{104,72},{1,9... | collective-permute-start | bytes 589832 | tf_op jit(solution)/shard_map/ppermute | solution.py:258
  211.6 4.5 %collective-permute-start.23 = (f32[2,2,8,640]{3,2,1,0:T(8,128)S(1)}, f32[2,2,8,640]{3,2,1,0:T(8,128)S(1)}, u32[]{:S(2)}, u32[]{:S(2)}) collective-permute-start(f32[2,2,8,640]{3,2,1,0:T(8,128)S(1)} %get-tuple-element.116), channel_id=1, source_target_pairs={{0,8},{8,0},{1,9},{9,1},{2,10},{10,2},{3,11},{11,3},{4,12},{12,4},... | collective-permute-start | bytes 245768 | tf_op jit(solution)/shard_map/ppermute | solution.py:262
  215.3 4.2 %collective-permute-start.21 = (f32[2,2,2,8,640]{4,3,2,1,0:T(8,128)S(1)}, f32[2,2,2,8,640]{4,3,2,1,0:T(8,128)S(1)}, u32[]{:S(2)}, u32[]{:S(2)}) collective-permute-start(f32[2,2,2,8,640]{4,3,2,1,0:T(8,128)S(1)} %fusion.40), channel_id=1, source_target_pairs={{0,20},{16,4},{4,16},{20,0},{8,24},{24,8},{12,28},{28,12},{1,21},{... | collective-permute-start | bytes 491528 | tf_op jit(solution)/shard_map/ppermute | solution.py:258
  219.6 4.0 %collective-permute-start.24 = (f32[2,2,8,640]{3,2,1,0:T(8,128)S(1)}, f32[2,2,8,640]{3,2,1,0:T(8,128)S(1)}, u32[]{:S(2)}, u32[]{:S(2)}) collective-permute-start(f32[2,2,8,640]{3,2,1,0:T(8,128)S(1)} %get-tuple-element.114), channel_id=1, source_target_pairs={{0,8},{8,0},{1,9},{9,1},{2,10},{10,2},{3,11},{11,3},{4,12},{12,4},... | collective-permute-start | bytes 245768 | tf_op jit(solution)/shard_map/ppermute | solution.py:262
  222.7 1.3 collective-permute-start.22
